TPU v7x, 32 devices: a whole 2x2x4 slice. The times are simulated.
32 devices in a mesh: row: 8 (over y, x, core), col: 4 (over z).
Axes of the slice: x: 2, y: 2, z: 4, core: 2. Of those that a mesh axis runs over, the one named last changes fastest.
Arguments:
- test_kernel: float32 [16384, 2048], P('row', 'col'), may hold values from -6 to 6
- first_panel: float32 [16384, 512], P('row', 'col'), may hold values from -0.25 to 0.25
- second_panel: float32 [16384, 512], P('row', 'col'), may hold values from -0.25 to 0.25
- first_inverse: float32 [512, 512], replicated, may hold values from -0.15 to 1.5, as said below
- second_inverse: float32 [512, 512], replicated, may hold values from -0.15 to 1.5, as said below
Outputs:
- solution: float32 [16384, 2048], P('row', 'col')
Inputs may be any that keep to these rules, and one draw needn't show every extreme that they name: `first_inverse`: lower triangular: zeros above the diagonal, diagonal entries positive. `second_inverse`: lower triangular: zeros above the diagonal, diagonal entries positive.
All inputs are finite; a program needn't handle non-finite values.
Results may differ from a plain program's by a relative error of at most 0.000075.
Values sent between devices are 32-bit elements; how exact they have to be, the bound alone decides.
No kernel may reach another device: no remote copies, remote signals or barrier semaphores. Data moves between devices by JAX's collectives and lax.ppermute only.
A program may use at most 64 MiB of HBM per device.

v0:
```python
import jax
import jax.numpy as jnp
from jax import lax
from jax.sharding import PartitionSpec as P


def broadcast(value, axis, source):
    kept = jnp.where(lax.axis_index(axis) == source, value, 0).astype(value.dtype)
    return lax.psum(kept, axis)


def product(left, right):
    return jnp.dot(left, right, precision=lax.Precision.HIGHEST, preferred_element_type=jnp.float32)


def folding(solved, piece):
    return product(piece, solved)


def per_device(test_kernel, first_panel, second_panel, first_inverse, second_inverse):
    block = first_inverse.shape[0]
    position = lax.axis_index("row")
    first_rows = broadcast(test_kernel[:block], "row", 0)
    first_solved = product(first_inverse, first_rows)
    update_one = folding(first_solved, lax.all_gather(first_panel, "col", axis=1, tiled=True))
    partial_value = test_kernel - update_one
    second_rows = broadcast(partial_value[:block], "row", 1)
    second_solved = product(second_inverse, second_rows)
    update_two = folding(second_solved, lax.all_gather(second_panel, "col", axis=1, tiled=True))
    final = partial_value - update_two
    leading_final = jnp.where(
        position == 0, first_solved, jnp.where(position == 1, second_solved, final[:block])
    )
    return final.at[:block].set(leading_final)


def solution(mesh):
    in_specs = (P("row", "col"), P("row", "col"), P("row", "col"), P(), P())
    out_specs = P("row", "col")
    return jax.shard_map(
        per_device, mesh=mesh, in_specs=in_specs, out_specs=out_specs, check_vma=False
    )
```

profile of v0, /device:TPU:0, one launch (start us, length us, event | category | flops | bytes accessed | tf_op | source)
XLA Modules:
  0.0 219.8 jit_solution(2210618295947269373)
XLA Ops:
  7.4 0.0 copy-start
  7.4 0.0 all-reduce.3.cloned.1.call-start
  7.4 5.4 %copy.7 = f32[2048,512]{0,1:T(8,128)} copy(f32[2048,512]{1,0:T(8,128)} %param.7) | data formatting | bytes 8388608 | tf_op args[0]
  12.8 2.3 %slice_select_fusion.2 = f32[512,512]{0,1:T(8,128)} fusion(f32[2048,512]{0,1:T(8,128)} %copy.7, pred[]{:T(512)S(6)} %eq.8), kind=kLoop, calls=%fused_computation.6 | loop fusion | flops 262144 | bytes 2097153 | tf_op jit(solution)/shard_map/jit(_where)/select_n | solution.py:8
  15.1 0.0 all-reduce.3.cloned.1.call-update
  15.1 0.0 all-gather.3.cloned.1.call-start
  15.2 0.5 all-gather.3.cloned.1.call-update
  15.7 0.0 all-reduce.5.cloned.1.call-start
  15.8 58.7 %all-reduce.3.cloned.1.call-done = f32[512,512]{0,1:T(8,128)} async-done(((f32[512,512]{0,1:T(8,128)}), f32[512,512]{0,1:T(8,128)}) %all-reduce.3.cloned.1.call-update) | async-done | bytes 1048592 | tf_op jit(solution)/shard_map/psum | solution.py:9
  74.5 0.0 copy-done
  74.5 3.1 %fusion.2 = f32[512,512]{1,0:T(8,128)S(1)} fusion(f32[512,512]{0,1:T(8,128)} %all-reduce.3.cloned.1.call-done, f32[512,512]{1,0:T(8,128)S(1)} %copy-done), kind=kOutput, calls=%fused_computation.7 | convolution fusion | flops 1610612736 | bytes 3145728 | tf_op jit(solution)/shard_map/dot_general | solution.py:13
  77.6 22.7 %all-gather.3.cloned.1.call-done = f32[2048,512]{1,0:T(8,128)} async-done(((f32[2048,128]{1,0:T(8,128)}), f32[2048,512]{1,0:T(8,128)}) %all-gather.3.cloned.1.call-update) | async-done | bytes 4194320 | tf_op jit(solution)/shard_map/all_gather | solution.py:25
  100.3 9.4 %bitcast_subtract_fusion.1 = f32[2048,512]{0,1:T(8,128)S(1)} fusion(f32[2048,512]{0,1:T(8,128)} %copy.7, f32[512,512]{1,0:T(8,128)S(1)} %fusion.2, f32[2048,512]{1,0:T(8,128)} %all-gather.3.cloned.1.call-done), kind=kOutput, calls=%fused_computation.1 | convolution fusion | flops 6443499520 | bytes 13631488 | tf_op jit(solution)/shard_map/dot_general | solution.py:13
  109.7 0.0 copy-start.1
  109.7 2.0 copy-done.1
  111.7 1.1 slice_select_fusion.1
  112.9 0.0 all-reduce.5.cloned.1.call-update
  112.9 0.2 all-gather.5.cloned.1.call-start
  113.1 0.4 all-gather.5.cloned.1.call-update
  113.5 54.2 %all-reduce.5.cloned.1.call-done = f32[512,512]{0,1:T(8,128)} async-done(((f32[512,512]{0,1:T(8,128)}), f32[512,512]{0,1:T(8,128)}) %all-reduce.5.cloned.1.call-update) | async-done | bytes 1048592 | tf_op jit(solution)/shard_map/psum | solution.py:9
  167.7 3.4 %fusion.3 = f32[512,512]{1,0:T(8,128)S(1)} fusion(f32[512,512]{0,1:T(8,128)} %all-reduce.5.cloned.1.call-done, f32[512,512]{1,0:T(8,128)} %param.11), kind=kOutput, calls=%fused_computation.8 | convolution fusion | flops 1610612736 | bytes 3145728 | tf_op jit(solution)/shard_map/dot_general | solution.py:13
  171.1 22.4 %all-gather.5.cloned.1.call-done = f32[2048,512]{1,0:T(8,128)} async-done(((f32[2048,128]{1,0:T(8,128)}), f32[2048,512]{1,0:T(8,128)}) %all-gather.5.cloned.1.call-update) | async-done | bytes 4194320 | tf_op jit(solution)/shard_map/all_gather | solution.py:29
  193.6 10.8 %bitcast_subtract_fusion = f32[2048,512]{0,1:T(8,128)} fusion(f32[2048,512]{0,1:T(8,128)} %copy-done.1, f32[512,512]{1,0:T(8,128)S(1)} %fusion.3, f32[2048,512]{1,0:T(8,128)} %all-gather.5.cloned.1.call-done), kind=kOutput, calls=%fused_computation | convolution fusion | flops 6443499520 | bytes 13631488 | tf_op jit(solution)/shard_map/dot_general | solution.py:13
  204.4 2.6 %fusion.1 = f32[2048,512]{0,1:T(8,128)} fusion(f32[2048,512]{0,1:T(8,128)} %bitcast_subtract_fusion, f32[512,512]{1,0:T(8,128)S(1)} %fusion.3, f32[512,512]{1,0:T(8,128)S(1)} %fusion.2, pred[]{:T(512)S(6)} %eq.9, pred[]{:T(512)S(6)} %eq.8), kind=kLoop, calls=%fused_computation.4 | loop fusion | flops 524288 | bytes 4194306 | tf_op jit(solution)/shard_map/scatter | solution.py:34
  207.0 5.3 %copy.8 = f32[2048,512]{1,0:T(8,128)} copy(f32[2048,512]{0,1:T(8,128)} %fusion.1) | data formatting | bytes 8388608 | tf_op jit(solution)/shard_map/scatter | solution.py:34
Async XLA Ops:
  7.4 67.1 %copy-start = (f32[512,512]{1,0:T(8,128)S(1)}, f32[512,512]{1,0:T(8,128)}, u32[]{:S(2)}) copy-start(f32[512,512]{1,0:T(8,128)} %param.10) | copy-start | bytes 3145732
  7.4 67.1 %all-reduce.3.cloned.1.call-start = ((), (), s32[]{:S(2)}) async-start(), calls=%async_computation | async-start | bytes 2097152 | tf_op jit(solution)/shard_map/psum | solution.py:9
  15.1 85.2 %all-gather.3.cloned.1.call-start = ((), (), s32[]{:S(2)}) async-start(), calls=%async_computation.1 | async-start | bytes 5242880 | tf_op jit(solution)/shard_map/all_gather | solution.py:25
  15.7 152.0 %all-reduce.5.cloned.1.call-start = ((), (), s32[]{:S(2)}) async-start(), calls=%async_computation.2 | async-start | bytes 2097152 | tf_op jit(solution)/shard_map/psum | solution.py:9
  109.7 2.0 copy-start.1
  112.9 80.7 %all-gather.5.cloned.1.call-start = ((), (), s32[]{:S(2)}) async-start(), calls=%async_computation.3 | async-start | bytes 5242880 | tf_op jit(solution)/shard_map/all_gather | solution.py:29
Sparse Core Ops, SparseCore 0:
  15.3 59.1 all-reduce.2
  113.0 54.6 all-reduce.4
Sparse Core Ops, SparseCore 1:
  17.2 83.1 all-gather.2
  114.9 78.6 all-gather.4
where the time goes:
time: 220 us
  waiting for transfers between devices  159 us (72%)
  matrix products  26.7 us (12%)
  between operations  14.9 us (7%)
  local copies, waits for them, and re-layouts  12.8 us (6%)
  other arithmetic  6.08 us (3%)
    psum x2, waiting for transfers between devices, broadcast(): return lax.psum(kept, axis)  113 us
    dot_general x4, matrix products, product(): jnp.dot(left, right, precision=lax.Precision.HIGHEST, preferred_element_t...  26.7 us
    all_gather x1, waiting for transfers between devices, per_device(): lax.all_gather(first_panel, 'col', axis=1, tiled=True)  22.7 us
    all_gather x1, waiting for transfers between devices, per_device(): lax.all_gather(second_panel, 'col', axis=1, tiled=True)  22.4 us
    unnamed x5, local copies, waits for them, and re-layouts  7.44 us
    scatter x1, local copies, waits for them, and re-layouts, per_device(): return final.at[:block].set(leading_final)  5.34 us
  transfers between devices with their start and end apart: 4, of which 4 were waited for; matrix products, arithmetic and copies ran while one was open for 3% of the time, Pallas kernels for 0%

commit v1 on v0

v1 whole, which is shorter than its diff:
```python
import jax
import jax.numpy as jnp
from jax import lax
from jax.sharding import PartitionSpec as P

PARTS = 8
RAW_PARTS = 4


def product(left, right):
    return jnp.dot(left, right, precision=lax.Precision.HIGH, preferred_element_type=jnp.float32)


def broadcast(value, axis, source):
    kept = jnp.where(lax.axis_index(axis) == source, value, 0).astype(value.dtype)
    return lax.psum(kept, axis)


def general(test_kernel, first_panel, second_panel, first_inverse, second_inverse):
    block = first_inverse.shape[0]
    position = lax.axis_index("row")
    first_rows = broadcast(test_kernel[:block], "row", 0)
    first_solved = product(first_inverse, first_rows)
    partial_value = test_kernel - product(lax.all_gather(first_panel, "col", axis=1, tiled=True), first_solved)
    second_rows = broadcast(partial_value[:block], "row", 1)
    second_solved = product(second_inverse, second_rows)
    final = partial_value - product(lax.all_gather(second_panel, "col", axis=1, tiled=True), second_solved)
    leading_final = jnp.where(
        position == 0, first_solved, jnp.where(position == 1, second_solved, final[:block])
    )
    return final.at[:block].set(leading_final)


AXES = ("row", "col")
ROWS, COLS = 8, 4
END_MID = ((0, 1), (3, 2))
MID_MID = ((1, 2), (2, 1))
MID_END = ((1, 0), (2, 3))


def along_col(value, pairs, rows):
    return lax.ppermute(value, AXES, [(r * COLS + a, r * COLS + b) for r in rows for a, b in pairs])


def along_row(value, pairs, cols):
    return lax.ppermute(value, AXES, [(a * COLS + c, b * COLS + c) for a, b in pairs for c in cols])


ALL_COLS = (0, 1, 2, 3)
MID_COLS = (1, 2)
SWAP = tuple((r, r ^ 1) for r in range(ROWS))


def spread(value, cols):
    row = lax.axis_index("row")
    even = row % 2 == 0
    half = value.shape[0] // 2
    mine = jnp.where(even, value[:half], value[half:])
    near = along_row(mine, ((0, 2), (1, 5)), cols)
    mine = jnp.where((row == 2) | (row == 5), near, mine)
    far = along_row(mine, ((2, 6), (5, 7), (0, 4), (1, 3)), cols)
    mine = jnp.where((row == 3) | (row == 4) | (row >= 6), far, mine)
    other = along_row(mine, SWAP, cols)
    return jnp.concatenate([jnp.where(even, mine, other), jnp.where(even, other, mine)], axis=0)


def four(test_kernel, first_panel, second_panel, first_inverse, second_inverse):
    block = first_inverse.shape[0]
    rows, width = test_kernel.shape
    slab = first_panel.shape[1]
    part = rows // PARTS
    row, col = lax.axis_index("row"), lax.axis_index("col")
    end = (col == 0) | (col == COLS - 1)
    left = col < COLS // 2
    every = range(ROWS)

    corner = first_panel[:block]
    one = (1,)
    corner_end = along_col(corner, END_MID, one)
    corner_mid = along_col(corner, MID_MID, one)
    corner_far = along_col(corner_end, MID_MID, one)
    corner_c = along_col(corner, MID_END, one)
    corner_c2 = along_col(corner_mid, MID_END, one)
    corner_c3 = along_col(corner_far, MID_END, one)
    corner_all = jnp.concatenate(
        [
            jnp.where(end, corner, corner_end),
            jnp.where(end, corner_c, corner),
            jnp.where(end, corner_c2, corner_mid),
            jnp.where(end, corner_c3, corner_far),
        ],
        axis=1,
    )

    def relative(solved):
        pieces = solved.reshape(COLS, block // COLS, width)
        return jnp.where(left, pieces, pieces[::-1])

    top = test_kernel[:block]
    top_end = along_col(top, END_MID, (0, 1))

    def solve(own_top, cols):
        first = jnp.where(row == 1, along_row(own_top, ((0, 1),), cols), own_top)
        first_solved = product(first_inverse, first)
        value = own_top - product(corner_all, relative(first_solved).reshape(block, width))
        second_solved = product(second_inverse, value)
        second_half = along_row(second_solved[: block // 2], ((1, 0),), cols)
        second_held = second_solved.at[: block // 2].set(
            jnp.where(row == 0, second_half, second_solved[: block // 2])
        )
        return first_solved, second_held

    def stacked(first_solved, second_solved):
        return jnp.concatenate([relative(first_solved), relative(second_solved)], axis=1).reshape(
            2 * block, width
        )

    first_end, second_end = solve(top_end, MID_COLS)
    first_end, second_end = spread(first_end, MID_COLS), spread(second_end, MID_COLS)
    solved_end = stacked(first_end, second_end)
    first_own, second_own = solve(top, ALL_COLS)
    first_own, second_own = spread(first_own, ALL_COLS), spread(second_own, ALL_COLS)
    solved_own = stacked(first_own, second_own)

    out = []
    for index in range(PARTS):
        low, high = index * part, (index + 1) * part
        members = every if low >= block else range(2, ROWS)
        own = jnp.concatenate([first_panel[low:high], second_panel[low:high]], axis=1)
        from_end = along_col(own, END_MID, members)
        from_mid = along_col(own, MID_MID, members)
        from_far = along_col(from_end, MID_MID, members)
        if index < RAW_PARTS:
            near = along_col(own, MID_END, members)
            mid = along_col(from_mid, MID_END, members)
            far = along_col(from_far, MID_END, members)
            panels = jnp.concatenate(
                [
                    jnp.where(end, own, from_end),
                    jnp.where(end, near, own),
                    jnp.where(end, mid, from_mid),
                    jnp.where(end, far, from_far),
                ],
                axis=1,
            )
            update = product(panels, solved_own)
        else:
            panels = jnp.concatenate([from_end, own, from_mid, from_far], axis=1)
            sent = along_col(product(panels, solved_end), MID_END, members)
            update = jnp.where(end, sent, product(panels, solved_own))
        piece = test_kernel[low:high] - update
        if low < block:
            piece = jnp.where(
                row == 0, first_own[low:high], jnp.where(row == 1, second_own[low:high], piece)
            )
        out.append(piece)
    return jnp.concatenate(out, axis=0)


def solution(mesh):
    in_specs = (P("row", "col"), P("row", "col"), P("row", "col"), P(), P())
    out_specs = P("row", "col")
    body = four if dict(mesh.shape) == {"row": ROWS, "col": COLS} else general
    return jax.shard_map(body, mesh=mesh, in_specs=in_specs, out_specs=out_specs, check_vma=False)
```

time: 220 us -> 275 us (1.25)
  starting transfers between devices: 0.31 us -> 117 us
  waiting for transfers between devices: 159 us -> 117 us
  between operations: 14.9 us -> 1.57 us
  matrix products: 26.7 us -> 20.5 us
  local copies, waits for them, and re-layouts: 12.8 us -> 9 us
    ppermute x0 -> x63, starting transfers between devices: none -> 117 us  [the longest x47 78.5 us: along_col(): lax.ppermute(value, AXES, [(r * COLS + a, r * COLS + b) for r in rows for...]
    ppermute x0 -> x63, waiting for transfers between devices: none -> 117 us  [the longest x47 106 us: along_col(): lax.ppermute(value, AXES, [(r * COLS + a, r * COLS + b) for r in rows for...]
    psum x2 -> x0, waiting for transfers between devices: 113 us -> none  [broadcast(): return lax.psum(kept, axis)]
    all_gather x2 -> x0, waiting for transfers between devices: 45.2 us -> none  [the longest x1 22.7 us: per_device(): lax.all_gather(first_panel, 'col', axis=1, tiled=True)]
    dot_general x4 -> x18, matrix products: 26.7 us -> 20.5 us  [product(): jnp.dot(left, right, precision=lax.Precision.HIGH, preferred_element_type...]
    slice x0 -> x6, local copies, waits for them, and re-layouts: none -> 5.47 us  [the longest x1 1.76 us: four(): corner = first_panel[:block]]
    scatter x1 -> x0, local copies, waits for them, and re-layouts: 5.34 us -> none  [per_device(): return final.at[:block].set(leading_final)]
    concatenate x0 -> x15, other arithmetic: none -> 4.55 us  [the longest x8 2.98 us: four(): jnp.concatenate([first_panel[low:high], second_panel[low:high]], axis=1)]
  transfers between devices with their start and end apart: 4 -> 63, of which waited for: 4 -> 14; matrix products, arithmetic and copies ran while one was open for 3% -> 12% of each run, Pallas kernels for 0% -> 0%
where the time goes in v1:
time: 275 us; the launch traced here: 273 us
  starting transfers between devices  117 us (43%)
  waiting for transfers between devices  117 us (43%)
  matrix products  20.5 us (7%)
  local copies, waits for them, and re-layouts  9 us (3%)
  other arithmetic  7.91 us (3%)
    ppermute x47, waiting for transfers between devices, along_col(): lax.ppermute(value, AXES, [(r * COLS + a, r * COLS + b) for r in rows for...  106 us
    ppermute x47, starting transfers between devices, along_col(): lax.ppermute(value, AXES, [(r * COLS + a, r * COLS + b) for r in rows for...  78.5 us
    ppermute x16, starting transfers between devices, along_row(): lax.ppermute(value, AXES, [(a * COLS + c, b * COLS + c) for a, b in pairs...  38.9 us
    dot_general x18, matrix products, product(): jnp.dot(left, right, precision=lax.Precision.HIGH, preferred_element_type...  20.5 us
    ppermute x16, waiting for transfers between devices, along_row(): lax.ppermute(value, AXES, [(a * COLS + c, b * COLS + c) for a, b in pairs...  10.8 us
  transfers between devices with their start and end apart: 63, of which 14 were waited for; matrix products, arithmetic and copies ran while one was open for 12% of the time, Pallas kernels for 0%

profile of v1, /device:TPU:0, one launch (start us, length us, event | category | flops | bytes accessed | tf_op | source)
XLA Modules:
  0.0 273.4 jit_solution(3570061887015244718)
XLA Ops:
  0.0 1.8 slice.143
  2.4 1.4 collective-permute-start.6
  6.8 5.6 %collective-permute-start.59 = (f32[256,256]{1,0:T(8,128)}, f32[256,256]{1,0:T(8,128)}, u32[]{:S(2)}, u32[]{:S(2)}) collective-permute-start(f32[256,256]{1,0:T(8,128)} %pad_maximum_fusion.16), channel_id=1, source_target_pairs={{0,1},{3,2},{4,5},{7,6},{8,9},{11,10},{12,13},{15,14},{16,17},{19,... | collective-permute-start | bytes 786440 | tf_op jit(solution)/shard_map/ppermute | solution.py:42
  13.2 2.0 collective-permute-start.51
  15.9 2.0 collective-permute-start.38
  18.6 1.4 slice.140
  20.0 1.4 collective-permute-start.55
  24.1 2.5 collective-permute-done.38
  28.3 4.0 %collective-permute-done.55 = f32[256,256]{1,0:T(8,128)S(1)} collective-permute-done((f32[256,256]{1,0:T(8,128)}, f32[256,256]{1,0:T(8,128)S(1)}, u32[]{:S(2)}, u32[]{:S(2)}) %collective-permute-start.55) | collective-permute-done | bytes 262176 | tf_op jit(solution)/shard_map/ppermute | solution.py:42
  37.7 1.3 collective-permute-start.27
  39.0 25.2 %collective-permute-start.26 = (f32[256,256]{1,0:T(8,128)S(1)}, f32[256,256]{1,0:T(8,128)S(1)}, u32[]{:S(2)}, u32[]{:S(2)}) collective-permute-start(f32[256,256]{1,0:T(8,128)S(1)} %pad_maximum_fusion.11), channel_id=1, source_target_pairs={{0,1},{3,2},{4,5},{7,6},{8,9},{11,10},{12,13},{15,14},{16,17},{19,... | collective-permute-start | bytes 786440 | tf_op jit(solution)/shard_map/ppermute | solution.py:42
  64.3 1.3 collective-permute-start.33
  65.6 4.6 %collective-permute-start.32 = (f32[256,256]{1,0:T(8,128)S(1)}, f32[256,256]{1,0:T(8,128)S(1)}, u32[]{:S(2)}, u32[]{:S(2)}) collective-permute-start(f32[256,256]{1,0:T(8,128)S(1)} %pad_maximum_fusion.12), channel_id=1, source_target_pairs={{0,1},{3,2},{4,5},{7,6},{8,9},{11,10},{12,13},{15,14},{16,17},{19,... | collective-permute-start | bytes 786440 | tf_op jit(solution)/shard_map/ppermute | solution.py:42
  72.4 2.9 %collective-permute-done.33 = f32[256,256]{1,0:T(8,128)S(1)} collective-permute-done((f32[256,256]{1,0:T(8,128)S(1)}, f32[256,256]{1,0:T(8,128)S(1)}, u32[]{:S(2)}, u32[]{:S(2)}) %collective-permute-start.33) | collective-permute-done | bytes 262176 | tf_op jit(solution)/shard_map/ppermute | solution.py:42
  82.3 4.9 %collective-permute-start = (f32[512,512]{1,0:T(8,128)S(1)}, f32[512,512]{1,0:T(8,128)S(1)}, u32[]{:S(2)}, u32[]{:S(2)}) collective-permute-start(f32[512,512]{1,0:T(8,128)S(1)} %slice.140), channel_id=1, source_target_pairs={{0,4},{1,5},{2,6},{3,7}} | collective-permute-start | bytes 3145736 | tf_op jit(solution)/shard_map/ppermute | solution.py:46
  88.7 1.3 collective-permute-start.29
  90.0 1.3 collective-permute-start.35
  92.1 30.5 %collective-permute-done.29 = f32[256,256]{1,0:T(8,128)S(1)} collective-permute-done((f32[256,256]{1,0:T(8,128)S(1)}, f32[256,256]{1,0:T(8,128)S(1)}, u32[]{:S(2)}, u32[]{:S(2)}) %collective-permute-start.29) | collective-permute-done | bytes 262176 | tf_op jit(solution)/shard_map/ppermute | solution.py:42
  123.2 4.3 %collective-permute-done.35 = f32[256,256]{1,0:T(8,128)S(1)} collective-permute-done((f32[256,256]{1,0:T(8,128)S(1)}, f32[256,256]{1,0:T(8,128)S(1)}, u32[]{:S(2)}, u32[]{:S(2)}) %collective-permute-start.35) | collective-permute-done | bytes 262176 | tf_op jit(solution)/shard_map/ppermute | solution.py:42
  128.3 3.6 %collective-permute-start.41 = (f32[512,512]{1,0:T(8,128)S(1)}, f32[512,512]{1,0:T(8,128)S(1)}, u32[]{:S(2)}, u32[]{:S(2)}) collective-permute-start(f32[512,512]{1,0:T(8,128)S(1)} %slice.140), channel_id=1, source_target_pairs={{0,1},{3,2},{4,5},{7,6}} | collective-permute-start | bytes 3145736 | tf_op jit(solution)/shard_map/ppermute | solution.py:42
  133.3 1.3 collective-permute-start.31
  134.6 1.3 collective-permute-start.37
  139.4 14.0 %collective-permute-start.1 = (f32[256,512]{1,0:T(8,128)S(1)}, f32[256,512]{1,0:T(8,128)S(1)}, u32[]{:S(2)}, u32[]{:S(2)}) collective-permute-start(f32[256,512]{1,0:T(8,128)S(1)} %slice_select_fusion.3), channel_id=1, source_target_pairs={{0,8},{1,9},{2,10},{3,11},{4,20},{5,21},{6,22},{7,23}} | collective-permute-start | bytes 1572872 | tf_op jit(solution)/shard_map/ppermute | solution.py:46
  153.6 1.3 collective-permute-start.10
  155.8 4.4 %collective-permute-done.1 = f32[256,512]{1,0:T(8,128)S(1)} collective-permute-done((f32[256,512]{1,0:T(8,128)S(1)}, f32[256,512]{1,0:T(8,128)S(1)}, u32[]{:S(2)}, u32[]{:S(2)}) %collective-permute-start.1) | collective-permute-done | bytes 524320 | tf_op jit(solution)/shard_map/ppermute | solution.py:46
  160.3 5.3 %collective-permute-start.2 = (f32[256,512]{1,0:T(8,128)S(1)}, f32[256,512]{1,0:T(8,128)S(1)}, u32[]{:S(2)}, u32[]{:S(2)}) collective-permute-start(f32[256,512]{1,0:T(8,128)S(1)} %broadcast_select_fusion.3), channel_id=1, source_target_pairs={{8,24},{9,25},{10,26},{11,27},{20,28},{21,29},{22,30},{23,31},{0,1... | collective-permute-start | bytes 1572872 | tf_op jit(solution)/shard_map/ppermute | solution.py:46
  165.7 3.4 %collective-permute-start.11 = (f32[256,512]{1,0:T(8,128)S(1)}, f32[256,512]{1,0:T(8,128)S(1)}, u32[]{:S(2)}, u32[]{:S(2)}) collective-permute-start(f32[256,512]{1,0:T(8,128)S(1)} %slice_select_fusion.2), channel_id=1, source_target_pairs={{0,8},{1,9},{2,10},{3,11},{4,20},{5,21},{6,22},{7,23}} | collective-permute-start | bytes 1572872 | tf_op jit(solution)/shard_map/ppermute | solution.py:46
  175.9 4.0 %collective-permute-start.12 = (f32[256,512]{1,0:T(8,128)S(1)}, f32[256,512]{1,0:T(8,128)S(1)}, u32[]{:S(2)}, u32[]{:S(2)}) collective-permute-start(f32[256,512]{1,0:T(8,128)S(1)} %broadcast_select_fusion.2), channel_id=1, source_target_pairs={{8,24},{9,25},{10,26},{11,27},{20,28},{21,29},{22,30},{23,31},{0,1... | collective-permute-start | bytes 1572872 | tf_op jit(solution)/shard_map/ppermute | solution.py:46
  181.7 4.9 %collective-permute-done.12 = f32[256,512]{1,0:T(8,128)S(1)} collective-permute-done((f32[256,512]{1,0:T(8,128)S(1)}, f32[256,512]{1,0:T(8,128)S(1)}, u32[]{:S(2)}, u32[]{:S(2)}) %collective-permute-start.12) | collective-permute-done | bytes 524320 | tf_op jit(solution)/shard_map/ppermute | solution.py:46
  189.1 1.2 fusion.58
  190.3 1.2 fusion.56
  191.5 1.2 fusion.54
  192.7 1.2 fusion.52
  193.9 1.2 fusion.4
  195.1 1.3 fusion.7
  196.4 1.2 fusion.1
  197.6 1.2 fusion
  200.4 1.2 fusion.53
  201.6 1.2 fusion.51
  202.8 1.3 collective-permute-start.50
  204.1 1.5 collective-permute-start.54
  206.8 1.3 collective-permute-start.58
  208.1 1.2 fusion.57
  209.3 1.3 collective-permute-start.62
  210.6 28.6 %collective-permute-done.50 = f32[256,512]{1,0:T(8,128)S(1)} collective-permute-done((f32[256,512]{1,0:T(8,128)S(1)}, f32[256,512]{1,0:T(8,128)S(1)}, u32[]{:S(2)}, u32[]{:S(2)}) %collective-permute-start.50) | collective-permute-done | bytes 524320 | tf_op jit(solution)/shard_map/ppermute | solution.py:42
  239.4 11.1 %collective-permute-done.54 = f32[256,512]{1,0:T(8,128)S(1)} collective-permute-done((f32[256,512]{1,0:T(8,128)S(1)}, f32[256,512]{1,0:T(8,128)S(1)}, u32[]{:S(2)}, u32[]{:S(2)}) %collective-permute-start.54) | collective-permute-done | bytes 524320 | tf_op jit(solution)/shard_map/ppermute | solution.py:42
  250.6 11.1 %collective-permute-done.58 = f32[256,512]{1,0:T(8,128)S(1)} collective-permute-done((f32[256,512]{1,0:T(8,128)S(1)}, f32[256,512]{1,0:T(8,128)S(1)}, u32[]{:S(2)}, u32[]{:S(2)}) %collective-permute-start.58) | collective-permute-done | bytes 524320 | tf_op jit(solution)/shard_map/ppermute | solution.py:42
  261.8 10.6 %collective-permute-done.62 = f32[256,512]{1,0:T(8,128)S(1)} collective-permute-done((f32[256,512]{1,0:T(8,128)S(1)}, f32[256,512]{1,0:T(8,128)S(1)}, u32[]{:S(2)}, u32[]{:S(2)}) %collective-permute-start.62) | collective-permute-done | bytes 524320 | tf_op jit(solution)/shard_map/ppermute | solution.py:42
  (185 shorter events, 48.8 us)
Async XLA Ops:
  1.8 31.5 %collective-permute-start.5 = (f32[512,128]{1,0:T(8,128)}, f32[512,128]{1,0:T(8,128)S(1)}, u32[]{:S(2)}, u32[]{:S(2)}) collective-permute-start(f32[512,128]{1,0:T(8,128)} %slice.143), channel_id=1, source_target_pairs={{5,4},{6,7}} | collective-permute-start | bytes 786440 | tf_op jit(solution)/shard_map/ppermute | solution.py:42
  2.4 67.8 %collective-permute-start.6 = (f32[512,128]{1,0:T(8,128)}, f32[512,128]{1,0:T(8,128)}, u32[]{:S(2)}, u32[]{:S(2)}) collective-permute-start(f32[512,128]{1,0:T(8,128)} %slice.143), channel_id=1, source_target_pairs={{5,6},{6,5}} | collective-permute-start | bytes 786440 | tf_op jit(solution)/shard_map/ppermute | solution.py:42
  6.8 13.2 %collective-permute-start.59 = (f32[256,256]{1,0:T(8,128)}, f32[256,256]{1,0:T(8,128)}, u32[]{:S(2)}, u32[]{:S(2)}) collective-permute-start(f32[256,256]{1,0:T(8,128)} %pad_maximum_fusion.16), channel_id=1, source_target_pairs={{0,1},{3,2},{4,5},{7,6},{8,9},{11,10},{12,13},{15,14},{16,17},{19,... | collective-permute-start | bytes 786440 | tf_op jit(solution)/shard_map/ppermute | solution.py:42
  13.2 9.3 %collective-permute-start.51 = (f32[256,256]{1,0:T(8,128)}, f32[256,256]{1,0:T(8,128)}, u32[]{:S(2)}, u32[]{:S(2)}) collective-permute-start(f32[256,256]{1,0:T(8,128)} %pad_maximum_fusion.14), channel_id=1, source_target_pairs={{0,1},{3,2},{4,5},{7,6},{8,9},{11,10},{12,13},{15,14},{16,17},{19,... | collective-permute-start | bytes 786440 | tf_op jit(solution)/shard_map/ppermute | solution.py:42
  15.9 10.8 %collective-permute-start.38 = (f32[256,256]{1,0:T(8,128)}, f32[256,256]{1,0:T(8,128)}, u32[]{:S(2)}, u32[]{:S(2)}) collective-permute-start(f32[256,256]{1,0:T(8,128)} %pad_maximum_fusion.13), channel_id=1, source_target_pairs={{0,1},{3,2},{4,5},{7,6},{8,9},{11,10},{12,13},{15,14},{16,17},{19,... | collective-permute-start | bytes 786440 | tf_op jit(solution)/shard_map/ppermute | solution.py:42
  20.0 12.2 %collective-permute-start.55 = (f32[256,256]{1,0:T(8,128)}, f32[256,256]{1,0:T(8,128)S(1)}, u32[]{:S(2)}, u32[]{:S(2)}) collective-permute-start(f32[256,256]{1,0:T(8,128)} %pad_maximum_fusion.15), channel_id=1, source_target_pairs={{0,1},{3,2},{4,5},{7,6},{8,9},{11,10},{12,13},{15,14},{16,17},{19,... | collective-permute-start | bytes 786440 | tf_op jit(solution)/shard_map/ppermute | solution.py:42
  22.5 11.5 %collective-permute-start.4 = (f32[512,128]{1,0:T(8,128)}, f32[512,128]{1,0:T(8,128)S(1)}, u32[]{:S(2)}, u32[]{:S(2)}) collective-permute-start(f32[512,128]{1,0:T(8,128)} %slice.143), channel_id=1, source_target_pairs={{4,5},{7,6}} | collective-permute-start | bytes 786440 | tf_op jit(solution)/shard_map/ppermute | solution.py:42
  26.7 10.3 %collective-permute-start.56 = (f32[256,256]{1,0:T(8,128)}, f32[256,256]{1,0:T(8,128)S(1)}, u32[]{:S(2)}, u32[]{:S(2)}) collective-permute-start(f32[256,256]{1,0:T(8,128)} %pad_maximum_fusion.15), channel_id=1, source_target_pairs={{1,2},{2,1},{5,6},{6,5},{9,10},{10,9},{13,14},{14,13},{17,18},{18,... | collective-permute-start | bytes 786440 | tf_op jit(solution)/shard_map/ppermute | solution.py:42
  36.2 28.0 %collective-permute-start.21 = (f32[256,256]{1,0:T(8,128)S(1)}, f32[256,256]{1,0:T(8,128)S(1)}, u32[]{:S(2)}, u32[]{:S(2)}) collective-permute-start(f32[256,256]{1,0:T(8,128)S(1)} %pad_maximum_fusion.10), channel_id=1, source_target_pairs={{9,8},{10,11},{13,12},{14,15},{17,16},{18,19},{21,20},{22,23},{25,... | collective-permute-start | bytes 786440 | tf_op jit(solution)/shard_map/ppermute | solution.py:42
  37.0 28.6 %collective-permute-start.20 = (f32[256,256]{1,0:T(8,128)S(1)}, f32[256,256]{1,0:T(8,128)S(1)}, u32[]{:S(2)}, u32[]{:S(2)}) collective-permute-start(f32[256,256]{1,0:T(8,128)S(1)} %pad_maximum_fusion.10), channel_id=1, source_target_pairs={{8,9},{11,10},{12,13},{15,14},{16,17},{19,18},{20,21},{23,22},{24,... | collective-permute-start | bytes 786440 | tf_op jit(solution)/shard_map/ppermute | solution.py:42
  37.7 33.2 %collective-permute-start.27 = (f32[256,256]{1,0:T(8,128)S(1)}, f32[256,256]{1,0:T(8,128)S(1)}, u32[]{:S(2)}, u32[]{:S(2)}) collective-permute-start(f32[256,256]{1,0:T(8,128)S(1)} %pad_maximum_fusion.11), channel_id=1, source_target_pairs={{1,0},{2,3},{5,4},{6,7},{9,8},{10,11},{13,12},{14,15},{17,16},{18,... | collective-permute-start | bytes 786440 | tf_op jit(solution)/shard_map/ppermute | solution.py:42
  39.0 32.6 %collective-permute-start.26 = (f32[256,256]{1,0:T(8,128)S(1)}, f32[256,256]{1,0:T(8,128)S(1)}, u32[]{:S(2)}, u32[]{:S(2)}) collective-permute-start(f32[256,256]{1,0:T(8,128)S(1)} %pad_maximum_fusion.11), channel_id=1, source_target_pairs={{0,1},{3,2},{4,5},{7,6},{8,9},{11,10},{12,13},{15,14},{16,17},{19,... | collective-permute-start | bytes 786440 | tf_op jit(solution)/shard_map/ppermute | solution.py:42
  64.3 11.0 %collective-permute-start.33 = (f32[256,256]{1,0:T(8,128)S(1)}, f32[256,256]{1,0:T(8,128)S(1)}, u32[]{:S(2)}, u32[]{:S(2)}) collective-permute-start(f32[256,256]{1,0:T(8,128)S(1)} %pad_maximum_fusion.12), channel_id=1, source_target_pairs={{1,0},{2,3},{5,4},{6,7},{9,8},{10,11},{13,12},{14,15},{17,16},{18,... | collective-permute-start | bytes 786440 | tf_op jit(solution)/shard_map/ppermute | solution.py:42
  65.6 10.9 %collective-permute-start.32 = (f32[256,256]{1,0:T(8,128)S(1)}, f32[256,256]{1,0:T(8,128)S(1)}, u32[]{:S(2)}, u32[]{:S(2)}) collective-permute-start(f32[256,256]{1,0:T(8,128)S(1)} %pad_maximum_fusion.12), channel_id=1, source_target_pairs={{0,1},{3,2},{4,5},{7,6},{8,9},{11,10},{12,13},{15,14},{16,17},{19,... | collective-permute-start | bytes 786440 | tf_op jit(solution)/shard_map/ppermute | solution.py:42
  70.2 11.3 %collective-permute-start.16 = (f32[256,256]{1,0:T(8,128)S(1)}, f32[256,256]{1,0:T(8,128)S(1)}, u32[]{:S(2)}, u32[]{:S(2)}) collective-permute-start(f32[256,256]{1,0:T(8,128)S(1)} %pad_maximum_fusion.9), channel_id=1, source_target_pairs={{9,10},{10,9},{13,14},{14,13},{17,18},{18,17},{21,22},{22,21},{25,... | collective-permute-start | bytes 786440 | tf_op jit(solution)/shard_map/ppermute | solution.py:42
  70.9 7.8 %collective-permute-start.8 = (f32[512,128]{1,0:T(8,128)S(1)}, f32[512,128]{1,0:T(8,128)S(1)}, u32[]{:S(2)}, u32[]{:S(2)}) collective-permute-start(f32[512,128]{1,0:T(8,128)S(1)} %collective-permute-done.4), channel_id=1, source_target_pairs={{5,6},{6,5}} | collective-permute-start | bytes 786440 | tf_op jit(solution)/shard_map/ppermute | solution.py:42
  79.4 7.8 %collective-permute-start.9 = (f32[512,128]{1,0:T(8,128)S(1)}, f32[512,128]{1,0:T(8,128)S(1)}, u32[]{:S(2)}, u32[]{:S(2)}) collective-permute-start(f32[512,128]{1,0:T(8,128)S(1)} %collective-permute-done.8), channel_id=1, source_target_pairs={{5,4},{6,7}} | collective-permute-start | bytes 786440 | tf_op jit(solution)/shard_map/ppermute | solution.py:42
  80.1 7.8 %collective-permute-start.28 = (f32[256,256]{1,0:T(8,128)S(1)}, f32[256,256]{1,0:T(8,128)S(1)}, u32[]{:S(2)}, u32[]{:S(2)}) collective-permute-start(f32[256,256]{1,0:T(8,128)S(1)} %pad_maximum_fusion.11), channel_id=1, source_target_pairs={{1,2},{2,1},{5,6},{6,5},{9,10},{10,9},{13,14},{14,13},{17,18},{18,... | collective-permute-start | bytes 786440 | tf_op jit(solution)/shard_map/ppermute | solution.py:42
  80.9 7.8 %collective-permute-start.34 = (f32[256,256]{1,0:T(8,128)S(1)}, f32[256,256]{1,0:T(8,128)S(1)}, u32[]{:S(2)}, u32[]{:S(2)}) collective-permute-start(f32[256,256]{1,0:T(8,128)S(1)} %pad_maximum_fusion.12), channel_id=1, source_target_pairs={{1,2},{2,1},{5,6},{6,5},{9,10},{10,9},{13,14},{14,13},{17,18},{18,... | collective-permute-start | bytes 786440 | tf_op jit(solution)/shard_map/ppermute | solution.py:42
  81.6 8.4 %collective-permute-start.17 = (f32[256,256]{1,0:T(8,128)S(1)}, f32[256,256]{1,0:T(8,128)S(1)}, u32[]{:S(2)}, u32[]{:S(2)}) collective-permute-start(f32[256,256]{1,0:T(8,128)S(1)} %collective-permute-done.16), channel_id=1, source_target_pairs={{9,8},{10,11},{13,12},{14,15},{17,16},{18,19},{21,20},{22,23},{25,... | collective-permute-start | bytes 786440 | tf_op jit(solution)/shard_map/ppermute | solution.py:42
  82.3 52.3 %collective-permute-start = (f32[512,512]{1,0:T(8,128)S(1)}, f32[512,512]{1,0:T(8,128)S(1)}, u32[]{:S(2)}, u32[]{:S(2)}) collective-permute-start(f32[512,512]{1,0:T(8,128)S(1)} %slice.140), channel_id=1, source_target_pairs={{0,4},{1,5},{2,6},{3,7}} | collective-permute-start | bytes 3145736 | tf_op jit(solution)/shard_map/ppermute | solution.py:46
  88.0 40.3 %collective-permute-start.18 = (f32[256,256]{1,0:T(8,128)S(1)}, f32[256,256]{1,0:T(8,128)S(1)}, u32[]{:S(2)}, u32[]{:S(2)}) collective-permute-start(f32[256,256]{1,0:T(8,128)S(1)} %collective-permute-done.14), channel_id=1, source_target_pairs={{9,10},{10,9},{13,14},{14,13},{17,18},{18,17},{21,22},{22,21},{25,... | collective-permute-start | bytes 786440 | tf_op jit(solution)/shard_map/ppermute | solution.py:42
  88.7 33.9 %collective-permute-start.29 = (f32[256,256]{1,0:T(8,128)S(1)}, f32[256,256]{1,0:T(8,128)S(1)}, u32[]{:S(2)}, u32[]{:S(2)}) collective-permute-start(f32[256,256]{1,0:T(8,128)S(1)} %collective-permute-done.28), channel_id=1, source_target_pairs={{1,0},{2,3},{5,4},{6,7},{9,8},{10,11},{13,12},{14,15},{17,16},{18,... | collective-permute-start | bytes 786440 | tf_op jit(solution)/shard_map/ppermute | solution.py:42
  90.0 37.5 %collective-permute-start.35 = (f32[256,256]{1,0:T(8,128)S(1)}, f32[256,256]{1,0:T(8,128)S(1)}, u32[]{:S(2)}, u32[]{:S(2)}) collective-permute-start(f32[256,256]{1,0:T(8,128)S(1)} %collective-permute-done.34), channel_id=1, source_target_pairs={{1,0},{2,3},{5,4},{6,7},{9,8},{10,11},{13,12},{14,15},{17,16},{18,... | collective-permute-start | bytes 786440 | tf_op jit(solution)/shard_map/ppermute | solution.py:42
  91.3 40.6 %collective-permute-start.24 = (f32[256,256]{1,0:T(8,128)S(1)}, f32[256,256]{1,0:T(8,128)S(1)}, u32[]{:S(2)}, u32[]{:S(2)}) collective-permute-start(f32[256,256]{1,0:T(8,128)S(1)} %collective-permute-done.20), channel_id=1, source_target_pairs={{9,10},{10,9},{13,14},{14,13},{17,18},{18,17},{21,22},{22,21},{25,... | collective-permute-start | bytes 786440 | tf_op jit(solution)/shard_map/ppermute | solution.py:42
  122.5 10.1 %collective-permute-start.30 = (f32[256,256]{1,0:T(8,128)S(1)}, f32[256,256]{1,0:T(8,128)S(1)}, u32[]{:S(2)}, u32[]{:S(2)}) collective-permute-start(f32[256,256]{1,0:T(8,128)S(1)} %collective-permute-done.26), channel_id=1, source_target_pairs={{1,2},{2,1},{5,6},{6,5},{9,10},{10,9},{13,14},{14,13},{17,18},{18,... | collective-permute-start | bytes 786440 | tf_op jit(solution)/shard_map/ppermute | solution.py:42
  128.3 26.6 %collective-permute-start.41 = (f32[512,512]{1,0:T(8,128)S(1)}, f32[512,512]{1,0:T(8,128)S(1)}, u32[]{:S(2)}, u32[]{:S(2)}) collective-permute-start(f32[512,512]{1,0:T(8,128)S(1)} %slice.140), channel_id=1, source_target_pairs={{0,1},{3,2},{4,5},{7,6}} | collective-permute-start | bytes 3145736 | tf_op jit(solution)/shard_map/ppermute | solution.py:42
  131.9 7.5 %collective-permute-start.19 = (f32[256,256]{1,0:T(8,128)S(1)}, f32[256,256]{1,0:T(8,128)S(1)}, u32[]{:S(2)}, u32[]{:S(2)}) collective-permute-start(f32[256,256]{1,0:T(8,128)S(1)} %collective-permute-done.18), channel_id=1, source_target_pairs={{9,8},{10,11},{13,12},{14,15},{17,16},{18,19},{21,20},{22,23},{25,... | collective-permute-start | bytes 786440 | tf_op jit(solution)/shard_map/ppermute | solution.py:42
  132.6 21.0 %collective-permute-start.25 = (f32[256,256]{1,0:T(8,128)S(1)}, f32[256,256]{1,0:T(8,128)S(1)}, u32[]{:S(2)}, u32[]{:S(2)}) collective-permute-start(f32[256,256]{1,0:T(8,128)S(1)} %collective-permute-done.24), channel_id=1, source_target_pairs={{9,8},{10,11},{13,12},{14,15},{17,16},{18,19},{21,20},{22,23},{25,... | collective-permute-start | bytes 786440 | tf_op jit(solution)/shard_map/ppermute | solution.py:42
  133.3 22.4 %collective-permute-start.31 = (f32[256,256]{1,0:T(8,128)S(1)}, f32[256,256]{1,0:T(8,128)S(1)}, u32[]{:S(2)}, u32[]{:S(2)}) collective-permute-start(f32[256,256]{1,0:T(8,128)S(1)} %collective-permute-done.30), channel_id=1, source_target_pairs={{1,0},{2,3},{5,4},{6,7},{9,8},{10,11},{13,12},{14,15},{17,16},{18,... | collective-permute-start | bytes 786440 | tf_op jit(solution)/shard_map/ppermute | solution.py:42
  134.6 21.1 %collective-permute-start.37 = (f32[256,256]{1,0:T(8,128)S(1)}, f32[256,256]{1,0:T(8,128)S(1)}, u32[]{:S(2)}, u32[]{:S(2)}) collective-permute-start(f32[256,256]{1,0:T(8,128)S(1)} %collective-permute-done.36), channel_id=1, source_target_pairs={{1,0},{2,3},{5,4},{6,7},{9,8},{10,11},{13,12},{14,15},{17,16},{18,... | collective-permute-start | bytes 786440 | tf_op jit(solution)/shard_map/ppermute | solution.py:42
  139.4 20.7 %collective-permute-start.1 = (f32[256,512]{1,0:T(8,128)S(1)}, f32[256,512]{1,0:T(8,128)S(1)}, u32[]{:S(2)}, u32[]{:S(2)}) collective-permute-start(f32[256,512]{1,0:T(8,128)S(1)} %slice_select_fusion.3), channel_id=1, source_target_pairs={{0,8},{1,9},{2,10},{3,11},{4,20},{5,21},{6,22},{7,23}} | collective-permute-start | bytes 1572872 | tf_op jit(solution)/shard_map/ppermute | solution.py:46
  153.6 12.0 %collective-permute-start.10 = (f32[256,512]{1,0:T(8,128)S(1)}, f32[256,512]{1,0:T(8,128)S(1)}, u32[]{:S(2)}, u32[]{:S(2)}) collective-permute-start(f32[256,512]{1,0:T(8,128)S(1)} %slice.176), channel_id=1, source_target_pairs={{4,0},{5,1},{6,2},{7,3}} | collective-permute-start | bytes 1572872 | tf_op jit(solution)/shard_map/ppermute | solution.py:46
  154.9 14.3 %collective-permute-start.42 = (f32[512,512]{1,0:T(8,128)S(1)}, f32[512,512]{1,0:T(8,128)S(1)}, u32[]{:S(2)}, u32[]{:S(2)}) collective-permute-start(f32[512,512]{1,0:T(8,128)S(1)} %collective-permute-done.41), channel_id=1, source_target_pairs={{1,5},{2,6}} | collective-permute-start | bytes 3145736 | tf_op jit(solution)/shard_map/ppermute | solution.py:46
  160.3 15.0 %collective-permute-start.2 = (f32[256,512]{1,0:T(8,128)S(1)}, f32[256,512]{1,0:T(8,128)S(1)}, u32[]{:S(2)}, u32[]{:S(2)}) collective-permute-start(f32[256,512]{1,0:T(8,128)S(1)} %broadcast_select_fusion.3), channel_id=1, source_target_pairs={{8,24},{9,25},{10,26},{11,27},{20,28},{21,29},{22,30},{23,31},{0,1... | collective-permute-start | bytes 1572872 | tf_op jit(solution)/shard_map/ppermute | solution.py:46
  165.7 10.1 %collective-permute-start.11 = (f32[256,512]{1,0:T(8,128)S(1)}, f32[256,512]{1,0:T(8,128)S(1)}, u32[]{:S(2)}, u32[]{:S(2)}) collective-permute-start(f32[256,512]{1,0:T(8,128)S(1)} %slice_select_fusion.2), channel_id=1, source_target_pairs={{0,8},{1,9},{2,10},{3,11},{4,20},{5,21},{6,22},{7,23}} | collective-permute-start | bytes 1572872 | tf_op jit(solution)/shard_map/ppermute | solution.py:46
  170.3 9.6 %collective-permute-start.43 = (f32[256,512]{1,0:T(8,128)S(1)}, f32[256,512]{1,0:T(8,128)S(1)}, u32[]{:S(2)}, u32[]{:S(2)}) collective-permute-start(f32[256,512]{1,0:T(8,128)S(1)} %slice_select_fusion.1), channel_id=1, source_target_pairs={{1,9},{2,10},{5,21},{6,22}} | collective-permute-start | bytes 1572872 | tf_op jit(solution)/shard_map/ppermute | solution.py:46
  173.4 7.4 %collective-permute-start.46 = (f32[256,512]{1,0:T(8,128)S(1)}, f32[256,512]{1,0:T(8,128)S(1)}, u32[]{:S(2)}, u32[]{:S(2)}) collective-permute-start(f32[256,512]{1,0:T(8,128)S(1)} %slice.180), channel_id=1, source_target_pairs={{5,1},{6,2}} | collective-permute-start | bytes 1572872 | tf_op jit(solution)/shard_map/ppermute | solution.py:46
  175.3 11.4 %collective-permute-start.3 = (f32[256,512]{1,0:T(8,128)S(1)}, f32[256,512]{1,0:T(8,128)S(1)}, u32[]{:S(2)}, u32[]{:S(2)}) collective-permute-start(f32[256,512]{1,0:T(8,128)S(1)} %broadcast_select_fusion.7), channel_id=1, source_target_pairs={{0,4},{1,5},{2,6},{3,7},{4,0},{5,1},{6,2},{7,3},{8,12},{9,13},{10,... | collective-permute-start | bytes 1572872 | tf_op jit(solution)/shard_map/ppermute | solution.py:46
  175.9 10.7 %collective-permute-start.12 = (f32[256,512]{1,0:T(8,128)S(1)}, f32[256,512]{1,0:T(8,128)S(1)}, u32[]{:S(2)}, u32[]{:S(2)}) collective-permute-start(f32[256,512]{1,0:T(8,128)S(1)} %broadcast_select_fusion.2), channel_id=1, source_target_pairs={{8,24},{9,25},{10,26},{11,27},{20,28},{21,29},{22,30},{23,31},{0,1... | collective-permute-start | bytes 1572872 | tf_op jit(solution)/shard_map/ppermute | solution.py:46
  180.1 7.0 %collective-permute-start.44 = (f32[256,512]{1,0:T(8,128)S(1)}, f32[256,512]{1,0:T(8,128)S(1)}, u32[]{:S(2)}, u32[]{:S(2)}) collective-permute-start(f32[256,512]{1,0:T(8,128)S(1)} %broadcast_select_fusion.1), channel_id=1, source_target_pairs={{9,25},{10,26},{21,29},{22,30},{1,17},{2,18},{5,13},{6,14}} | collective-permute-start | bytes 1572872 | tf_op jit(solution)/shard_map/ppermute | solution.py:46
  181.0 6.9 %collective-permute-start.47 = (f32[256,512]{1,0:T(8,128)S(1)}, f32[256,512]{1,0:T(8,128)S(1)}, u32[]{:S(2)}, u32[]{:S(2)}) collective-permute-start(f32[256,512]{1,0:T(8,128)S(1)} %slice_select_fusion), channel_id=1, source_target_pairs={{1,9},{2,10},{5,21},{6,22}} | collective-permute-start | bytes 1572872 | tf_op jit(solution)/shard_map/ppermute | solution.py:46
  187.1 12.5 %collective-permute-start.45 = (f32[256,512]{1,0:T(8,128)S(1)}, f32[256,512]{1,0:T(8,128)S(1)}, u32[]{:S(2)}, u32[]{:S(2)}) collective-permute-start(f32[256,512]{1,0:T(8,128)S(1)} %broadcast_select_fusion.5), channel_id=1, source_target_pairs={{1,5},{2,6},{5,1},{6,2},{9,13},{10,14},{13,9},{14,10},{17,21},{18,... | collective-permute-start | bytes 1572872 | tf_op jit(solution)/shard_map/ppermute | solution.py:46
  187.9 10.9 %collective-permute-start.48 = (f32[256,512]{1,0:T(8,128)S(1)}, f32[256,512]{1,0:T(8,128)S(1)}, u32[]{:S(2)}, u32[]{:S(2)}) collective-permute-start(f32[256,512]{1,0:T(8,128)S(1)} %broadcast_select_fusion), channel_id=1, source_target_pairs={{9,25},{10,26},{21,29},{22,30},{1,17},{2,18},{5,13},{6,14}} | collective-permute-start | bytes 1572872 | tf_op jit(solution)/shard_map/ppermute | solution.py:46
  202.8 36.4 %collective-permute-start.50 = (f32[256,512]{1,0:T(8,128)S(1)}, f32[256,512]{1,0:T(8,128)S(1)}, u32[]{:S(2)}, u32[]{:S(2)}) collective-permute-start(f32[256,512]{1,0:T(8,128)S(1)} %fusion.51), channel_id=1, source_target_pairs={{1,0},{2,3},{5,4},{6,7},{9,8},{10,11},{13,12},{14,15},{17,16},{18,... | collective-permute-start | bytes 1572872 | tf_op jit(solution)/shard_map/ppermute | solution.py:42
  204.1 46.4 %collective-permute-start.54 = (f32[256,512]{1,0:T(8,128)S(1)}, f32[256,512]{1,0:T(8,128)S(1)}, u32[]{:S(2)}, u32[]{:S(2)}) collective-permute-start(f32[256,512]{1,0:T(8,128)S(1)} %fusion.53), channel_id=1, source_target_pairs={{1,0},{2,3},{5,4},{6,7},{9,8},{10,11},{13,12},{14,15},{17,16},{18,... | collective-permute-start | bytes 1572872 | tf_op jit(solution)/shard_map/ppermute | solution.py:42
  206.8 54.9 %collective-permute-start.58 = (f32[256,512]{1,0:T(8,128)S(1)}, f32[256,512]{1,0:T(8,128)S(1)}, u32[]{:S(2)}, u32[]{:S(2)}) collective-permute-start(f32[256,512]{1,0:T(8,128)S(1)} %fusion.55), channel_id=1, source_target_pairs={{1,0},{2,3},{5,4},{6,7},{9,8},{10,11},{13,12},{14,15},{17,16},{18,... | collective-permute-start | bytes 1572872 | tf_op jit(solution)/shard_map/ppermute | solution.py:42
  209.3 63.2 %collective-permute-start.62 = (f32[256,512]{1,0:T(8,128)S(1)}, f32[256,512]{1,0:T(8,128)S(1)}, u32[]{:S(2)}, u32[]{:S(2)}) collective-permute-start(f32[256,512]{1,0:T(8,128)S(1)} %fusion.57), channel_id=1, source_target_pairs={{1,0},{2,3},{5,4},{6,7},{9,8},{10,11},{13,12},{14,15},{17,16},{18,... | collective-permute-start | bytes 1572872 | tf_op jit(solution)/shard_map/ppermute | solution.py:42
  (22 other events, 298.5 us)

commit v2 on v0

v2 whole, which is shorter than its diff:
```python
import jax
import jax.numpy as jnp
from jax import lax
from jax.sharding import PartitionSpec as P


def product(left, right):
    return jnp.dot(left, right, precision=lax.Precision.HIGH, preferred_element_type=jnp.float32)


def broadcast(value, axis, source):
    kept = jnp.where(lax.axis_index(axis) == source, value, 0).astype(value.dtype)
    return lax.psum(kept, axis)


def general(test_kernel, first_panel, second_panel, first_inverse, second_inverse):
    block = first_inverse.shape[0]
    position = lax.axis_index("row")
    first_rows = broadcast(test_kernel[:block], "row", 0)
    first_solved = product(first_inverse, first_rows)
    partial_value = test_kernel - product(lax.all_gather(first_panel, "col", axis=1, tiled=True), first_solved)
    second_rows = broadcast(partial_value[:block], "row", 1)
    second_solved = product(second_inverse, second_rows)
    final = partial_value - product(lax.all_gather(second_panel, "col", axis=1, tiled=True), second_solved)
    leading_final = jnp.where(
        position == 0, first_solved, jnp.where(position == 1, second_solved, final[:block])
    )
    return final.at[:block].set(leading_final)


AXES = ("row", "col")
ROWS, COLS = 8, 4
END_MID = ((0, 1), (3, 2))
MID_MID = ((1, 2), (2, 1))
MID_END = ((1, 0), (2, 3))


def along_col(value, pairs, rows):
    return lax.ppermute(value, AXES, [(r * COLS + a, r * COLS + b) for r in rows for a, b in pairs])


def along_row(value, pairs, cols):
    return lax.ppermute(value, AXES, [(a * COLS + c, b * COLS + c) for a, b in pairs for c in cols])


ALL_COLS = (0, 1, 2, 3)
MID_COLS = (1, 2)
SWAP = tuple((r, r ^ 1) for r in range(ROWS))


def four(test_kernel, first_panel, second_panel, first_inverse, second_inverse):
    block = first_inverse.shape[0]
    rows, width = test_kernel.shape
    raw = 2 * block
    bounds = [(2 * block, 3 * block), (3 * block, 4 * block)]
    row, col = lax.axis_index("row"), lax.axis_index("col")
    end = (col == 0) | (col == COLS - 1)
    left = col < COLS // 2
    every = range(ROWS)
    tied = lax.optimization_barrier
    even = row % 2 == 0
    half = block // 2

    def pieces(solved):
        return solved.reshape(COLS, block // COLS, width)

    def both(low, high):
        return jnp.concatenate([first_panel[low:high], second_panel[low:high]], axis=1)

    def near(mine):
        got = along_row(mine, ((0, 2), (1, 5)), ALL_COLS)
        return jnp.where((row == 2) | (row == 5), got, mine)

    def far(mine):
        got = along_row(mine, ((2, 6), (5, 7), (0, 4), (1, 3)), ALL_COLS)
        return jnp.where((row == 3) | (row == 4) | (row >= 6), got, mine)

    def whole(mine):
        other = along_row(mine, SWAP, ALL_COLS)
        low, high = jnp.where(even, mine, other), jnp.where(even, other, mine)
        first = jnp.concatenate([low[:half], high[:half]], axis=0)
        second = jnp.concatenate([low[half:], high[half:]], axis=0)
        return jnp.concatenate([pieces(first), pieces(second)], axis=1)

    most, corner_rows = range(2, ROWS), (0, 1)
    corner = first_panel[:block]
    one = (1,)
    corner_swap = along_col(corner, END_MID + MID_END, one)
    corner_mid = along_col(corner, MID_MID, one)
    raw_own = both(0, raw)
    raw_swap = along_col(raw_own, END_MID + MID_END, most)
    raw_mid = along_col(raw_own, MID_MID, most)
    corner_far = along_col(corner_swap, MID_MID, one)
    corner_c = along_col(corner_mid, MID_END, one)
    corner_cc = along_col(corner_far, MID_END, one)
    corners = jnp.concatenate(
        [
            jnp.where(end, corner, corner_swap),
            jnp.where(end, corner_swap, corner),
            jnp.where(end, corner_c, corner_mid),
            jnp.where(end, corner_cc, corner_far),
        ],
        axis=1,
    )

    top = test_kernel[:block]
    first = product(first_inverse, top)
    first = jnp.where(row == 1, along_row(first, ((0, 1),), ALL_COLS), first)
    mine_one = far(near(jnp.where(even, first[:half], first[half:])))
    own = [both(low, high) for low, high in bounds]
    few_own = both(block, raw)

    corners, mine_one, own, few_own, raw_swap, raw_mid = tied(
        (corners, mine_one, own, few_own, raw_swap, raw_mid)
    )
    raw_far = along_col(raw_swap, MID_MID, most)
    raw_c = along_col(raw_mid, MID_END, most)
    from_end = [along_col(own[0], END_MID, every)]
    hop_one = along_col(mine_one, END_MID, every)
    few_swap = along_col(few_own, END_MID + MID_END, corner_rows)
    few_mid = along_col(few_own, MID_MID, corner_rows)
    slices = pieces(first)
    slices = jnp.where(left, slices, slices[::-1]).reshape(block, width)
    second = product(second_inverse, top - product(corners, slices))
    upper = along_row(second[:half], ((1, 0),), ALL_COLS)
    mine_two = near(jnp.where(even, upper, second[half:]))

    mine_two, few_swap, few_mid, own = tied((mine_two, few_swap, few_mid, own))
    few_far = along_col(few_swap, MID_MID, corner_rows)
    few_c = along_col(few_mid, MID_END, corner_rows)
    from_mid = [along_col(own[0], MID_MID, every)]
    mine_two = far(mine_two)

    mine_two, raw_far, raw_c, from_end[0], hop_one, few_far, few_c, own = tied(
        (mine_two, raw_far, raw_c, from_end[0], hop_one, few_far, few_c, own)
    )
    hop_two = along_col(mine_two, END_MID, every)
    raw_cc = along_col(raw_far, MID_END, most)
    few_cc = along_col(few_far, MID_END, corner_rows)
    from_far = [along_col(from_end[0], MID_MID, every)]
    from_mid.append(along_col(own[1], MID_MID, every))
    solved_own = whole(jnp.concatenate([mine_one, mine_two], axis=0))

    hop_two, solved_own, own = tied((hop_two, solved_own, own))
    from_end.append(along_col(own[1], END_MID, every))
    solved_end = whole(jnp.concatenate([hop_one, hop_two], axis=0))
    solved_end = jnp.where(left, solved_end, solved_end[::-1]).reshape(2 * block, width)
    solved_turned = jnp.where(left, solved_own, solved_own[::-1]).reshape(2 * block, width)

    solved_end, solved_turned, from_end[1], from_far[0], from_mid[0] = tied(
        (solved_end, solved_turned, from_end[1], from_far[0], from_mid[0])
    )
    from_far.append(along_col(from_end[1], MID_MID, every))

    def panels(i):
        return jnp.concatenate([from_end[i], own[i], from_mid[i], from_far[i]], axis=1)

    sent = product(panels(0), solved_end)
    sent, raw_cc, few_cc = tied((sent, raw_cc, few_cc))
    returned = [along_col(sent, MID_END, every)]

    def raw_panels(own, swap, mid, far, c, cc):
        return jnp.concatenate(
            [
                jnp.where(end, own, swap),
                jnp.where(end, swap, own),
                jnp.where(end, c, mid),
                jnp.where(end, cc, far),
            ],
            axis=1,
        )

    few_panels = raw_panels(few_own, few_swap, few_mid, few_far, few_c, few_cc)
    most_panels = raw_panels(raw_own, raw_swap, raw_mid, raw_far, raw_c, raw_cc)
    first_own = solved_own[:, : block // COLS].reshape(block, width)
    second_own = solved_own[:, block // COLS :].reshape(block, width)
    lead = test_kernel[:block] - product(most_panels[:block], solved_turned)
    lead = jnp.where(row == 0, first_own, jnp.where(row == 1, second_own, lead))
    lower = jnp.where(row < 2, few_panels, most_panels[block:])
    out = [lead, test_kernel[block:raw] - product(lower, solved_turned)]
    mine = [test_kernel[low:high] - product(panels(i), solved_turned) for i, (low, high) in enumerate(bounds)]
    returned.append(along_col(product(panels(1), solved_end), MID_END, every))
    for i, (low, high) in enumerate(bounds):
        out.append(jnp.where(end, test_kernel[low:high] - returned[i], mine[i]))
    return jnp.concatenate(out, axis=0)


def solution(mesh):
    in_specs = (P("row", "col"), P("row", "col"), P("row", "col"), P(), P())
    out_specs = P("row", "col")
    body = four if dict(mesh.shape) == {"row": ROWS, "col": COLS} else general
    return jax.shard_map(body, mesh=mesh, in_specs=in_specs, out_specs=out_specs, check_vma=False)
```

time: 220 us -> 187 us (0.85)
  waiting for transfers between devices: 159 us -> 88.4 us
  starting transfers between devices: 0.31 us -> 62 us
  between operations: 14.9 us -> 0.83 us
  matrix products: 26.7 us -> 17 us
  local copies, waits for them, and re-layouts: 12.8 us -> 4.71 us
  other arithmetic: 6.08 us -> 13.2 us
    psum x2 -> x0, waiting for transfers between devices: 113 us -> none  [broadcast(): return lax.psum(kept, axis)]
    ppermute x0 -> x33, waiting for transfers between devices: none -> 88.4 us  [the longest x25 74 us: along_col(): lax.ppermute(value, AXES, [(r * COLS + a, r * COLS + b) for r in rows for...]
    ppermute x0 -> x33, starting transfers between devices: none -> 62 us  [the longest x25 47.4 us: along_col(): lax.ppermute(value, AXES, [(r * COLS + a, r * COLS + b) for r in rows for...]
    all_gather x2 -> x0, waiting for transfers between devices: 45.2 us -> none  [the longest x1 22.7 us: per_device(): lax.all_gather(first_panel, 'col', axis=1, tiled=True)]
    dot_general x4 -> x9, matrix products: 26.7 us -> 17 us  [product(): jnp.dot(left, right, precision=lax.Precision.HIGH, preferred_element_type...]
    scatter x1 -> x0, local copies, waits for them, and re-layouts: 5.34 us -> none  [per_device(): return final.at[:block].set(leading_final)]
    concatenate x0 -> x12, other arithmetic: none -> 4.94 us  [the longest x1 2.46 us: four(): return jnp.concatenate(out, axis=0)]
    select_n x2 -> x21, other arithmetic: 3.46 us -> 8.25 us  [the longest x2 2.55 us: raw_panels(): jnp.where(end, own, swap)]
  transfers between devices with their start and end apart: 4 -> 33, of which waited for: 4 -> 13; matrix products, arithmetic and copies ran while one was open for 3% -> 13% of each run, Pallas kernels for 0% -> 0%
where the time goes in v2:
time: 187 us; the launch traced here: 186 us
  waiting for transfers between devices  88.4 us (47%)
  starting transfers between devices  62 us (33%)
  matrix products  17 us (9%)
  other arithmetic  13.2 us (7%)
  local copies, waits for them, and re-layouts  4.71 us (3%)
    ppermute x25, waiting for transfers between devices, along_col(): lax.ppermute(value, AXES, [(r * COLS + a, r * COLS + b) for r in rows for...  74 us
    ppermute x25, starting transfers between devices, along_col(): lax.ppermute(value, AXES, [(r * COLS + a, r * COLS + b) for r in rows for...  47.4 us
    dot_general x9, matrix products, product(): jnp.dot(left, right, precision=lax.Precision.HIGH, preferred_element_type...  17 us
    ppermute x8, starting transfers between devices, along_row(): lax.ppermute(value, AXES, [(a * COLS + c, b * COLS + c) for a, b in pairs...  14.6 us
    ppermute x8, waiting for transfers between devices, along_row(): lax.ppermute(value, AXES, [(a * COLS + c, b * COLS + c) for a, b in pairs...  14.4 us
  transfers between devices with their start and end apart: 33, of which 13 were waited for; matrix products, arithmetic and copies ran while one was open for 13% of the time, Pallas kernels for 0%

profile of v2, /device:TPU:0, one launch (start us, length us, event | category | flops | bytes accessed | tf_op | source)
XLA Modules:
  0.0 186.1 jit_solution(6753087500120156890)
XLA Ops:
  0.0 1.2 copy-done
  1.2 2.2 %fusion.16 = f32[512,512]{1,0:T(8,128)S(1)} fusion(f32[512,512]{1,0:T(8,128)S(1)} %copy-done, f32[2048,512]{1,0:T(8,128)} %param.5), kind=kOutput, calls=%fused_computation.35 | convolution fusion | flops 805306368 | bytes 3145728 | tf_op jit(solution)/shard_map/dot_general | solution.py:8
  3.5 3.3 %collective-permute-start.5 = (f32[512,512]{1,0:T(8,128)S(1)}, f32[512,512]{1,0:T(8,128)}, u32[]{:S(2)}, u32[]{:S(2)}) collective-permute-start(f32[512,512]{1,0:T(8,128)S(1)} %fusion.16), channel_id=1, source_target_pairs={{0,4},{1,5},{2,6},{3,7}} | collective-permute-start | bytes 3145736 | tf_op jit(solution)/shard_map/ppermute | solution.py:43
  6.8 1.4 collective-permute-start
  8.2 1.4 collective-permute-start.1
  10.7 1.6 collective-permute-start.8
  12.3 1.6 collective-permute-start.9
  13.9 1.2 fusion.26
  16.8 5.0 %collective-permute-start.6 = (f32[256,512]{1,0:T(8,128)S(1)}, f32[256,512]{1,0:T(8,128)S(1)}, u32[]{:S(2)}, u32[]{:S(2)}) collective-permute-start(f32[256,512]{1,0:T(8,128)S(1)} %slice_select_fusion.5), channel_id=1, source_target_pairs={{0,8},{1,9},{2,10},{3,11},{4,20},{5,21},{6,22},{7,23}} | collective-permute-start | bytes 1572872 | tf_op jit(solution)/shard_map/ppermute | solution.py:43
  23.8 4.7 %collective-permute-done.6 = f32[256,512]{1,0:T(8,128)S(1)} collective-permute-done((f32[256,512]{1,0:T(8,128)S(1)}, f32[256,512]{1,0:T(8,128)S(1)}, u32[]{:S(2)}, u32[]{:S(2)}) %collective-permute-start.6) | collective-permute-done | bytes 524320 | tf_op jit(solution)/shard_map/ppermute | solution.py:43
  28.7 1.3 collective-permute-start.7
  30.2 6.4 %collective-permute-done.7 = f32[256,512]{1,0:T(8,128)S(1)} collective-permute-done((f32[256,512]{1,0:T(8,128)S(1)}, f32[256,512]{1,0:T(8,128)S(1)}, u32[]{:S(2)}, u32[]{:S(2)}) %collective-permute-start.7) | collective-permute-done | bytes 524320 | tf_op jit(solution)/shard_map/ppermute | solution.py:43
  36.8 2.3 %convolution_subtract_fusion.2 = f32[512,512]{1,0:T(8,128)S(1)} fusion(f32[512,512]{1,0:T(8,128)S(1)} %pad_maximum_fusion.4, f32[512,512]{1,0:T(8,128)S(1)} %bitcast.38, f32[2048,512]{1,0:T(8,128)} %param.5), kind=kOutput, calls=%fused_computation.22 | convolution fusion | flops 805568512 | bytes 4194304 | tf_op jit(solution)/shard_map/dot_general | solution.py:8
  40.2 1.3 collective-permute-start.10
  41.5 2.5 %collective-permute-done.10 = f32[256,512]{1,0:T(8,128)S(1)} collective-permute-done((f32[256,512]{1,0:T(8,128)S(1)}, f32[256,512]{1,0:T(8,128)S(1)}, u32[]{:S(2)}, u32[]{:S(2)}) %collective-permute-start.10) | collective-permute-done | bytes 524320 | tf_op jit(solution)/shard_map/ppermute | solution.py:43
  44.1 1.3 collective-permute-start.11
  45.4 6.3 %collective-permute-start.12 = (f32[512,256]{1,0:T(8,128)S(1)}, f32[512,256]{1,0:T(8,128)}, u32[]{:S(2)}, u32[]{:S(2)}) collective-permute-start(f32[512,256]{1,0:T(8,128)S(1)} %pad_maximum_fusion.12), channel_id=1, source_target_pairs={{0,1},{3,2},{1,0},{2,3},{4,5},{7,6},{5,4},{6,7}} | collective-permute-start | bytes 1572872 | tf_op jit(solution)/shard_map/ppermute | solution.py:39
  51.7 1.5 collective-permute-start.13
  53.2 1.6 collective-permute-start.15
  54.8 4.1 %collective-permute-start.17 = (f32[512,256]{1,0:T(8,128)S(1)}, f32[512,256]{1,0:T(8,128)S(1)}, u32[]{:S(2)}, u32[]{:S(2)}) collective-permute-start(f32[512,256]{1,0:T(8,128)S(1)} %get-tuple-element.56), channel_id=1, source_target_pairs={{0,1},{3,2},{4,5},{7,6},{8,9},{11,10},{12,13},{15,14},{16,17},{19,... | collective-permute-start | bytes 1572872 | tf_op jit(solution)/shard_map/ppermute | solution.py:39
  59.0 5.0 %collective-permute-done.12 = f32[512,256]{1,0:T(8,128)} collective-permute-done((f32[512,256]{1,0:T(8,128)S(1)}, f32[512,256]{1,0:T(8,128)}, u32[]{:S(2)}, u32[]{:S(2)}) %collective-permute-start.12) | collective-permute-done | bytes 524320 | tf_op jit(solution)/shard_map/ppermute | solution.py:39
  64.1 2.1 %collective-permute-start.14 = (f32[256,512]{1,0:T(8,128)S(1)}, f32[256,512]{1,0:T(8,128)}, u32[]{:S(2)}, u32[]{:S(2)}) collective-permute-start(f32[256,512]{1,0:T(8,128)S(1)} %broadcast_select_fusion.13), channel_id=1, source_target_pairs={{8,24},{9,25},{10,26},{11,27},{20,28},{21,29},{22,30},{23,31},{0,1... | collective-permute-start | bytes 1572872 | tf_op jit(solution)/shard_map/ppermute | solution.py:43
  66.2 1.6 collective-permute-start.16
  67.8 5.4 %collective-permute-start.18 = (f32[256,512]{1,0:T(8,128)S(1)}, f32[256,512]{1,0:T(8,128)}, u32[]{:S(2)}, u32[]{:S(2)}) collective-permute-start(f32[256,512]{1,0:T(8,128)S(1)} %broadcast_select_fusion.16), channel_id=1, source_target_pairs={{0,1},{3,2},{4,5},{7,6},{8,9},{11,10},{12,13},{15,14},{16,17},{19,... | collective-permute-start | bytes 1572872 | tf_op jit(solution)/shard_map/ppermute | solution.py:39
  73.2 2.1 %collective-permute-done.17 = f32[512,256]{1,0:T(8,128)S(1)} collective-permute-done((f32[512,256]{1,0:T(8,128)S(1)}, f32[512,256]{1,0:T(8,128)S(1)}, u32[]{:S(2)}, u32[]{:S(2)}) %collective-permute-start.17) | collective-permute-done | bytes 524320 | tf_op jit(solution)/shard_map/ppermute | solution.py:39
  75.3 1.5 collective-permute-start.19
  76.8 1.3 collective-permute-start.20
  78.2 6.5 %collective-permute-done.18 = f32[256,512]{1,0:T(8,128)} collective-permute-done((f32[256,512]{1,0:T(8,128)S(1)}, f32[256,512]{1,0:T(8,128)}, u32[]{:S(2)}, u32[]{:S(2)}) %collective-permute-start.18) | collective-permute-done | bytes 524320 | tf_op jit(solution)/shard_map/ppermute | solution.py:39
  84.7 5.5 %collective-permute-done.20 = f32[512,256]{1,0:T(8,128)} collective-permute-done((f32[512,256]{1,0:T(8,128)}, f32[512,256]{1,0:T(8,128)}, u32[]{:S(2)}, u32[]{:S(2)}) %collective-permute-start.20) | collective-permute-done | bytes 524320 | tf_op jit(solution)/shard_map/ppermute | solution.py:39
  90.3 1.4 broadcast_select_fusion.3
  93.7 4.1 %collective-permute-start.21 = (f32[256,512]{1,0:T(8,128)S(1)}, f32[256,512]{1,0:T(8,128)S(1)}, u32[]{:S(2)}, u32[]{:S(2)}) collective-permute-start(f32[256,512]{1,0:T(8,128)S(1)} %broadcast_select_fusion.15), channel_id=1, source_target_pairs={{0,1},{3,2},{4,5},{7,6},{8,9},{11,10},{12,13},{15,14},{16,17},{19,... | collective-permute-start | bytes 1572872 | tf_op jit(solution)/shard_map/ppermute | solution.py:39
  103.0 6.3 %collective-permute-done.21 = f32[256,512]{1,0:T(8,128)S(1)} collective-permute-done((f32[256,512]{1,0:T(8,128)S(1)}, f32[256,512]{1,0:T(8,128)S(1)}, u32[]{:S(2)}, u32[]{:S(2)}) %collective-permute-start.21) | collective-permute-done | bytes 524320 | tf_op jit(solution)/shard_map/ppermute | solution.py:39
  109.4 1.4 broadcast_select_fusion.1
  112.0 4.4 %collective-permute-start.24 = (f32[512,256]{1,0:T(8,128)S(1)}, f32[512,256]{1,0:T(8,128)S(1)}, u32[]{:S(2)}, u32[]{:S(2)}) collective-permute-start(f32[512,256]{1,0:T(8,128)S(1)} %get-tuple-element.59), channel_id=1, source_target_pairs={{0,1},{3,2},{4,5},{7,6},{8,9},{11,10},{12,13},{15,14},{16,17},{19,... | collective-permute-start | bytes 1572872 | tf_op jit(solution)/shard_map/ppermute | solution.py:39
  117.5 1.3 collective-permute-start.28
  118.8 9.1 %collective-permute-done.24 = f32[512,256]{1,0:T(8,128)S(1)} collective-permute-done((f32[512,256]{1,0:T(8,128)S(1)}, f32[512,256]{1,0:T(8,128)S(1)}, u32[]{:S(2)}, u32[]{:S(2)}) %collective-permute-start.24) | collective-permute-done | bytes 524320 | tf_op jit(solution)/shard_map/ppermute | solution.py:39
  128.9 1.9 fusion.27
  130.8 2.5 %collective-permute-done.28 = f32[512,256]{1,0:T(8,128)S(1)} collective-permute-done((f32[512,256]{1,0:T(8,128)}, f32[512,256]{1,0:T(8,128)S(1)}, u32[]{:S(2)}, u32[]{:S(2)}) %collective-permute-start.28) | collective-permute-done | bytes 524320 | tf_op jit(solution)/shard_map/ppermute | solution.py:39
  133.3 1.3 collective-permute-start.29
  135.8 1.9 fusion.28
  137.6 1.3 collective-permute-start.32
  139.0 1.9 %fusion.13 = f32[512,512]{1,0:T(8,128)S(1)} fusion(f32[1024,512]{1,0:T(8,128)S(1)} %bitcast.31, f32[1024,1024]{1,0:T(8,128)S(1)} %pad_maximum_fusion, f32[512,256]{1,0:T(8,128)S(1)} %broadcast_select_fusion.9, f32[512,256]{1,0:T(8,128)S(1)} %broadcast_select_fusion.10, f32[512,256]{1,0:T(8,128)S(1)} %get-tuple-element.82, ...), kind=kOutput, calls=%fused_computation.23 | convolution fusion | flops 1612972032 | bytes 8388609 | tf_op jit(solution)/shard_map/dot_general | solution.py:8
  140.9 2.0 %fusion.14 = f32[512,512]{1,0:T(8,128)S(1)} fusion(f32[4,128,512]{2,1,0:T(8,128)S(1)} %get-tuple-element.72, f32[4,128,512]{2,1,0:T(8,128)S(1)} %get-tuple-element.71, f32[1024,512]{1,0:T(8,128)S(1)} %bitcast.32, f32[1024,1024]{1,0:T(8,128)S(1)} %pad_maximum_fusion, f32[2048,512]{1,0:T(8,128)S(1)} %copy-done.2, pred[]{:T(512)S(6)} %eq.42, pred[]{:T(512)S(6)} %eq.34), kind=kOutput, calls=%fused_computation.31 | convolution fusion | flops 1611399168 | bytes 8388610 | tf_op jit(solution)/shard_map/dot_general | solution.py:8
  142.9 18.4 %collective-permute-done.29 = f32[512,512]{1,0:T(8,128)S(1)} collective-permute-done((f32[512,512]{1,0:T(8,128)S(1)}, f32[512,512]{1,0:T(8,128)S(1)}, u32[]{:S(2)}, u32[]{:S(2)}) %collective-permute-start.29) | collective-permute-done | bytes 1048608 | tf_op jit(solution)/shard_map/ppermute | solution.py:39
  161.3 1.9 %subtract_select_fusion.1 = f32[512,512]{1,0:T(8,128)S(1)} fusion(f32[512,512]{1,0:T(8,128)S(1)} %collective-permute-done.29, f32[2048,512]{1,0:T(8,128)S(1)} %copy-done.2, f32[512,1024]{1,0:T(8,128)S(1)} %constant_dynamic-update-slice_fusion.4, f32[1024,512]{1,0:T(8,128)S(1)} %bitcast.33, pred[]{:T(512)S(6)} %or.18), kind=kOutput, calls=%fused_computation.33 | convolution fusion | flops 1611399168 | bytes 7340033 | tf_op jit(solution)/shard_map/dot_general | solution.py:8
  163.2 18.6 %collective-permute-done.32 = f32[512,512]{1,0:T(8,128)S(1)} collective-permute-done((f32[512,512]{1,0:T(8,128)S(1)}, f32[512,512]{1,0:T(8,128)S(1)}, u32[]{:S(2)}, u32[]{:S(2)}) %collective-permute-start.32) | collective-permute-done | bytes 1048608 | tf_op jit(solution)/shard_map/ppermute | solution.py:39
  181.7 1.9 %subtract_select_fusion = f32[512,512]{1,0:T(8,128)S(1)} fusion(f32[512,512]{1,0:T(8,128)S(1)} %collective-permute-done.32, f32[2048,512]{1,0:T(8,128)S(1)} %copy-done.2, f32[512,1024]{1,0:T(8,128)S(1)} %constant_dynamic-update-slice_fusion.8, f32[1024,512]{1,0:T(8,128)S(1)} %bitcast.34, pred[]{:T(512)S(6)} %or.18), kind=kOutput, calls=%fused_computation.32 | convolution fusion | flops 1611399168 | bytes 7340033 | tf_op jit(solution)/shard_map/dot_general | solution.py:8
  183.7 2.5 %pad_maximum_fusion.1 = f32[2048,512]{1,0:T(8,128)} fusion(f32[512,512]{1,0:T(8,128)S(1)} %subtract_select_fusion, f32[512,512]{1,0:T(8,128)S(1)} %subtract_select_fusion.1, f32[512,512]{1,0:T(8,128)S(1)} %fusion.13, f32[512,512]{1,0:T(8,128)S(1)} %fusion.14), kind=kLoop, calls=%fused_computation.1 | loop fusion | flops 3145728 | bytes 8388608 | tf_op jit(solution)/shard_map/concatenate | solution.py:185
  (102 shorter events, 18.1 us)
Async XLA Ops:
  0.0 1.2 copy-start
  0.0 6.8 %copy-start.3 = (f32[2048,128]{1,0:T(8,128)S(1)}, f32[2048,128]{1,0:T(8,128)}, u32[]{:S(2)}) copy-start(f32[2048,128]{1,0:T(8,128)} %param.6) | copy-start | bytes 3145732
  0.0 9.6 %copy-start.6 = (f32[2048,128]{1,0:T(8,128)S(1)}, f32[2048,128]{1,0:T(8,128)}, u32[]{:S(2)}) copy-start(f32[2048,128]{1,0:T(8,128)} %param.7) | copy-start | bytes 3145732
  3.5 13.0 %collective-permute-start.5 = (f32[512,512]{1,0:T(8,128)S(1)}, f32[512,512]{1,0:T(8,128)}, u32[]{:S(2)}, u32[]{:S(2)}) collective-permute-start(f32[512,512]{1,0:T(8,128)S(1)} %fusion.16), channel_id=1, source_target_pairs={{0,4},{1,5},{2,6},{3,7}} | collective-permute-start | bytes 3145736 | tf_op jit(solution)/shard_map/ppermute | solution.py:43
  6.8 8.3 %collective-permute-start = (f32[512,128]{1,0:T(8,128)S(1)}, f32[512,128]{1,0:T(8,128)}, u32[]{:S(2)}, u32[]{:S(2)}) collective-permute-start(f32[512,128]{1,0:T(8,128)S(1)} %slice.91), channel_id=1, source_target_pairs={{4,5},{7,6},{5,4},{6,7}} | collective-permute-start | bytes 786440 | tf_op jit(solution)/shard_map/ppermute | solution.py:39
  8.2 7.6 %collective-permute-start.1 = (f32[512,128]{1,0:T(8,128)S(1)}, f32[512,128]{1,0:T(8,128)}, u32[]{:S(2)}, u32[]{:S(2)}) collective-permute-start(f32[512,128]{1,0:T(8,128)S(1)} %slice.91), channel_id=1, source_target_pairs={{5,6},{6,5}} | collective-permute-start | bytes 786440 | tf_op jit(solution)/shard_map/ppermute | solution.py:39
  10.7 26.1 %collective-permute-start.8 = (f32[1024,256]{1,0:T(8,128)}, f32[1024,256]{1,0:T(8,128)}, u32[]{:S(2)}, u32[]{:S(2)}) collective-permute-start(f32[1024,256]{1,0:T(8,128)} %pad_maximum_fusion.5), channel_id=1, source_target_pairs={{8,9},{11,10},{9,8},{10,11},{12,13},{15,14},{13,12},{14,15},{16,17... | collective-permute-start | bytes 3145736 | tf_op jit(solution)/shard_map/ppermute | solution.py:39
  12.3 24.5 %collective-permute-start.9 = (f32[1024,256]{1,0:T(8,128)}, f32[1024,256]{1,0:T(8,128)}, u32[]{:S(2)}, u32[]{:S(2)}) collective-permute-start(f32[1024,256]{1,0:T(8,128)} %pad_maximum_fusion.5), channel_id=1, source_target_pairs={{9,10},{10,9},{13,14},{14,13},{17,18},{18,17},{21,22},{22,21},{25,... | collective-permute-start | bytes 3145736 | tf_op jit(solution)/shard_map/ppermute | solution.py:39
  15.1 7.9 %collective-permute-start.3 = (f32[512,128]{1,0:T(8,128)}, f32[512,128]{1,0:T(8,128)S(1)}, u32[]{:S(2)}, u32[]{:S(2)}) collective-permute-start(f32[512,128]{1,0:T(8,128)} %collective-permute-done), channel_id=1, source_target_pairs={{5,6},{6,5}} | collective-permute-start | bytes 786440 | tf_op jit(solution)/shard_map/ppermute | solution.py:39
  15.8 7.9 %collective-permute-start.2 = (f32[512,128]{1,0:T(8,128)}, f32[512,128]{1,0:T(8,128)S(1)}, u32[]{:S(2)}, u32[]{:S(2)}) collective-permute-start(f32[512,128]{1,0:T(8,128)} %collective-permute-done.1), channel_id=1, source_target_pairs={{5,4},{6,7}} | collective-permute-start | bytes 786440 | tf_op jit(solution)/shard_map/ppermute | solution.py:39
  16.8 11.7 %collective-permute-start.6 = (f32[256,512]{1,0:T(8,128)S(1)}, f32[256,512]{1,0:T(8,128)S(1)}, u32[]{:S(2)}, u32[]{:S(2)}) collective-permute-start(f32[256,512]{1,0:T(8,128)S(1)} %slice_select_fusion.5), channel_id=1, source_target_pairs={{0,8},{1,9},{2,10},{3,11},{4,20},{5,21},{6,22},{7,23}} | collective-permute-start | bytes 1572872 | tf_op jit(solution)/shard_map/ppermute | solution.py:43
  23.0 31.8 %copy-start.4 = (f32[512,256]{1,0:T(8,128)}, f32[512,256]{1,0:T(8,128)S(1)}, u32[]{:S(2)}) copy-start(f32[512,256]{1,0:T(8,128)S(1)} %get-tuple-element.56) | copy-start | bytes 1572868
  23.1 6.9 %collective-permute-start.4 = (f32[512,128]{1,0:T(8,128)S(1)}, f32[512,128]{1,0:T(8,128)S(1)}, u32[]{:S(2)}, u32[]{:S(2)}) collective-permute-start(f32[512,128]{1,0:T(8,128)S(1)} %collective-permute-done.3), channel_id=1, source_target_pairs={{5,4},{6,7}} | collective-permute-start | bytes 786440 | tf_op jit(solution)/shard_map/ppermute | solution.py:39
  28.7 8.0 %collective-permute-start.7 = (f32[256,512]{1,0:T(8,128)S(1)}, f32[256,512]{1,0:T(8,128)S(1)}, u32[]{:S(2)}, u32[]{:S(2)}) collective-permute-start(f32[256,512]{1,0:T(8,128)S(1)} %broadcast_select_fusion.14), channel_id=1, source_target_pairs={{8,24},{9,25},{10,26},{11,27},{20,28},{21,29},{22,30},{23,31},{0,1... | collective-permute-start | bytes 1572872 | tf_op jit(solution)/shard_map/ppermute | solution.py:43
  36.8 2.3 %copy-start.7 = (f32[512,512]{1,0:T(8,128)S(1)}, f32[512,512]{1,0:T(8,128)}, u32[]{:S(2)}) copy-start(f32[512,512]{1,0:T(8,128)} %param.9) | copy-start | bytes 3145732
  40.2 3.8 %collective-permute-start.10 = (f32[256,512]{1,0:T(8,128)S(1)}, f32[256,512]{1,0:T(8,128)S(1)}, u32[]{:S(2)}, u32[]{:S(2)}) collective-permute-start(f32[256,512]{1,0:T(8,128)S(1)} %slice.121), channel_id=1, source_target_pairs={{4,0},{5,1},{6,2},{7,3}} | collective-permute-start | bytes 1572872 | tf_op jit(solution)/shard_map/ppermute | solution.py:43
  44.1 14.9 %collective-permute-start.11 = (f32[256,512]{1,0:T(8,128)S(1)}, f32[256,512]{1,0:T(8,128)S(1)}, u32[]{:S(2)}, u32[]{:S(2)}) collective-permute-start(f32[256,512]{1,0:T(8,128)S(1)} %slice_select_fusion.4), channel_id=1, source_target_pairs={{0,8},{1,9},{2,10},{3,11},{4,20},{5,21},{6,22},{7,23}} | collective-permute-start | bytes 1572872 | tf_op jit(solution)/shard_map/ppermute | solution.py:43
  45.4 18.7 %collective-permute-start.12 = (f32[512,256]{1,0:T(8,128)S(1)}, f32[512,256]{1,0:T(8,128)}, u32[]{:S(2)}, u32[]{:S(2)}) collective-permute-start(f32[512,256]{1,0:T(8,128)S(1)} %pad_maximum_fusion.12), channel_id=1, source_target_pairs={{0,1},{3,2},{1,0},{2,3},{4,5},{7,6},{5,4},{6,7}} | collective-permute-start | bytes 1572872 | tf_op jit(solution)/shard_map/ppermute | solution.py:39
  51.7 12.4 %collective-permute-start.13 = (f32[512,256]{1,0:T(8,128)S(1)}, f32[512,256]{1,0:T(8,128)}, u32[]{:S(2)}, u32[]{:S(2)}) collective-permute-start(f32[512,256]{1,0:T(8,128)S(1)} %pad_maximum_fusion.12), channel_id=1, source_target_pairs={{1,2},{2,1},{5,6},{6,5}} | collective-permute-start | bytes 1572872 | tf_op jit(solution)/shard_map/ppermute | solution.py:39
  53.2 31.5 %collective-permute-start.15 = (f32[1024,256]{1,0:T(8,128)}, f32[1024,256]{1,0:T(8,128)}, u32[]{:S(2)}, u32[]{:S(2)}) collective-permute-start(f32[1024,256]{1,0:T(8,128)} %collective-permute-done.8), channel_id=1, source_target_pairs={{9,10},{10,9},{13,14},{14,13},{17,18},{18,17},{21,22},{22,21},{25,... | collective-permute-start | bytes 3145736 | tf_op jit(solution)/shard_map/ppermute | solution.py:39
  54.8 20.5 %collective-permute-start.17 = (f32[512,256]{1,0:T(8,128)S(1)}, f32[512,256]{1,0:T(8,128)S(1)}, u32[]{:S(2)}, u32[]{:S(2)}) collective-permute-start(f32[512,256]{1,0:T(8,128)S(1)} %get-tuple-element.56), channel_id=1, source_target_pairs={{0,1},{3,2},{4,5},{7,6},{8,9},{11,10},{12,13},{15,14},{16,17},{19,... | collective-permute-start | bytes 1572872 | tf_op jit(solution)/shard_map/ppermute | solution.py:39
  64.1 12.7 %collective-permute-start.14 = (f32[256,512]{1,0:T(8,128)S(1)}, f32[256,512]{1,0:T(8,128)}, u32[]{:S(2)}, u32[]{:S(2)}) collective-permute-start(f32[256,512]{1,0:T(8,128)S(1)} %broadcast_select_fusion.13), channel_id=1, source_target_pairs={{8,24},{9,25},{10,26},{11,27},{20,28},{21,29},{22,30},{23,31},{0,1... | collective-permute-start | bytes 1572872 | tf_op jit(solution)/shard_map/ppermute | solution.py:43
  66.2 18.5 %collective-permute-start.16 = (f32[1024,256]{1,0:T(8,128)}, f32[1024,256]{1,0:T(8,128)}, u32[]{:S(2)}, u32[]{:S(2)}) collective-permute-start(f32[1024,256]{1,0:T(8,128)} %collective-permute-done.9), channel_id=1, source_target_pairs={{9,8},{10,11},{13,12},{14,15},{17,16},{18,19},{21,20},{22,23},{25,... | collective-permute-start | bytes 3145736 | tf_op jit(solution)/shard_map/ppermute | solution.py:39
  67.8 16.9 %collective-permute-start.18 = (f32[256,512]{1,0:T(8,128)S(1)}, f32[256,512]{1,0:T(8,128)}, u32[]{:S(2)}, u32[]{:S(2)}) collective-permute-start(f32[256,512]{1,0:T(8,128)S(1)} %broadcast_select_fusion.16), channel_id=1, source_target_pairs={{0,1},{3,2},{4,5},{7,6},{8,9},{11,10},{12,13},{15,14},{16,17},{19,... | collective-permute-start | bytes 1572872 | tf_op jit(solution)/shard_map/ppermute | solution.py:39
  75.3 1.5 copy-start.8
  75.3 9.4 %collective-permute-start.19 = (f32[512,256]{1,0:T(8,128)}, f32[512,256]{1,0:T(8,128)}, u32[]{:S(2)}, u32[]{:S(2)}) collective-permute-start(f32[512,256]{1,0:T(8,128)} %collective-permute-done.12), channel_id=1, source_target_pairs={{1,2},{2,1},{5,6},{6,5}} | collective-permute-start | bytes 1572872 | tf_op jit(solution)/shard_map/ppermute | solution.py:39
  76.8 13.4 %collective-permute-start.20 = (f32[512,256]{1,0:T(8,128)}, f32[512,256]{1,0:T(8,128)}, u32[]{:S(2)}, u32[]{:S(2)}) collective-permute-start(f32[512,256]{1,0:T(8,128)} %collective-permute-done.13), channel_id=1, source_target_pairs={{1,0},{2,3},{5,4},{6,7}} | collective-permute-start | bytes 1572872 | tf_op jit(solution)/shard_map/ppermute | solution.py:39
  90.2 1.5 copy-start.5
  90.2 11.3 %collective-permute-start.22 = (f32[512,512]{1,0:T(8,128)S(1)}, f32[512,512]{1,0:T(8,128)S(1)}, u32[]{:S(2)}, u32[]{:S(2)}) collective-permute-start(f32[512,512]{1,0:T(8,128)S(1)} %constant_dynamic-update-slice_fusion), channel_id=1, source_target_pairs={{0,4},{1,5},{2,6},{3,7},{4,0},{5,1},{6,2},{7,3},{8,12},{9,13},{10,... | collective-permute-start | bytes 3145736 | tf_op jit(solution)/shard_map/ppermute | solution.py:43
  91.8 6.0 %copy-start.9 = (f32[512,256]{1,0:T(8,128)S(1)}, f32[512,256]{1,0:T(8,128)}, u32[]{:S(2)}) copy-start(f32[512,256]{1,0:T(8,128)} %copy-done.8) | copy-start | bytes 1572868
  91.8 25.7 %collective-permute-start.26 = (f32[512,256]{1,0:T(8,128)S(1)}, f32[512,256]{1,0:T(8,128)S(1)}, u32[]{:S(2)}, u32[]{:S(2)}) collective-permute-start(f32[512,256]{1,0:T(8,128)S(1)} %copy-done.5), channel_id=1, source_target_pairs={{1,2},{2,1},{5,6},{6,5},{9,10},{10,9},{13,14},{14,13},{17,18},{18,... | collective-permute-start | bytes 1572872 | tf_op jit(solution)/shard_map/ppermute | solution.py:39
  93.7 15.5 %collective-permute-start.21 = (f32[256,512]{1,0:T(8,128)S(1)}, f32[256,512]{1,0:T(8,128)S(1)}, u32[]{:S(2)}, u32[]{:S(2)}) collective-permute-start(f32[256,512]{1,0:T(8,128)S(1)} %broadcast_select_fusion.15), channel_id=1, source_target_pairs={{0,1},{3,2},{4,5},{7,6},{8,9},{11,10},{12,13},{15,14},{16,17},{19,... | collective-permute-start | bytes 1572872 | tf_op jit(solution)/shard_map/ppermute | solution.py:39
  97.8 21.0 %collective-permute-start.25 = (f32[512,256]{1,0:T(8,128)S(1)}, f32[512,256]{1,0:T(8,128)S(1)}, u32[]{:S(2)}, u32[]{:S(2)}) collective-permute-start(f32[512,256]{1,0:T(8,128)S(1)} %copy-done.9), channel_id=1, source_target_pairs={{1,2},{2,1},{5,6},{6,5},{9,10},{10,9},{13,14},{14,13},{17,18},{18,... | collective-permute-start | bytes 1572872 | tf_op jit(solution)/shard_map/ppermute | solution.py:39
  98.5 36.4 %collective-permute-start.30 = (f32[512,256]{1,0:T(8,128)S(1)}, f32[512,256]{1,0:T(8,128)S(1)}, u32[]{:S(2)}, u32[]{:S(2)}) collective-permute-start(f32[512,256]{1,0:T(8,128)S(1)} %get-tuple-element.59), channel_id=1, source_target_pairs={{1,2},{2,1},{5,6},{6,5},{9,10},{10,9},{13,14},{14,13},{17,18},{18,... | collective-permute-start | bytes 1572872 | tf_op jit(solution)/shard_map/ppermute | solution.py:39
  101.5 31.8 %collective-permute-start.27 = (f32[1024,256]{1,0:T(8,128)}, f32[1024,256]{1,0:T(8,128)S(1)}, u32[]{:S(2)}, u32[]{:S(2)}) collective-permute-start(f32[1024,256]{1,0:T(8,128)} %collective-permute-done.15), channel_id=1, source_target_pairs={{9,8},{10,11},{13,12},{14,15},{17,16},{18,19},{21,20},{22,23},{25,... | collective-permute-start | bytes 3145736 | tf_op jit(solution)/shard_map/ppermute | solution.py:39
  109.3 2.7 %collective-permute-start.23 = (f32[512,512]{1,0:T(8,128)S(1)}, f32[512,512]{1,0:T(8,128)S(1)}, u32[]{:S(2)}, u32[]{:S(2)}) collective-permute-start(f32[512,512]{1,0:T(8,128)S(1)} %constant_dynamic-update-slice_fusion.2), channel_id=1, source_target_pairs={{0,4},{1,5},{2,6},{3,7},{4,0},{5,1},{6,2},{7,3},{8,12},{9,13},{10,... | collective-permute-start | bytes 3145736 | tf_op jit(solution)/shard_map/ppermute | solution.py:43
  112.0 15.8 %collective-permute-start.24 = (f32[512,256]{1,0:T(8,128)S(1)}, f32[512,256]{1,0:T(8,128)S(1)}, u32[]{:S(2)}, u32[]{:S(2)}) collective-permute-start(f32[512,256]{1,0:T(8,128)S(1)} %get-tuple-element.59), channel_id=1, source_target_pairs={{0,1},{3,2},{4,5},{7,6},{8,9},{11,10},{12,13},{15,14},{16,17},{19,... | collective-permute-start | bytes 1572872 | tf_op jit(solution)/shard_map/ppermute | solution.py:39
  117.5 15.8 %collective-permute-start.28 = (f32[512,256]{1,0:T(8,128)}, f32[512,256]{1,0:T(8,128)S(1)}, u32[]{:S(2)}, u32[]{:S(2)}) collective-permute-start(f32[512,256]{1,0:T(8,128)} %collective-permute-done.19), channel_id=1, source_target_pairs={{1,0},{2,3},{5,4},{6,7}} | collective-permute-start | bytes 1572872 | tf_op jit(solution)/shard_map/ppermute | solution.py:39
  127.9 7.8 %collective-permute-start.31 = (f32[512,256]{1,0:T(8,128)S(1)}, f32[512,256]{1,0:T(8,128)S(1)}, u32[]{:S(2)}, u32[]{:S(2)}) collective-permute-start(f32[512,256]{1,0:T(8,128)S(1)} %collective-permute-done.24), channel_id=1, source_target_pairs={{1,2},{2,1},{5,6},{6,5},{9,10},{10,9},{13,14},{14,13},{17,18},{18,... | collective-permute-start | bytes 1572872 | tf_op jit(solution)/shard_map/ppermute | solution.py:39
  133.3 28.0 %collective-permute-start.29 = (f32[512,512]{1,0:T(8,128)S(1)}, f32[512,512]{1,0:T(8,128)S(1)}, u32[]{:S(2)}, u32[]{:S(2)}) collective-permute-start(f32[512,512]{1,0:T(8,128)S(1)} %fusion.27), channel_id=1, source_target_pairs={{1,0},{2,3},{5,4},{6,7},{9,8},{10,11},{13,12},{14,15},{17,16},{18,... | collective-permute-start | bytes 3145736 | tf_op jit(solution)/shard_map/ppermute | solution.py:39
  135.8 3.2 %copy-start.2 = (f32[2048,512]{1,0:T(8,128)S(1)}, f32[2048,512]{1,0:T(8,128)}, u32[]{:S(2)}) copy-start(f32[2048,512]{1,0:T(8,128)} %param.5) | copy-start | bytes 12582916
  137.6 44.1 %collective-permute-start.32 = (f32[512,512]{1,0:T(8,128)S(1)}, f32[512,512]{1,0:T(8,128)S(1)}, u32[]{:S(2)}, u32[]{:S(2)}) collective-permute-start(f32[512,512]{1,0:T(8,128)S(1)} %fusion.28), channel_id=1, source_target_pairs={{1,0},{2,3},{5,4},{6,7},{9,8},{10,11},{13,12},{14,15},{17,16},{18,... | collective-permute-start | bytes 3145736 | tf_op jit(solution)/shard_map/ppermute | solution.py:39
  183.7 2.5 %copy-start.1 = (f32[512,512]{1,0:T(8,128)S(1)}, f32[512,512]{1,0:T(8,128)}, u32[]{:S(2)}) copy-start(f32[512,512]{1,0:T(8,128)} %param.8) | copy-start | bytes 3145732

commit v3 on v0

v3 whole, which is shorter than its diff:
```python
import functools

import jax
import jax.numpy as jnp
from jax import lax
from jax.experimental import pallas as pl
from jax.experimental.pallas import tpu as pltpu
from jax.sharding import PartitionSpec as P

STAGE_FLOPS = 8*10**10


def product(left, right):
    return jnp.dot(left, right, precision=lax.Precision.HIGH, preferred_element_type=jnp.float32)


def broadcast(value, axis, source):
    kept = jnp.where(lax.axis_index(axis) == source, value, 0).astype(value.dtype)
    return lax.psum(kept, axis)


def general(test_kernel, first_panel, second_panel, first_inverse, second_inverse):
    block = first_inverse.shape[0]
    position = lax.axis_index("row")
    first_rows = broadcast(test_kernel[:block], "row", 0)
    first_solved = product(first_inverse, first_rows)
    partial_value = test_kernel - product(lax.all_gather(first_panel, "col", axis=1, tiled=True), first_solved)
    second_rows = broadcast(partial_value[:block], "row", 1)
    second_solved = product(second_inverse, second_rows)
    final = partial_value - product(lax.all_gather(second_panel, "col", axis=1, tiled=True), second_solved)
    leading_final = jnp.where(
        position == 0, first_solved, jnp.where(position == 1, second_solved, final[:block])
    )
    return final.at[:block].set(leading_final)


AXES = ("row", "col")
ROWS, COLS = 8, 4
END_MID = ((0, 1), (3, 2))
MID_MID = ((1, 2), (2, 1))
MID_END = ((1, 0), (2, 3))


def along_col(value, pairs, rows):
    return lax.ppermute(value, AXES, [(r * COLS + a, r * COLS + b) for r in rows for a, b in pairs])


def along_row(value, pairs, cols):
    return lax.ppermute(value, AXES, [(a * COLS + c, b * COLS + c) for a, b in pairs for c in cols])


ALL_COLS = (0, 1, 2, 3)
MID_COLS = (1, 2)
SWAP = tuple((r, r ^ 1) for r in range(ROWS))


def split(value):
    high = value.astype(jnp.bfloat16)
    return high, (value - high.astype(jnp.float32)).astype(jnp.bfloat16)


def three_pass(left, right):
    def one(a, b):
        return jnp.dot(a, b, preferred_element_type=jnp.float32)

    return one(left[0], right[0]) + (one(left[0], right[1]) + one(left[1], right[0]))


TILE = 256
VMEM_BYTES = 40 * 2**20
SMEM = pl.BlockSpec(memory_space=pltpu.SMEM)


def halves(place, held, other):
    a, b = held[...], other[...]
    return jnp.where(place[0] == 1, a, b), jnp.where(place[0] == 1, b, a)


def solved_tile(place, tops, inverses, corner):
    low, high = halves(place, *tops)
    half = low.shape[0] // 2
    first_top = jnp.concatenate([low[:half], high[:half]], axis=0)
    second_top = jnp.concatenate([low[half:], high[half:]], axis=0)
    slab = first_top.shape[0] // COLS

    def turned(solved):
        pieces = [solved[k * slab : (k + 1) * slab] for k in range(COLS)]
        return [jnp.where(place[1] == 1, pieces[k], pieces[COLS - 1 - k]) for k in range(COLS)]

    first_high, first_low, second_high, second_low = (ref[...] for ref in inverses)
    first = turned(three_pass((first_high, first_low), split(first_top)))
    value = second_top - three_pass(corner, split(jnp.concatenate(first, axis=0)))
    second = turned(three_pass((second_high, second_low), split(value)))
    return jnp.concatenate([p for pair in zip(first, second) for p in pair], axis=0)


def split_kernel(one, two, *outs):
    outs[0][...], outs[1][...] = split(one[...])
    outs[2][...], outs[3][...] = split(two[...])


def split_inverses(one, two):
    return pl.pallas_call(
        split_kernel, out_shape=[jax.ShapeDtypeStruct(one.shape, jnp.bfloat16)] * 4
    )(one, two)


def multiply_kernel(place, *refs):
    inverses, corner, out = refs[2:6], refs[6:8], refs[-1]
    solved = solved_tile(place, refs[:2], inverses, (corner[0][...], corner[1][...]))
    own, near_end, both = refs[8:11]
    panels = jnp.concatenate([near_end[...], own[...], both[...]], axis=1)
    out[...] = three_pass(split(panels), split(solved))


def own_kernel(place, *refs):
    held, other, inverses, (out, high, low) = refs[2], refs[3], refs[4:8], refs[8:]

    @pl.when(pl.program_id(0) == 0)
    def _():
        high[...], low[...] = split(jnp.concatenate(halves(place, held, other), axis=0))

    out[...] = solved_tile(place, refs[:2], inverses, (high[...], low[...]))


def fixed(value):
    return pl.BlockSpec(value.shape, lambda j: (0, 0))


def solve_and_multiply(place, held, other, inverses, corner, panels):
    width, rows = held.shape[1], panels[0].shape[0]
    tops = pl.BlockSpec((held.shape[0], TILE), lambda j: (0, j))
    fixed_ones = (*inverses, *corner, *panels)
    return pl.pallas_call(
        multiply_kernel,
        grid=(width // TILE,),
        out_shape=jax.ShapeDtypeStruct((rows, width), jnp.float32),
        in_specs=[SMEM, tops, tops] + [fixed(v) for v in fixed_ones],
        out_specs=pl.BlockSpec((rows, TILE), lambda j: (0, j)),
        compiler_params=pltpu.CompilerParams(vmem_limit_bytes=VMEM_BYTES),
        cost_estimate=pl.CostEstimate(flops=4 * 10**9, bytes_accessed=0, transcendentals=0),
    )(place, held, other, *fixed_ones)


def solve_own(place, held, other, inverses):
    block, width = inverses[0].shape[0], held.shape[1]
    tops = pl.BlockSpec((block, TILE), lambda j: (0, j))
    corners = pl.BlockSpec((block // 2, width), lambda j: (2, 0))
    corner = jax.ShapeDtypeStruct((block, block), jnp.bfloat16)
    return pl.pallas_call(
        own_kernel,
        grid=(width // TILE,),
        out_shape=[jax.ShapeDtypeStruct((2 * block, width), jnp.float32), corner, corner],
        in_specs=[SMEM, tops, tops, corners, corners] + [fixed(v) for v in inverses],
        out_specs=[pl.BlockSpec((2 * block, TILE), lambda j: (0, j)), fixed(corner), fixed(corner)],
        compiler_params=pltpu.CompilerParams(vmem_limit_bytes=VMEM_BYTES),
        cost_estimate=pl.CostEstimate(flops=3 * 10**9, bytes_accessed=0, transcendentals=0),
    )(place, held, other, held, other, *inverses)


def update_kernel(sizes, place, top, solved, *refs):
    index = pl.program_id(0)
    out, high, low = refs[-3:]
    groups, last = (refs[:6], refs[6:12]), refs[12:15]
    left, end = place[1] == 1, place[2] == 1

    @pl.when(index == 0)
    def _():
        high[...], low[...] = split(solved[...])

    def apply(panels):
        out[...] = top[...] - three_pass(split(panels), (high[...], low[...]))

    def raw_panels(own, swap, mid, far, c, cc):
        pairs = ((own, swap), (swap, own), (c, mid), (cc, far))
        return jnp.concatenate([jnp.where(end, a[...], b[...]) for a, b in pairs], axis=1)

    @pl.when(index < sizes[0])
    def _():
        apply(raw_panels(*groups[0]))
        slab = solved.shape[0] // (2 * COLS)
        for which in range(2):
            @pl.when(place[3 + which] == 1)
            def _():
                for k in range(TILE // slab):
                    here = index * (TILE // slab) + k
                    here = jnp.where(left, here, COLS - 1 - here)
                    start = pl.multiple_of((2 * here + which) * slab, slab)
                    out[k * slab : (k + 1) * slab] = solved[pl.ds(start, slab)]

    @pl.when((index >= sizes[0]) & (index < sizes[1]))
    def _():
        apply(raw_panels(*groups[1]))

    @pl.when(index >= sizes[1])
    def _():
        own, near_end, both = last
        apply(jnp.concatenate([near_end[...], own[...], both[...]], axis=1))


def update(place, top, solved, groups, last):
    rows, width = top.shape
    ends = [groups[0][0].shape[0] // TILE]
    ends.append(ends[0] + groups[1][0].shape[0] // TILE)
    tiles = rows // TILE

    def rows_of(value, first, past):
        return pl.BlockSpec((TILE, value.shape[1]), lambda i: (jnp.clip(i, first, past - 1) - first, 0))

    specs = [rows_of(v, 0, ends[0]) for v in groups[0]]
    specs += [rows_of(v, ends[0], ends[1]) for v in groups[1]]
    specs += [rows_of(v, ends[1], tiles) for v in last]
    tile = pl.BlockSpec((TILE, width), lambda i: (i, 0))
    return pl.pallas_call(
        functools.partial(update_kernel, ends),
        grid=(tiles,),
        out_shape=jax.ShapeDtypeStruct(top.shape, top.dtype),
        in_specs=[SMEM, tile, pl.BlockSpec(solved.shape, lambda i: (0, 0))] + specs,
        out_specs=tile,
        scratch_shapes=[pltpu.VMEM(solved.shape, jnp.bfloat16)] * 2,
        compiler_params=pltpu.CompilerParams(vmem_limit_bytes=VMEM_BYTES),
        cost_estimate=pl.CostEstimate(flops=7 * 10**9, bytes_accessed=0, transcendentals=0),
    )(place, top, solved, *groups[0], *groups[1], *last)


def finish_kernel(place, top, returned, kept, out):
    out[...] = jnp.where(place[2] == 1, top[...] - returned[...], kept[...])


def finish(place, top, returned, kept):
    rows, width = top.shape
    count = returned.shape[0] // TILE
    first = (rows - returned.shape[0]) // TILE
    tile = pl.BlockSpec((TILE, width), lambda i: (first + i, 0))
    return pl.pallas_call(
        finish_kernel,
        grid=(count,),
        out_shape=jax.ShapeDtypeStruct(top.shape, top.dtype),
        in_specs=[SMEM, tile, pl.BlockSpec((TILE, width), lambda i: (i, 0)), tile],
        out_specs=tile,
        input_output_aliases={3: 0},
        compiler_params=pltpu.CompilerParams(vmem_limit_bytes=VMEM_BYTES),
    )(place, top, returned, kept)


def nothing(*refs):
    pass


def stage(*values):
    anywhere = [pl.BlockSpec(memory_space=pl.ANY)] * len(values)
    return pl.pallas_call(
        nothing,
        out_shape=[jax.ShapeDtypeStruct(v.shape, v.dtype) for v in values],
        in_specs=anywhere,
        out_specs=anywhere,
        input_output_aliases={i: i for i in range(len(values))},
        cost_estimate=pl.CostEstimate(flops=STAGE_FLOPS, bytes_accessed=0, transcendentals=0),
    )(*values)


def four(test_kernel, first_panel, second_panel, first_inverse, second_inverse):
    block = first_inverse.shape[0]
    rows, width = test_kernel.shape
    raw = 3 * block
    half = block // 2
    row, col = lax.axis_index("row"), lax.axis_index("col")
    end = (col == 0) | (col == COLS - 1)
    left = col < COLS // 2
    even = row % 2 == 0
    every, most, one = range(ROWS), range(2, ROWS), (1,)
    both_ways = END_MID + MID_END
    tied = lax.optimization_barrier

    def both(low, high):
        return jnp.concatenate([first_panel[low:high], second_panel[low:high]], axis=1)

    def near(mine):
        got = along_row(mine, ((0, 2), (1, 5)), ALL_COLS)
        return jnp.where((row == 2) | (row == 5), got, mine)

    def far(mine):
        got = along_row(mine, ((2, 6), (5, 7), (0, 4), (1, 3)), ALL_COLS)
        return jnp.where((row == 3) | (row == 4) | (row >= 6), got, mine)

    def ordered(own, swap, mid, far, c, cc):
        return jnp.concatenate(
            [
                jnp.where(end, own, swap),
                jnp.where(end, swap, own),
                jnp.where(end, c, mid),
                jnp.where(end, cc, far),
            ],
            axis=1,
        )

    first_high, first_low, second_high, second_low = split_inverses(first_inverse, second_inverse)
    inverses = (first_high, first_low, second_high, second_low)

    corner = first_panel[:block]
    corner_swap = along_col(corner, both_ways, one)
    corner_mid = along_col(corner, MID_MID, one)
    corner_far = along_col(corner_swap, MID_MID, one)
    corner_c = along_col(corner_mid, MID_END, one)

    lead_own = both(0, block)
    lead_swap = along_col(lead_own, both_ways, most)
    lead_mid = along_col(lead_own, MID_MID, most)
    rest_own = both(block, raw)
    rest_swap = along_col(rest_own, both_ways, every)
    rest_mid = along_col(rest_own, MID_MID, every)

    top = test_kernel[:block]
    given = along_row(jnp.where(even, top[half:], top[:half]), ((0, 1), (1, 0)), ALL_COLS)
    mine = jnp.where(
        even,
        jnp.concatenate([top[:half], given], axis=0),
        jnp.concatenate([given, top[half:]], axis=0),
    )
    mine, lead_swap, lead_mid = tied((near(mine), lead_swap, lead_mid))
    lead_swap, lead_mid = stage(lead_swap, lead_mid)
    lead_c = along_col(lead_mid, MID_END, most)
    lead_far = along_col(lead_swap, MID_MID, most)
    mine = far(mine)

    mine, rest_swap, rest_mid = tied((mine, rest_swap, rest_mid))
    rest_swap, rest_mid = stage(rest_swap, rest_mid)
    rest_c = along_col(rest_mid, MID_END, every)
    rest_far = along_col(rest_swap, MID_MID, every)
    hop = along_col(mine, END_MID, every)
    corner_far, corner_c, mine = tied((corner_far, corner_c, mine))
    corner_cc = along_col(corner_far, MID_END, one)

    lead_c, lead_far, last_own, corner_c = tied((lead_c, lead_far, both(raw, rows), corner_c))
    lead_far, lead_c = stage(lead_far, lead_c)
    lead_cc = along_col(lead_far, MID_END, most)
    last_end = along_col(last_own, END_MID, every)
    corners = ordered(corner, corner_swap, corner_mid, corner_far, corner_c, corner_cc)
    corners, last_own = tied((corners, last_own))
    upper = along_row(corners[:half], ((1, 0),), ALL_COLS)
    corners = near(jnp.where(even, upper, corners[half:]))

    corners, rest_c, rest_far, hop = tied((corners, rest_c, rest_far, hop))
    rest_far, rest_c = stage(rest_far, rest_c)
    rest_cc = along_col(rest_far, MID_END, every)
    last_both = along_col(jnp.concatenate([last_own, last_end], axis=1), MID_MID, every)
    hop_other = along_row(hop, SWAP, ALL_COLS)
    corners = far(corners)
    held = jnp.concatenate([mine, corners], axis=0)
    other = along_row(held, SWAP, ALL_COLS)
    place = jnp.stack([even, left, end, row == 0, row == 1]).astype(jnp.int32)
    solved, corner_high, corner_low = solve_own(place, held, other, inverses)
    sent = solve_and_multiply(
        place, hop, hop_other, inverses, (corner_high, corner_low), (last_own, last_end, last_both)
    )
    returned = along_col(sent, MID_END, every)
    sent, lead_cc, rest_cc = tied((sent, lead_cc, rest_cc))
    groups = [
        (lead_own, lead_swap, lead_mid, lead_far, lead_c, lead_cc),
        (rest_own, rest_swap, rest_mid, rest_far, rest_c, rest_cc),
    ]
    out = update(place, test_kernel, solved, groups, (last_own, last_end, last_both))
    return finish(place, test_kernel, returned, out)


def solution(mesh):
    in_specs = (P("row", "col"), P("row", "col"), P("row", "col"), P(), P())
    out_specs = P("row", "col")
    body = four if dict(mesh.shape) == {"row": ROWS, "col": COLS} else general
    return jax.shard_map(body, mesh=mesh, in_specs=in_specs, out_specs=out_specs, check_vma=False)
```

time: 220 us -> 161 us (0.73)
  the two profiles are of different devices: /device:TPU:0 before, /device:TPU:4 now
where the time goes in v3:
time: 161 us; the launch traced here: 159 us
  waiting for transfers between devices  58 us (36%)
  starting transfers between devices  46.4 us (29%)
  Pallas kernels  34 us (21%)
  other arithmetic  12.5 us (8%)
  local copies, waits for them, and re-layouts  7.87 us (5%)
    ppermute x19, waiting for transfers between devices, along_col(): lax.ppermute(value, AXES, [(r * COLS + a, r * COLS + b) for r in rows for...  51.8 us
    ppermute x19, starting transfers between devices, along_col(): lax.ppermute(value, AXES, [(r * COLS + a, r * COLS + b) for r in rows for...  38.4 us
    pallas_call x1, Pallas kernels, update(): pl.pallas_call(functools.partial(update_kernel, ends), grid=(tiles,), out...  12.2 us
    pallas_call x1, Pallas kernels, solve_and_multiply(): pl.pallas_call(multiply_kernel, grid=(width // TILE,), out_shape=jax.Shap...  10.1 us
    ppermute x8, starting transfers between devices, along_row(): lax.ppermute(value, AXES, [(a * COLS + c, b * COLS + c) for a, b in pairs...  8.05 us
    pallas_call x1, Pallas kernels, solve_own(): pl.pallas_call(own_kernel, grid=(width // TILE,), out_shape=[jax.ShapeDty...  6.64 us
    ppermute x8, waiting for transfers between devices, along_row(): lax.ppermute(value, AXES, [(a * COLS + c, b * COLS + c) for a, b in pairs...  6.28 us
    unnamed x52, local copies, waits for them, and re-layouts  3.22 us
  transfers between devices with their start and end apart: 27, of which 7 were waited for; matrix products, arithmetic and copies ran while one was open for 10% of the time, Pallas kernels for 20%

profile of v3, /device:TPU:4, one launch (start us, length us, event | category | flops | bytes accessed | tf_op | source)
XLA Modules:
  0.0 159.5 jit_solution(13320760363906502925)
XLA Ops:
  0.0 1.4 fusion
  1.4 0.8 collective-permute-start.1
  2.5 1.7 %collective-permute-start.2 = (f32[512,512]{1,0:T(8,128)S(1)}, f32[512,512]{1,0:T(8,128)}, u32[]{:S(2)}, u32[]{:S(2)}) collective-permute-start(f32[512,512]{1,0:T(8,128)S(1)} %maximum_select_fusion), channel_id=1, source_target_pairs={{0,8},{1,9},{2,10},{3,11},{4,20},{5,21},{6,22},{7,23}} | collective-permute-start | bytes 3145736 | tf_op jit(solution)/shard_map/ppermute | solution.py:49
  5.0 3.5 %collective-permute-start.3 = (f32[512,256]{1,0:T(8,128)S(1)}, f32[512,256]{1,0:T(8,128)S(1)}, u32[]{:S(2)}, u32[]{:S(2)}) collective-permute-start(f32[512,256]{1,0:T(8,128)S(1)} %pad_maximum_fusion.4.refs_0_), channel_id=1, source_target_pairs={{8,9},{11,10},{9,8},{10,11},{12,13},{15,14},{13,12},{14,15},{16,17... | collective-permute-start | bytes 1572872 | tf_op jit(solution)/shard_map/ppermute | solution.py:45
  8.5 1.5 collective-permute-start.4
  10.0 1.4 collective-permute-start
  11.3 1.4 collective-permute-start.8
  12.7 1.9 %slice.43 = f32[1024,128]{1,0:T(8,128)} slice(f32[2048,128]{1,0:T(8,128)} %param.7), slice={[512:1536], [0:128]} | slice | bytes 1048576 | tf_op jit(solution)/shard_map/slice | solution.py:276
  14.6 0.9 slice.42
  15.5 1.4 pad_maximum_fusion.1.refs_6_
  16.9 3.7 %collective-permute-start.11 = (f32[1024,256]{1,0:T(8,128)S(1)}, f32[1024,256]{1,0:T(8,128)S(1)}, u32[]{:S(2)}, u32[]{:S(2)}) collective-permute-start(f32[1024,256]{1,0:T(8,128)S(1)} %pad_maximum_fusion.1.refs_6_), channel_id=1, source_target_pairs={{0,1},{3,2},{1,0},{2,3},{4,5},{7,6},{5,4},{6,7},{8,9},{11,10},{9,8... | collective-permute-start | bytes 3145736 | tf_op jit(solution)/shard_map/ppermute | solution.py:45
  20.6 1.2 broadcast_select_fusion.1
  21.8 1.6 %collective-permute-start.12 = (f32[1024,256]{1,0:T(8,128)S(1)}, f32[1024,256]{1,0:T(8,128)}, u32[]{:S(2)}, u32[]{:S(2)}) collective-permute-start(f32[1024,256]{1,0:T(8,128)S(1)} %pad_maximum_fusion.1.refs_6_), channel_id=1, source_target_pairs={{1,2},{2,1},{5,6},{6,5},{9,10},{10,9},{13,14},{14,13},{17,18},{18,... | collective-permute-start | bytes 3145736 | tf_op jit(solution)/shard_map/ppermute | solution.py:45
  23.4 1.3 collective-permute-start.10
  24.7 1.3 collective-permute-start.5
  26.0 0.8 collective-permute-start.6
  26.9 1.2 broadcast_select_fusion.8
  28.0 16.4 %collective-permute-done.11.refs_0_ = f32[1024,256]{1,0:T(8,128)S(1)} collective-permute-done((f32[1024,256]{1,0:T(8,128)S(1)}, f32[1024,256]{1,0:T(8,128)S(1)}, u32[]{:S(2)}, u32[]{:S(2)}) %collective-permute-start.11) | collective-permute-done | bytes 1048608 | tf_op jit(solution)/shard_map/ppermute | solution.py:45
  45.8 2.4 %broadcast_select_fusion = f32[512,512]{1,0:T(8,128)} fusion(f32[512,512]{1,0:T(8,128)} %collective-permute-done.10, f32[512,512]{1,0:T(8,128)} %broadcast_select_fusion.1, pred[]{:T(512)S(6)} %or.18), kind=kLoop, calls=%fused_computation.8 | loop fusion | flops 262144 | bytes 3145729 | tf_op jit(solution)/shard_map/jit(_where)/select_n | solution.py:284
  49.0 4.8 %collective-permute-start.18 = (f32[512,512]{1,0:T(8,128)}, f32[512,512]{1,0:T(8,128)}, u32[]{:S(2)}, u32[]{:S(2)}) collective-permute-start(f32[512,512]{1,0:T(8,128)} %broadcast_select_fusion), channel_id=1, source_target_pairs={{0,1},{3,2},{4,5},{7,6},{8,9},{11,10},{12,13},{15,14},{16,17},{19,... | collective-permute-start | bytes 3145736 | tf_op jit(solution)/shard_map/ppermute | solution.py:45
  53.8 1.9 %collective-permute-done.5.refs_1_ = f32[512,256]{1,0:T(8,128)S(1)} collective-permute-done((f32[512,256]{1,0:T(8,128)}, f32[512,256]{1,0:T(8,128)S(1)}, u32[]{:S(2)}, u32[]{:S(2)}) %collective-permute-start.5) | collective-permute-done | bytes 524320 | tf_op jit(solution)/shard_map/ppermute | solution.py:45
  55.9 1.0 slice.44
  57.6 1.3 collective-permute-start.16
  58.9 1.7 %collective-permute-start.17 = (f32[1024,256]{1,0:T(8,128)}, f32[1024,256]{1,0:T(8,128)}, u32[]{:S(2)}, u32[]{:S(2)}) collective-permute-start(f32[1024,256]{1,0:T(8,128)} %get-tuple-element.55.refs_7_), channel_id=1, source_target_pairs={{1,2},{2,1},{5,6},{6,5},{9,10},{10,9},{13,14},{14,13},{17,18},{18,... | collective-permute-start | bytes 3145736 | tf_op jit(solution)/shard_map/ppermute | solution.py:45
  60.6 0.9 slice_select_fusion
  62.3 2.9 %shard_map.57 = (bf16[512,512]{1,0:T(8,128)(2,1)}, bf16[512,512]{1,0:T(8,128)(2,1)}, bf16[512,512]{1,0:T(8,128)(2,1)}, bf16[512,512]{1,0:T(8,128)(2,1)}) custom-call(f32[512,512]{1,0:T(8,128)} %one.1, f32[512,512]{1,0:T(8,128)} %two.1), custom_call_target="tpu_custom_call" | custom-call | tf_op jit(solution)/shard_map/pallas_call | solution.py:103
  65.2 7.6 %collective-permute-start.22 = (f32[512,256]{1,0:T(8,128)S(1)}, f32[512,256]{1,0:T(8,128)S(1)}, u32[]{:S(2)}, u32[]{:S(2)}) collective-permute-start(f32[512,256]{1,0:T(8,128)S(1)} %pad_maximum_fusion.5.refs_8_.refs_12_), channel_id=1, source_target_pairs={{0,1},{3,2},{4,5},{7,6},{8,9},{11,10},{12,13},{15,14},{16,17},{19,... | collective-permute-start | bytes 1572872 | tf_op jit(solution)/shard_map/ppermute | solution.py:45
  72.9 1.1 broadcast_select_fusion.4
  74.0 11.6 %collective-permute-done.16.refs_1_ = f32[1024,256]{1,0:T(8,128)S(1)} collective-permute-done((f32[1024,256]{1,0:T(8,128)}, f32[1024,256]{1,0:T(8,128)S(1)}, u32[]{:S(2)}, u32[]{:S(2)}) %collective-permute-start.16) | collective-permute-done | bytes 1048608 | tf_op jit(solution)/shard_map/ppermute | solution.py:45
  85.6 1.3 collective-permute-start.20
  86.9 1.3 collective-permute-start.25
  88.2 1.1 pad_maximum_fusion.3
  89.3 1.6 %collective-permute-start.23 = (f32[512,512]{1,0:T(8,128)}, f32[512,512]{1,0:T(8,128)}, u32[]{:S(2)}, u32[]{:S(2)}) collective-permute-start(f32[512,512]{1,0:T(8,128)} %pad_maximum_fusion.3), channel_id=1, source_target_pairs={{1,2},{2,1},{5,6},{6,5},{9,10},{10,9},{13,14},{14,13},{17,18},{18,... | collective-permute-start | bytes 3145736 | tf_op jit(solution)/shard_map/ppermute | solution.py:45
  91.0 1.5 collective-permute-start.19
  92.5 4.2 %collective-permute-done.20 = f32[256,512]{1,0:T(8,128)S(1)} collective-permute-done((f32[256,512]{1,0:T(8,128)S(1)}, f32[256,512]{1,0:T(8,128)S(1)}, u32[]{:S(2)}, u32[]{:S(2)}) %collective-permute-start.20) | collective-permute-done | bytes 524320 | tf_op jit(solution)/shard_map/ppermute | solution.py:49
  96.8 1.4 pad_maximum_fusion.refs_0_.refs_2_
  98.3 1.4 collective-permute-start.26
  99.7 2.1 %collective-permute-done.21.refs_1_.refs_3_ = f32[768,512]{1,0:T(8,128)} collective-permute-done((f32[768,512]{1,0:T(8,128)S(1)}, f32[768,512]{1,0:T(8,128)}, u32[]{:S(2)}, u32[]{:S(2)}) %collective-permute-start.21) | collective-permute-done | bytes 1572896 | tf_op jit(solution)/shard_map/ppermute | solution.py:49
  101.8 1.0 copy-done.14
  102.8 1.0 copy-done.15
  103.9 1.0 copy-done.17
  104.9 6.6 %shard_map.58 = (f32[1024,512]{1,0:T(8,128)S(1)}, bf16[512,512]{1,0:T(8,128)(2,1)S(1)}, bf16[512,512]{1,0:T(8,128)(2,1)S(1)}) custom-call(s32[5]{0:T(128)S(1)} %convert_element_type.3.place, f32[768,512]{1,0:T(8,128)S(1)} %pad_maximum_fusion.refs_0_.refs_2_, f32[768,512]{1,0:T(8,128)} %collective-permute-done.21.refs_1_.refs_3_, ...), custom_call_target="tpu_custom_call" | custom-call | flops 3000000000 | tf_op jit(solution)/shard_map/pallas_call | solution.py:150
  111.7 10.1 %shard_map.59 = f32[512,512]{1,0:T(8,128)S(1)} custom-call(s32[5]{0:T(128)S(1)} %convert_element_type.3.place, f32[512,512]{1,0:T(8,128)} %collective-permute-done.18.refs_0_, f32[512,512]{1,0:T(8,128)} %collective-permute-done.19.refs_1_, bf16[512,512]{1,0:T(8,128)(2,1)S(1)} %copy-done.13, bf16[512,512]{1,0:T(8,128)(2,1)S(1)} %copy-done.14, ...), custom_call_target="tpu_custom_call" | custom-call | flops 4000000000 | tf_op jit(solution)/shard_map/pallas_call | solution.py:134
  121.7 1.5 collective-permute-start.24
  123.2 4.8 %collective-permute-done.26.refs_11_ = f32[1024,256]{1,0:T(8,128)S(1)} collective-permute-done((f32[1024,256]{1,0:T(8,128)}, f32[1024,256]{1,0:T(8,128)S(1)}, u32[]{:S(2)}, u32[]{:S(2)}) %collective-permute-start.26) | collective-permute-done | bytes 1048608 | tf_op jit(solution)/shard_map/ppermute | solution.py:45
  128.1 12.2 %shard_map.62.kept = f32[2048,512]{1,0:T(8,128)} custom-call(s32[5]{0:T(128)S(1)} %convert_element_type.3.place, f32[2048,512]{1,0:T(8,128)} %top.3, f32[1024,512]{1,0:T(8,128)S(1)} %get-tuple-element.66.solved, f32[512,256]{1,0:T(8,128)S(1)} %copy-done.4, f32[512,256]{1,0:T(8,128)S(1)} %copy-done.20, f32[512,256]{1,0:T(8,128)} %get-tuple-element.43.refs_2_, ...), custom_call_target="tpu_custom_call" | custom-call | flops 7000000000 | tf_op jit(solution)/shard_map/pallas_call | solution.py:214
  140.4 17.0 %collective-permute-done.24.returned = f32[512,512]{1,0:T(8,128)S(1)} collective-permute-done((f32[512,512]{1,0:T(8,128)S(1)}, f32[512,512]{1,0:T(8,128)S(1)}, u32[]{:S(2)}, u32[]{:S(2)}) %collective-permute-start.24) | collective-permute-done | bytes 1048608 | tf_op jit(solution)/shard_map/ppermute | solution.py:45
  157.4 2.1 %shard_map.63 = f32[2048,512]{1,0:T(8,128)} custom-call(s32[5]{0:T(128)S(1)} %convert_element_type.3.place, f32[2048,512]{1,0:T(8,128)S(1)} %copy-done, f32[512,512]{1,0:T(8,128)S(1)} %collective-permute-done.24.returned, f32[2048,512]{1,0:T(8,128)} %shard_map.62.kept), custom_call_target="tpu_custom_call", output_to_operand_aliasing={{}: (3, {})} | custom-call | tf_op jit(solution)/shard_map/pallas_call | solution.py:235
  (90 shorter events, 5.0 us)
Async XLA Ops:
  0.0 4.2 %copy-start.23 = (f32[2048,128]{1,0:T(8,128)S(1)}, f32[2048,128]{1,0:T(8,128)}, u32[]{:S(2)}) copy-start(f32[2048,128]{1,0:T(8,128)} %param.6) | copy-start | bytes 3145732
  1.4 2.8 %copy-start.24 = (f32[2048,128]{1,0:T(8,128)S(1)}, f32[2048,128]{1,0:T(8,128)}, u32[]{:S(2)}) copy-start(f32[2048,128]{1,0:T(8,128)} %param.7) | copy-start | bytes 3145732
  1.4 0.8 collective-permute-start.1
  2.5 13.0 %copy-start.21 = (f32[512,512]{1,0:T(8,128)}, f32[512,512]{1,0:T(8,128)S(1)}, u32[]{:S(2)}) copy-start(f32[512,512]{1,0:T(8,128)S(1)} %maximum_select_fusion) | copy-start | bytes 3145732
  2.5 14.4 %collective-permute-start.2 = (f32[512,512]{1,0:T(8,128)S(1)}, f32[512,512]{1,0:T(8,128)}, u32[]{:S(2)}, u32[]{:S(2)}) collective-permute-start(f32[512,512]{1,0:T(8,128)S(1)} %maximum_select_fusion), channel_id=1, source_target_pairs={{0,8},{1,9},{2,10},{3,11},{4,20},{5,21},{6,22},{7,23}} | collective-permute-start | bytes 3145736 | tf_op jit(solution)/shard_map/ppermute | solution.py:49
  5.0 11.9 %copy-start.3 = (f32[512,256]{1,0:T(8,128)}, f32[512,256]{1,0:T(8,128)S(1)}, u32[]{:S(2)}) copy-start(f32[512,256]{1,0:T(8,128)S(1)} %pad_maximum_fusion.4.refs_0_) | copy-start | bytes 1572868
  5.0 16.8 %collective-permute-start.3 = (f32[512,256]{1,0:T(8,128)S(1)}, f32[512,256]{1,0:T(8,128)S(1)}, u32[]{:S(2)}, u32[]{:S(2)}) collective-permute-start(f32[512,256]{1,0:T(8,128)S(1)} %pad_maximum_fusion.4.refs_0_), channel_id=1, source_target_pairs={{8,9},{11,10},{9,8},{10,11},{12,13},{15,14},{13,12},{14,15},{16,17... | collective-permute-start | bytes 1572872 | tf_op jit(solution)/shard_map/ppermute | solution.py:45
  8.5 14.9 %collective-permute-start.4 = (f32[512,256]{1,0:T(8,128)S(1)}, f32[512,256]{1,0:T(8,128)}, u32[]{:S(2)}, u32[]{:S(2)}) collective-permute-start(f32[512,256]{1,0:T(8,128)S(1)} %pad_maximum_fusion.4.refs_0_), channel_id=1, source_target_pairs={{9,10},{10,9},{13,14},{14,13},{17,18},{18,17},{21,22},{22,21},{25,... | collective-permute-start | bytes 1572872 | tf_op jit(solution)/shard_map/ppermute | solution.py:45
  10.0 14.7 %collective-permute-start = (f32[512,128]{1,0:T(8,128)S(1)}, f32[512,128]{1,0:T(8,128)}, u32[]{:S(2)}, u32[]{:S(2)}) collective-permute-start(f32[512,128]{1,0:T(8,128)S(1)} %slice.36), channel_id=1, source_target_pairs={{4,5},{7,6},{5,4},{6,7}} | collective-permute-start | bytes 786440 | tf_op jit(solution)/shard_map/ppermute | solution.py:45
  11.3 14.7 %collective-permute-start.8 = (f32[512,128]{1,0:T(8,128)S(1)}, f32[512,128]{1,0:T(8,128)}, u32[]{:S(2)}, u32[]{:S(2)}) collective-permute-start(f32[512,128]{1,0:T(8,128)S(1)} %slice.36), channel_id=1, source_target_pairs={{5,6},{6,5}} | collective-permute-start | bytes 786440 | tf_op jit(solution)/shard_map/ppermute | solution.py:45
  15.5 5.1 %copy-start.22 = (f32[512,512]{1,0:T(8,128)S(1)}, f32[512,512]{1,0:T(8,128)}, u32[]{:S(2)}) copy-start(f32[512,512]{1,0:T(8,128)} %copy-done.21) | copy-start | bytes 3145732
  16.9 7.8 %copy-start.1 = (f32[1024,256]{1,0:T(8,128)}, f32[1024,256]{1,0:T(8,128)S(1)}, u32[]{:S(2)}) copy-start(f32[1024,256]{1,0:T(8,128)S(1)} %pad_maximum_fusion.1.refs_6_) | copy-start | bytes 3145732
  16.9 27.6 %collective-permute-start.11 = (f32[1024,256]{1,0:T(8,128)S(1)}, f32[1024,256]{1,0:T(8,128)S(1)}, u32[]{:S(2)}, u32[]{:S(2)}) collective-permute-start(f32[1024,256]{1,0:T(8,128)S(1)} %pad_maximum_fusion.1.refs_6_), channel_id=1, source_target_pairs={{0,1},{3,2},{1,0},{2,3},{4,5},{7,6},{5,4},{6,7},{8,9},{11,10},{9,8... | collective-permute-start | bytes 3145736 | tf_op jit(solution)/shard_map/ppermute | solution.py:45
  21.8 2.9 %copy-start.19 = (f32[512,256]{1,0:T(8,128)}, f32[512,256]{1,0:T(8,128)S(1)}, u32[]{:S(2)}) copy-start(f32[512,256]{1,0:T(8,128)S(1)} %collective-permute-done.3.refs_0_) | copy-start | bytes 1572868
  21.8 26.5 %collective-permute-start.12 = (f32[1024,256]{1,0:T(8,128)S(1)}, f32[1024,256]{1,0:T(8,128)}, u32[]{:S(2)}, u32[]{:S(2)}) collective-permute-start(f32[1024,256]{1,0:T(8,128)S(1)} %pad_maximum_fusion.1.refs_6_), channel_id=1, source_target_pairs={{1,2},{2,1},{5,6},{6,5},{9,10},{10,9},{13,14},{14,13},{17,18},{18,... | collective-permute-start | bytes 3145736 | tf_op jit(solution)/shard_map/ppermute | solution.py:45
  23.4 21.8 %collective-permute-start.10 = (f32[512,512]{1,0:T(8,128)}, f32[512,512]{1,0:T(8,128)}, u32[]{:S(2)}, u32[]{:S(2)}) collective-permute-start(f32[512,512]{1,0:T(8,128)} %broadcast_select_fusion.1), channel_id=1, source_target_pairs={{8,24},{9,25},{10,26},{11,27},{20,28},{21,29},{22,30},{23,31},{0,1... | collective-permute-start | bytes 3145736 | tf_op jit(solution)/shard_map/ppermute | solution.py:49
  24.7 31.0 %collective-permute-start.5 = (f32[512,256]{1,0:T(8,128)}, f32[512,256]{1,0:T(8,128)S(1)}, u32[]{:S(2)}, u32[]{:S(2)}) collective-permute-start(f32[512,256]{1,0:T(8,128)} %get-tuple-element.43.refs_2_), channel_id=1, source_target_pairs={{9,8},{10,11},{13,12},{14,15},{17,16},{18,19},{21,20},{22,23},{25,... | collective-permute-start | bytes 1572872 | tf_op jit(solution)/shard_map/ppermute | solution.py:45
  26.0 22.9 %copy-start.25 = (f32[512,128]{1,0:T(8,128)S(1)}, f32[512,128]{1,0:T(8,128)}, u32[]{:S(2)}) copy-start(f32[512,128]{1,0:T(8,128)} %get-tuple-element.83) | copy-start | bytes 786436
  26.0 29.7 %collective-permute-start.6 = (f32[512,256]{1,0:T(8,128)}, f32[512,256]{1,0:T(8,128)S(1)}, u32[]{:S(2)}, u32[]{:S(2)}) collective-permute-start(f32[512,256]{1,0:T(8,128)} %get-tuple-element.44.refs_1_), channel_id=1, source_target_pairs={{9,10},{10,9},{13,14},{14,13},{17,18},{18,17},{21,22},{22,21},{25,... | collective-permute-start | bytes 1572872 | tf_op jit(solution)/shard_map/ppermute | solution.py:45
  44.5 4.5 %copy-start.5 = (f32[1024,256]{1,0:T(8,128)}, f32[1024,256]{1,0:T(8,128)S(1)}, u32[]{:S(2)}) copy-start(f32[1024,256]{1,0:T(8,128)S(1)} %collective-permute-done.11.refs_0_) | copy-start | bytes 3145732
  44.5 3.8 %collective-permute-start.7 = (f32[512,128]{1,0:T(8,128)}, f32[512,128]{1,0:T(8,128)S(1)}, u32[]{:S(2)}, u32[]{:S(2)}) collective-permute-start(f32[512,128]{1,0:T(8,128)} %collective-permute-done), channel_id=1, source_target_pairs={{5,6},{6,5}} | collective-permute-start | bytes 786440 | tf_op jit(solution)/shard_map/ppermute | solution.py:45
  45.2 3.1 %collective-permute-start.9 = (f32[512,128]{1,0:T(8,128)}, f32[512,128]{1,0:T(8,128)S(1)}, u32[]{:S(2)}, u32[]{:S(2)}) collective-permute-start(f32[512,128]{1,0:T(8,128)} %collective-permute-done.8), channel_id=1, source_target_pairs={{5,4},{6,7}} | collective-permute-start | bytes 786440 | tf_op jit(solution)/shard_map/ppermute | solution.py:45
  48.3 7.5 %collective-permute-start.13 = (f32[512,128]{1,0:T(8,128)S(1)}, f32[512,128]{1,0:T(8,128)S(1)}, u32[]{:S(2)}, u32[]{:S(2)}) collective-permute-start(f32[512,128]{1,0:T(8,128)S(1)} %collective-permute-done.7), channel_id=1, source_target_pairs={{5,4},{6,7}} | collective-permute-start | bytes 786440 | tf_op jit(solution)/shard_map/ppermute | solution.py:45
  49.0 36.6 %collective-permute-start.18 = (f32[512,512]{1,0:T(8,128)}, f32[512,512]{1,0:T(8,128)}, u32[]{:S(2)}, u32[]{:S(2)}) collective-permute-start(f32[512,512]{1,0:T(8,128)} %broadcast_select_fusion), channel_id=1, source_target_pairs={{0,1},{3,2},{4,5},{7,6},{8,9},{11,10},{12,13},{15,14},{16,17},{19,... | collective-permute-start | bytes 3145736 | tf_op jit(solution)/shard_map/ppermute | solution.py:45
  56.9 3.7 %collective-permute-start.14 = (f32[256,512]{1,0:T(8,128)}, f32[256,512]{1,0:T(8,128)S(1)}, u32[]{:S(2)}, u32[]{:S(2)}) collective-permute-start(f32[256,512]{1,0:T(8,128)} %slice.44), channel_id=1, source_target_pairs={{4,0},{5,1},{6,2},{7,3}} | collective-permute-start | bytes 1572872 | tf_op jit(solution)/shard_map/ppermute | solution.py:49
  57.6 28.0 %collective-permute-start.16 = (f32[1024,256]{1,0:T(8,128)}, f32[1024,256]{1,0:T(8,128)S(1)}, u32[]{:S(2)}, u32[]{:S(2)}) collective-permute-start(f32[1024,256]{1,0:T(8,128)} %get-tuple-element.54.refs_8_), channel_id=1, source_target_pairs={{1,0},{2,3},{5,4},{6,7},{9,8},{10,11},{13,12},{14,15},{17,16},{18,... | collective-permute-start | bytes 3145736 | tf_op jit(solution)/shard_map/ppermute | solution.py:45
  58.9 26.7 %collective-permute-start.17 = (f32[1024,256]{1,0:T(8,128)}, f32[1024,256]{1,0:T(8,128)}, u32[]{:S(2)}, u32[]{:S(2)}) collective-permute-start(f32[1024,256]{1,0:T(8,128)} %get-tuple-element.55.refs_7_), channel_id=1, source_target_pairs={{1,2},{2,1},{5,6},{6,5},{9,10},{10,9},{13,14},{14,13},{17,18},{18,... | collective-permute-start | bytes 3145736 | tf_op jit(solution)/shard_map/ppermute | solution.py:45
  61.5 11.4 %collective-permute-start.15 = (f32[256,512]{1,0:T(8,128)}, f32[256,512]{1,0:T(8,128)S(1)}, u32[]{:S(2)}, u32[]{:S(2)}) collective-permute-start(f32[256,512]{1,0:T(8,128)} %slice_select_fusion), channel_id=1, source_target_pairs={{0,8},{1,9},{2,10},{3,11},{4,20},{5,21},{6,22},{7,23}} | collective-permute-start | bytes 1572872 | tf_op jit(solution)/shard_map/ppermute | solution.py:49
  65.2 23.0 %collective-permute-start.22 = (f32[512,256]{1,0:T(8,128)S(1)}, f32[512,256]{1,0:T(8,128)S(1)}, u32[]{:S(2)}, u32[]{:S(2)}) collective-permute-start(f32[512,256]{1,0:T(8,128)S(1)} %pad_maximum_fusion.5.refs_8_.refs_12_), channel_id=1, source_target_pairs={{0,1},{3,2},{4,5},{7,6},{8,9},{11,10},{12,13},{15,14},{16,17},{19,... | collective-permute-start | bytes 1572872 | tf_op jit(solution)/shard_map/ppermute | solution.py:45
  85.6 1.3 copy-start.7
  85.6 11.1 %collective-permute-start.20 = (f32[256,512]{1,0:T(8,128)S(1)}, f32[256,512]{1,0:T(8,128)S(1)}, u32[]{:S(2)}, u32[]{:S(2)}) collective-permute-start(f32[256,512]{1,0:T(8,128)S(1)} %broadcast_select_fusion.4), channel_id=1, source_target_pairs={{8,24},{9,25},{10,26},{11,27},{20,28},{21,29},{22,30},{23,31},{0,1... | collective-permute-start | bytes 1572872 | tf_op jit(solution)/shard_map/ppermute | solution.py:49
  86.9 36.3 %collective-permute-start.25 = (f32[512,256]{1,0:T(8,128)}, f32[512,256]{1,0:T(8,128)}, u32[]{:S(2)}, u32[]{:S(2)}) collective-permute-start(f32[512,256]{1,0:T(8,128)} %get-tuple-element.69.refs_3_), channel_id=1, source_target_pairs={{9,8},{10,11},{13,12},{14,15},{17,16},{18,19},{21,20},{22,23},{25,... | collective-permute-start | bytes 1572872 | tf_op jit(solution)/shard_map/ppermute | solution.py:45
  89.3 22.2 %collective-permute-start.23 = (f32[512,512]{1,0:T(8,128)}, f32[512,512]{1,0:T(8,128)}, u32[]{:S(2)}, u32[]{:S(2)}) collective-permute-start(f32[512,512]{1,0:T(8,128)} %pad_maximum_fusion.3), channel_id=1, source_target_pairs={{1,2},{2,1},{5,6},{6,5},{9,10},{10,9},{13,14},{14,13},{17,18},{18,... | collective-permute-start | bytes 3145736 | tf_op jit(solution)/shard_map/ppermute | solution.py:45
  91.0 20.6 %collective-permute-start.19 = (f32[512,512]{1,0:T(8,128)}, f32[512,512]{1,0:T(8,128)}, u32[]{:S(2)}, u32[]{:S(2)}) collective-permute-start(f32[512,512]{1,0:T(8,128)} %collective-permute-done.18.refs_0_), channel_id=1, source_target_pairs={{0,4},{1,5},{2,6},{3,7},{4,0},{5,1},{6,2},{7,3},{8,12},{9,13},{10,... | collective-permute-start | bytes 3145736 | tf_op jit(solution)/shard_map/ppermute | solution.py:49
  98.2 3.6 %copy-start.13 = (bf16[512,512]{1,0:T(8,128)(2,1)S(1)}, bf16[512,512]{1,0:T(8,128)(2,1)}, u32[]{:S(2)}) copy-start(bf16[512,512]{1,0:T(8,128)(2,1)} %get-tuple-element.57.refs_4_.refs_2_) | copy-start | bytes 1572868
  98.2 3.6 %collective-permute-start.21 = (f32[768,512]{1,0:T(8,128)S(1)}, f32[768,512]{1,0:T(8,128)}, u32[]{:S(2)}, u32[]{:S(2)}) collective-permute-start(f32[768,512]{1,0:T(8,128)S(1)} %pad_maximum_fusion.refs_0_.refs_2_), channel_id=1, source_target_pairs={{0,4},{1,5},{2,6},{3,7},{4,0},{5,1},{6,2},{7,3},{8,12},{9,13},{10,... | collective-permute-start | bytes 4718600 | tf_op jit(solution)/shard_map/ppermute | solution.py:49
  98.3 29.8 %collective-permute-start.26 = (f32[1024,256]{1,0:T(8,128)}, f32[1024,256]{1,0:T(8,128)S(1)}, u32[]{:S(2)}, u32[]{:S(2)}) collective-permute-start(f32[1024,256]{1,0:T(8,128)} %get-tuple-element.73.refs_9_), channel_id=1, source_target_pairs={{1,0},{2,3},{5,4},{6,7},{9,8},{10,11},{13,12},{14,15},{17,16},{18,... | collective-permute-start | bytes 3145736 | tf_op jit(solution)/shard_map/ppermute | solution.py:45
  104.9 6.7 %copy-start.16 = (bf16[512,512]{1,0:T(8,128)(2,1)S(1)}, bf16[512,512]{1,0:T(8,128)(2,1)}, u32[]{:S(2)}) copy-start(bf16[512,512]{1,0:T(8,128)(2,1)} %get-tuple-element.59.refs_6_.refs_4_) | copy-start | bytes 1572868
  104.9 6.7 %copy-start.18 = (bf16[512,512]{1,0:T(8,128)(2,1)S(1)}, bf16[512,512]{1,0:T(8,128)(2,1)}, u32[]{:S(2)}) copy-start(bf16[512,512]{1,0:T(8,128)(2,1)} %get-tuple-element.60.refs_7_.refs_5_) | copy-start | bytes 1572868
  111.6 16.5 %copy-start.2 = (f32[1024,256]{1,0:T(8,128)S(1)}, f32[1024,256]{1,0:T(8,128)}, u32[]{:S(2)}) copy-start(f32[1024,256]{1,0:T(8,128)} %copy-done.1) | copy-start | bytes 3145732
  111.6 16.4 %copy-start.4 = (f32[512,256]{1,0:T(8,128)S(1)}, f32[512,256]{1,0:T(8,128)}, u32[]{:S(2)}) copy-start(f32[512,256]{1,0:T(8,128)} %copy-done.3) | copy-start | bytes 1572868
  111.6 16.4 %copy-start.6 = (f32[1024,256]{1,0:T(8,128)S(1)}, f32[1024,256]{1,0:T(8,128)}, u32[]{:S(2)}) copy-start(f32[1024,256]{1,0:T(8,128)} %get-tuple-element.55.refs_7_) | copy-start | bytes 3145732
  111.6 16.4 %copy-start.8 = (f32[1024,256]{1,0:T(8,128)S(1)}, f32[1024,256]{1,0:T(8,128)}, u32[]{:S(2)}) copy-start(f32[1024,256]{1,0:T(8,128)} %get-tuple-element.75.refs_10_) | copy-start | bytes 3145732
  111.6 16.4 %copy-start.10 = (f32[512,256]{1,0:T(8,128)S(1)}, f32[512,256]{1,0:T(8,128)}, u32[]{:S(2)}) copy-start(f32[512,256]{1,0:T(8,128)} %get-tuple-element.70.refs_4_) | copy-start | bytes 1572868
  111.6 16.4 %copy-start.12 = (f32[512,256]{1,0:T(8,128)S(1)}, f32[512,256]{1,0:T(8,128)}, u32[]{:S(2)}) copy-start(f32[512,256]{1,0:T(8,128)} %get-tuple-element.69.refs_3_) | copy-start | bytes 1572868
  111.6 16.4 %copy-start.20 = (f32[512,256]{1,0:T(8,128)S(1)}, f32[512,256]{1,0:T(8,128)}, u32[]{:S(2)}) copy-start(f32[512,256]{1,0:T(8,128)} %get-tuple-element.44.refs_1_) | copy-start | bytes 1572868
  121.7 35.6 %collective-permute-start.24 = (f32[512,512]{1,0:T(8,128)S(1)}, f32[512,512]{1,0:T(8,128)S(1)}, u32[]{:S(2)}, u32[]{:S(2)}) collective-permute-start(f32[512,512]{1,0:T(8,128)S(1)} %shard_map.59), channel_id=1, source_target_pairs={{1,0},{2,3},{5,4},{6,7},{9,8},{10,11},{13,12},{14,15},{17,16},{18,... | collective-permute-start | bytes 3145736 | tf_op jit(solution)/shard_map/ppermute | solution.py:45
  128.1 29.3 %copy-start = (f32[2048,512]{1,0:T(8,128)S(1)}, f32[2048,512]{1,0:T(8,128)}, u32[]{:S(2)}) copy-start(f32[2048,512]{1,0:T(8,128)} %top.3) | copy-start | bytes 12582916
  (5 other events, 5.5 us)

commit v4 on v0

v4 whole, which is shorter than its diff:
```python
import functools

import jax
import jax.numpy as jnp
from jax import lax
from jax.experimental import pallas as pl
from jax.experimental.pallas import tpu as pltpu
from jax.sharding import PartitionSpec as P

STAGE_FLOPS = 4 * 10**10
FILLERS = 3


def product(left, right):
    return jnp.dot(left, right, precision=lax.Precision.HIGH, preferred_element_type=jnp.float32)


def broadcast(value, axis, source):
    kept = jnp.where(lax.axis_index(axis) == source, value, 0).astype(value.dtype)
    return lax.psum(kept, axis)


def general(test_kernel, first_panel, second_panel, first_inverse, second_inverse):
    block = first_inverse.shape[0]
    position = lax.axis_index("row")
    first_rows = broadcast(test_kernel[:block], "row", 0)
    first_solved = product(first_inverse, first_rows)
    partial_value = test_kernel - product(lax.all_gather(first_panel, "col", axis=1, tiled=True), first_solved)
    second_rows = broadcast(partial_value[:block], "row", 1)
    second_solved = product(second_inverse, second_rows)
    final = partial_value - product(lax.all_gather(second_panel, "col", axis=1, tiled=True), second_solved)
    leading_final = jnp.where(
        position == 0, first_solved, jnp.where(position == 1, second_solved, final[:block])
    )
    return final.at[:block].set(leading_final)


AXES = ("row", "col")
ROWS, COLS = 8, 4
END_MID = ((0, 1), (3, 2))
MID_MID = ((1, 2), (2, 1))
MID_END = ((1, 0), (2, 3))


def pairs_of(pairs, rows):
    return [(r * COLS + a, r * COLS + b) for r in rows for a, b in pairs]


def along_col(value, pairs, rows):
    return lax.ppermute(value, AXES, pairs_of(pairs, rows))


def along_row(value, pairs, cols):
    return lax.ppermute(value, AXES, [(a * COLS + c, b * COLS + c) for a, b in pairs for c in cols])


ALL_COLS = (0, 1, 2, 3)
SWAP = tuple((r, r ^ 1) for r in range(ROWS))


def split(value):
    high = value.astype(jnp.bfloat16)
    return high, (value - high.astype(jnp.float32)).astype(jnp.bfloat16)


def three_pass(left, right):
    def one(a, b):
        return jnp.dot(a, b, preferred_element_type=jnp.float32)

    return one(left[0], right[0]) + (one(left[0], right[1]) + one(left[1], right[0]))


TILE = 256
VMEM_BYTES = 56 * 2**20
SMEM = pl.BlockSpec(memory_space=pltpu.SMEM)


def halves(place, held, other):
    a, b = held[...], other[...]
    return jnp.where(place[0] == 1, a, b), jnp.where(place[0] == 1, b, a)


def solved_tile(place, tops, corners, inverses):
    low, high = halves(place, *tops)
    half = low.shape[0] // 2
    first_top = jnp.concatenate([low[:half], high[:half]], axis=0)
    second_top = jnp.concatenate([low[half:], high[half:]], axis=0)
    corner = jnp.concatenate(halves(place, *corners), axis=0)
    slab = first_top.shape[0] // COLS

    def turned(solved):
        pieces = [solved[k * slab : (k + 1) * slab] for k in range(COLS)]
        return [jnp.where(place[1] == 1, pieces[k], pieces[COLS - 1 - k]) for k in range(COLS)]

    first_high, first_low, second_high, second_low = (ref[...] for ref in inverses)
    first = turned(three_pass((first_high, first_low), split(first_top)))
    value = second_top - three_pass(split(corner), split(jnp.concatenate(first, axis=0)))
    second = turned(three_pass((second_high, second_low), split(value)))
    return jnp.concatenate([p for pair in zip(first, second) for p in pair], axis=0)


def split_kernel(one, two, *outs):
    outs[0][...], outs[1][...] = split(one[...])
    outs[2][...], outs[3][...] = split(two[...])


def split_inverses(one, two):
    return pl.pallas_call(
        split_kernel, out_shape=[jax.ShapeDtypeStruct(one.shape, jnp.bfloat16)] * 4
    )(one, two)


def solve_kernel(place, *refs):
    refs[8][...], refs[9][...] = split(solved_tile(place, refs[:2], refs[2:4], refs[4:8]))


def solve(place, tops, corners, inverses):
    rows, width = 2 * inverses[0].shape[0], tops[0].shape[1]
    part = jax.ShapeDtypeStruct((rows, width), jnp.bfloat16)
    return pl.pallas_call(
        solve_kernel,
        out_shape=[part, part],
        in_specs=[SMEM] + [pl.BlockSpec(memory_space=pltpu.VMEM)] * 8,
        compiler_params=pltpu.CompilerParams(vmem_limit_bytes=VMEM_BYTES),
        cost_estimate=pl.CostEstimate(flops=3 * 10**9, bytes_accessed=0, transcendentals=0),
    )(place, *tops, *corners, *inverses)


def multiply_kernel(near_end, own, both, high, low, out):
    panels = jnp.concatenate([near_end[...], own[...], both[...]], axis=1)
    out[...] = three_pass(split(panels), (high[...], low[...]))


def multiply(panels, solved):
    rows, width = panels[0].shape[0], solved[0].shape[1]
    return pl.pallas_call(
        multiply_kernel,
        grid=(rows // TILE,),
        out_shape=jax.ShapeDtypeStruct((rows, width), jnp.float32),
        in_specs=[pl.BlockSpec((TILE, v.shape[1]), lambda i: (i, 0)) for v in panels]
        + [pl.BlockSpec(v.shape, lambda i: (0, 0)) for v in solved],
        out_specs=pl.BlockSpec((TILE, width), lambda i: (i, 0)),
        compiler_params=pltpu.CompilerParams(vmem_limit_bytes=VMEM_BYTES),
        cost_estimate=pl.CostEstimate(flops=2 * 10**9, bytes_accessed=0, transcendentals=0),
    )(*panels, *solved)


def update_raw_kernel(blocks, place, top, high, low, own, swap, mid, far, c, cc, *outs):
    left, end, out = place[1] == 1, place[2] == 1, outs[-1]
    pairs = ((own, swap), (swap, own), (c, mid), (cc, far))
    panels = jnp.concatenate([jnp.where(end, a[...], b[...]) for a, b in pairs], axis=1)
    out[...] = top[...] - three_pass(split(panels), (high[...], low[...]))
    if blocks:
        slab = high.shape[0] // (2 * COLS)
        for which in range(2):
            @pl.when(place[3 + which] == 1)
            def _():
                for k in range(TILE // slab):
                    here = pl.program_id(0) * (TILE // slab) + k
                    here = jnp.where(left, here, COLS - 1 - here)
                    rows = pl.ds(pl.multiple_of((2 * here + which) * slab, slab), slab)
                    value = high[rows].astype(jnp.float32) + low[rows].astype(jnp.float32)
                    out[k * slab : (k + 1) * slab] = value


def update_raw(place, top, solved, group, first, blocks, *out):
    tile = pl.BlockSpec((TILE, top.shape[1]), lambda i: (first // TILE + i, 0))
    part = pl.BlockSpec((TILE, group[0].shape[1]), lambda i: (i, 0))
    return pl.pallas_call(
        functools.partial(update_raw_kernel, blocks),
        grid=(group[0].shape[0] // TILE,),
        out_shape=jax.ShapeDtypeStruct(top.shape, top.dtype),
        in_specs=[SMEM, tile]
        + [pl.BlockSpec(v.shape, lambda i: (0, 0)) for v in solved]
        + [part] * 6
        + [pl.BlockSpec(memory_space=pl.ANY)] * len(out),
        out_specs=tile,
        input_output_aliases={10: 0} if out else {},
        compiler_params=pltpu.CompilerParams(vmem_limit_bytes=VMEM_BYTES),
        cost_estimate=pl.CostEstimate(flops=3 * 10**9, bytes_accessed=0, transcendentals=0),
    )(place, top, *solved, *group, *out)


def finish_kernel(place, top, returned, near_end, own, both, high, low, kept, out):
    @pl.when(place[2] == 1)
    def _():
        out[...] = top[...] - returned[...]

    @pl.when(place[2] == 0)
    def _():
        panels = jnp.concatenate([near_end[...], own[...], both[...]], axis=1)
        out[...] = top[...] - three_pass(split(panels), (high[...], low[...]))


def finish(place, top, returned, last, solved, out):
    width, count = top.shape[1], returned.shape[0] // TILE
    first = top.shape[0] // TILE - count
    tile = pl.BlockSpec((TILE, width), lambda i: (first + i, 0))
    parts = (returned, *last)
    return pl.pallas_call(
        finish_kernel,
        grid=(count,),
        out_shape=jax.ShapeDtypeStruct(top.shape, top.dtype),
        in_specs=[SMEM, tile]
        + [pl.BlockSpec((TILE, v.shape[1]), lambda i: (i, 0)) for v in parts]
        + [pl.BlockSpec(v.shape, lambda i: (0, 0)) for v in solved]
        + [pl.BlockSpec(memory_space=pl.ANY)],
        out_specs=tile,
        input_output_aliases={8: 0},
        compiler_params=pltpu.CompilerParams(vmem_limit_bytes=VMEM_BYTES),
        cost_estimate=pl.CostEstimate(flops=2 * 10**9, bytes_accessed=0, transcendentals=0),
    )(place, top, *parts, *solved, out)


def nothing(*refs):
    pass


def hand_on(*values):
    anywhere = [pl.BlockSpec(memory_space=pl.ANY)] * len(values)
    return pl.pallas_call(
        nothing,
        out_shape=[jax.ShapeDtypeStruct(v.shape, v.dtype) for v in values],
        in_specs=anywhere,
        out_specs=anywhere,
        input_output_aliases={i: i for i in range(len(values))},
        compiler_params=pltpu.CompilerParams(vmem_limit_bytes=VMEM_BYTES),
        cost_estimate=pl.CostEstimate(flops=STAGE_FLOPS, bytes_accessed=0, transcendentals=0),
    )(*values)


def stage(token, *values):
    for _ in range(FILLERS):
        [token] = hand_on(token)
    return hand_on(token, *values)


def four(test_kernel, first_panel, second_panel, first_inverse, second_inverse):
    block = first_inverse.shape[0]
    rows, width = test_kernel.shape
    raw, slab = 3 * block, first_panel.shape[1]
    half = block // 2
    row, col = lax.axis_index("row"), lax.axis_index("col")
    end = (col == 0) | (col == COLS - 1)
    left = col < COLS // 2
    even = row % 2 == 0
    every, most = range(ROWS), range(1, ROWS)
    both_ways = END_MID + MID_END
    tied = lax.optimization_barrier

    def both(low, high):
        return jnp.concatenate([first_panel[low:high], second_panel[low:high]], axis=1)

    def near(mine):
        return along_row(mine, ((0, 2), (1, 5)), ALL_COLS)

    def far(mine):
        return along_row(mine, ((2, 6), (5, 7), (0, 4), (1, 3)), ALL_COLS)

    def near_or(got, mine):
        return jnp.where((row == 2) | (row == 5), got, mine)

    def far_or(got, mine):
        return jnp.where((row == 3) | (row == 4) | (row >= 6), got, mine)

    def ordered(own, swap, mid, far, c, cc):
        pairs = ((own, swap), (swap, own), (c, mid), (cc, far))
        return jnp.concatenate([jnp.where(end, a, b) for a, b in pairs], axis=1)

    place = jnp.stack([even, left, end, row == 0, row == 1]).astype(jnp.int32)

    lead_own, rest_own, last_own = both(0, block), both(block, raw), both(raw, rows)
    top = test_kernel[:block]
    given = along_row(jnp.where(even, top[half:], top[:half]), ((0, 1), (1, 0)), ALL_COLS)
    token = jnp.zeros((8, 128), jnp.float32)
    given, lead_own, rest_own = tied((given, lead_own, rest_own))

    mine = jnp.where(
        even,
        jnp.concatenate([top[:half], given], axis=0),
        jnp.concatenate([given, top[half:]], axis=0),
    )
    got = near(mine)
    lead_swap = along_col(lead_own, both_ways, most)
    lead_mid = along_col(lead_own, MID_MID, most)
    rest_swap = along_col(rest_own, both_ways, every)
    rest_mid = along_col(rest_own, MID_MID, every)
    token, lead_swap, lead_mid, got, last_own = stage(token, lead_swap, lead_mid, got, last_own)

    mine = near_or(got, mine)
    got = far(mine)
    crossed = lax.ppermute(
        jnp.where(end, last_own, lead_mid), AXES, pairs_of(MID_END, most) + pairs_of(END_MID, every)
    )
    lead_far = along_col(lead_swap, MID_MID, most)
    token, rest_swap, rest_mid, got = stage(token, rest_swap, rest_mid, got)

    mine = far_or(got, mine)
    token, crossed, lead_far = stage(token, crossed, lead_far)

    lead_cc = along_col(lead_far, MID_END, most)
    hop = along_col(mine, END_MID, every)
    rest_c = along_col(rest_mid, MID_END, every)
    rest_far = along_col(rest_swap, MID_MID, every)
    inverses = split_inverses(*tied((first_inverse, second_inverse, token))[:2])
    token, lead_cc = stage(token, lead_cc)

    slabs = [v[:, :slab] for v in (lead_own, lead_swap, lead_mid, lead_far, crossed, lead_cc)]
    corner = ordered(*slabs)
    upper = along_row(corner[:half], ((1, 0),), ALL_COLS)
    corner = jnp.where(even, upper, corner[half:])
    got = near(corner)
    last_sent = jnp.concatenate(tied((last_own, crossed, token))[:2], axis=1)
    last_both = along_col(last_sent, MID_MID, every)
    token, rest_far, hop, got = stage(token, rest_far, hop, got)

    corner = near_or(got, corner)
    got = far(corner)
    rest_cc = along_col(rest_far, MID_END, every)
    hop_other = along_row(hop, SWAP, ALL_COLS)
    token, rest_c, got, hop_other = stage(token, rest_c, got, hop_other)

    corner = far_or(got, corner)
    corner = (corner, along_row(corner, SWAP, ALL_COLS))
    mine, token = tied((mine, token))
    other = along_row(mine, SWAP, ALL_COLS)
    solved_end = solve(place, (hop, hop_other), corner, inverses)
    token, last_both, *solved_end = stage(token, last_both, *solved_end)

    last = (crossed, last_own, last_both)
    sent = multiply(last, solved_end)
    returned = along_col(sent, MID_END, every)
    sent, mine, other = tied((sent, mine, other))

    solved = solve(place, (mine, other), corner, inverses)
    lead = (lead_own, lead_swap, lead_mid, lead_far, crossed, lead_cc)
    out = update_raw(place, test_kernel, solved, lead, 0, True)
    token, rest_cc, out = stage(token, rest_cc, out)

    rest = (rest_own, rest_swap, rest_mid, rest_far, rest_c, rest_cc)
    out = update_raw(place, test_kernel, solved, rest, block, False, out)
    return finish(place, test_kernel, returned, last, solved, out)


def solution(mesh):
    in_specs = (P("row", "col"), P("row", "col"), P("row", "col"), P(), P())
    out_specs = P("row", "col")
    body = four if dict(mesh.shape) == {"row": ROWS, "col": COLS} else general
    return jax.shard_map(body, mesh=mesh, in_specs=in_specs, out_specs=out_specs, check_vma=False)
```

time: 220 us -> 153 us (0.70)
  waiting for transfers between devices: 159 us -> 32.3 us
  starting transfers between devices: 0.31 us -> 52.1 us
  Pallas kernels: 0 us -> 38.6 us
  matrix products: 26.7 us -> 0 us
  between operations: 14.9 us -> 0.56 us
  other arithmetic: 6.08 us -> 13.6 us
    psum x2 -> x0, waiting for transfers between devices: 113 us -> none  [broadcast(): return lax.psum(kept, axis)]
    ppermute x0 -> x22, starting transfers between devices: none -> 52.1 us  [the longest x12 23.8 us: along_col(): return lax.ppermute(value, AXES, pairs_of(pairs, rows))]
    all_gather x2 -> x0, waiting for transfers between devices: 45.2 us -> none  [the longest x1 22.7 us: per_device(): lax.all_gather(first_panel, 'col', axis=1, tiled=True)]
    pallas_call x0 -> x39, Pallas kernels: none -> 38.6 us  [the longest x2 13.7 us: solve(): pl.pallas_call(solve_kernel, out_shape=[part, part], in_specs=[SMEM] + [p...]
    ppermute x0 -> x22, waiting for transfers between devices: none -> 32.3 us  [the longest x9 15.4 us: along_row(): lax.ppermute(value, AXES, [(a * COLS + c, b * COLS + c) for a, b in pairs...]
    dot_general x4 -> x0, matrix products: 26.7 us -> none  [product(): jnp.dot(left, right, precision=lax.Precision.HIGHEST, preferred_element_t...]
    unnamed x5 -> x64, local copies, waits for them, and re-layouts: 7.44 us -> 13.4 us
    scatter x1 -> x0, local copies, waits for them, and re-layouts: 5.34 us -> none  [per_device(): return final.at[:block].set(leading_final)]
  transfers between devices with their start and end apart: 4 -> 22, of which waited for: 4 -> 8; matrix products, arithmetic and copies ran while one was open for 3% -> 9% of each run, Pallas kernels for 0% -> 23%
where the time goes in v4:
time: 153 us; the launch traced here: 152 us
  starting transfers between devices  52.1 us (34%)
  Pallas kernels  38.6 us (25%)
  waiting for transfers between devices  32.3 us (21%)
  local copies, waits for them, and re-layouts  14.9 us (10%)
  other arithmetic  13.6 us (9%)
    ppermute x12, starting transfers between devices, along_col(): return lax.ppermute(value, AXES, pairs_of(pairs, rows))  23.8 us
    ppermute x9, starting transfers between devices, along_row(): lax.ppermute(value, AXES, [(a * COLS + c, b * COLS + c) for a, b in pairs...  21.3 us
    ppermute x9, waiting for transfers between devices, along_row(): lax.ppermute(value, AXES, [(a * COLS + c, b * COLS + c) for a, b in pairs...  15.4 us
    pallas_call x2, Pallas kernels, solve(): pl.pallas_call(solve_kernel, out_shape=[part, part], in_specs=[SMEM] + [p...  13.7 us
    pallas_call x2, Pallas kernels, update_raw(): pl.pallas_call(functools.partial(update_raw_kernel, blocks), grid=(group[...  13.5 us
    unnamed x64, local copies, waits for them, and re-layouts  13.4 us
    ppermute x12, waiting for transfers between devices, along_col(): return lax.ppermute(value, AXES, pairs_of(pairs, rows))  9.08 us
    ppermute x1, waiting for transfers between devices, four(): lax.ppermute(jnp.where(end, last_own, lead_mid), AXES, pairs_of(MID_END,...  7.82 us
  transfers between devices with their start and end apart: 22, of which 8 were waited for; matrix products, arithmetic and copies ran while one was open for 9% of the time, Pallas kernels for 23%

profile of v4, /device:TPU:0, one launch (start us, length us, event | category | flops | bytes accessed | tf_op | source)
XLA Modules:
  0.0 152.1 jit_solution(4682906849923755742)
XLA Ops:
  0.0 1.4 fusion
  1.4 2.4 %collective-permute-start = (f32[256,512]{1,0:T(8,128)S(1)}, f32[256,512]{1,0:T(8,128)S(1)}, u32[]{:S(2)}, u32[]{:S(2)}) collective-permute-start(f32[256,512]{1,0:T(8,128)S(1)} %get-tuple-element.100), channel_id=1, source_target_pairs={{0,4},{1,5},{2,6},{3,7},{4,0},{5,1},{6,2},{7,3}} | collective-permute-start | bytes 1572872 | tf_op jit(solution)/shard_map/ppermute | solution.py:54
  4.4 1.2 copy-done.15
  6.8 1.2 pad_maximum_fusion.own
  8.0 1.4 collective-permute-start.1
  10.3 5.3 %collective-permute-start.3 = (f32[512,512]{1,0:T(8,128)S(1)}, f32[512,512]{1,0:T(8,128)S(1)}, u32[]{:S(2)}, u32[]{:S(2)}) collective-permute-start(f32[512,512]{1,0:T(8,128)S(1)} %maximum_select_fusion), channel_id=1, source_target_pairs={{0,8},{1,9},{2,10},{3,11},{4,20},{5,21},{6,22},{7,23}} | collective-permute-start | bytes 3145736 | tf_op jit(solution)/shard_map/ppermute | solution.py:54
  16.3 1.8 %pad_maximum_fusion.4.refs_4_ = f32[512,256]{1,0:T(8,128)} fusion(f32[512,128]{1,0:T(8,128)} %get-tuple-element.109, f32[512,128]{1,0:T(8,128)S(1)} %get-tuple-element.104), kind=kLoop, calls=%fused_computation.6 | loop fusion | flops 131072 | bytes 1048576 | tf_op jit(solution)/shard_map/concatenate | solution.py:252
  18.1 4.4 %collective-permute-start.4 = (f32[1024,256]{1,0:T(8,128)}, f32[1024,256]{1,0:T(8,128)}, u32[]{:S(2)}, u32[]{:S(2)}) collective-permute-start(f32[1024,256]{1,0:T(8,128)} %pad_maximum_fusion.own), channel_id=1, source_target_pairs={{0,1},{3,2},{1,0},{2,3},{4,5},{7,6},{5,4},{6,7},{8,9},{11,10},{9,8... | collective-permute-start | bytes 3145736 | tf_op jit(solution)/shard_map/ppermute | solution.py:50
  22.4 1.7 %collective-permute-start.5 = (f32[1024,256]{1,0:T(8,128)}, f32[1024,256]{1,0:T(8,128)}, u32[]{:S(2)}, u32[]{:S(2)}) collective-permute-start(f32[1024,256]{1,0:T(8,128)} %pad_maximum_fusion.own), channel_id=1, source_target_pairs={{1,2},{2,1},{5,6},{6,5},{9,10},{10,9},{13,14},{14,13},{17,18},{18,... | collective-permute-start | bytes 3145736 | tf_op jit(solution)/shard_map/ppermute | solution.py:50
  24.1 3.7 %collective-permute-done.3.refs_3_ = f32[512,512]{1,0:T(8,128)S(1)} collective-permute-done((f32[512,512]{1,0:T(8,128)S(1)}, f32[512,512]{1,0:T(8,128)S(1)}, u32[]{:S(2)}, u32[]{:S(2)}) %collective-permute-start.3) | collective-permute-done | bytes 1048608 | tf_op jit(solution)/shard_map/ppermute | solution.py:54
  27.8 1.0 copy-done.19
  28.8 1.2 copy-done.3
  30.6 1.6 %collective-permute-start.6 = (f32[512,512]{1,0:T(8,128)S(1)}, f32[512,512]{1,0:T(8,128)S(1)}, u32[]{:S(2)}, u32[]{:S(2)}) collective-permute-start(f32[512,512]{1,0:T(8,128)S(1)} %broadcast_select_fusion.1), channel_id=1, source_target_pairs={{8,24},{9,25},{10,26},{11,27},{20,28},{21,29},{22,30},{23,31},{0,1... | collective-permute-start | bytes 3145736 | tf_op jit(solution)/shard_map/ppermute | solution.py:54
  33.1 7.1 %collective-permute-start.7 = (f32[512,256]{1,0:T(8,128)}, f32[512,256]{1,0:T(8,128)}, u32[]{:S(2)}, u32[]{:S(2)}) collective-permute-start(f32[512,256]{1,0:T(8,128)} %broadcast_select_fusion.4), channel_id=1, source_target_pairs={{5,4},{6,7},{9,8},{10,11},{13,12},{14,15},{17,16},{18,19},{21,20},... | collective-permute-start | bytes 1572872 | tf_op jit(solution)/shard_map/ppermute | solution.py:292
  40.2 1.5 collective-permute-start.8
  41.6 1.8 %slice_select_fusion.4 = (f32[512,128]{1,0:T(8,128)}, f32[512,128]{1,0:T(8,128)}) fusion(f32[512,256]{1,0:T(8,128)} %get-tuple-element.60.swap, f32[512,256]{1,0:T(8,128)S(1)} %copy-done.7, pred[]{:T(512)} %or.15), kind=kLoop, calls=%fused_computation.16 | loop fusion | flops 131072 | bytes 1048577 | tf_op jit(solution)/shard_map/jit(_where)/select_n | solution.py:268
  43.4 3.4 %collective-permute-done.4.refs_1_ = f32[1024,256]{1,0:T(8,128)} collective-permute-done((f32[1024,256]{1,0:T(8,128)}, f32[1024,256]{1,0:T(8,128)}, u32[]{:S(2)}, u32[]{:S(2)}) %collective-permute-start.4) | collective-permute-done | bytes 1048608 | tf_op jit(solution)/shard_map/ppermute | solution.py:50
  46.8 1.0 copy-done.21
  47.8 7.8 %collective-permute-done.7.refs_1_ = f32[512,256]{1,0:T(8,128)} collective-permute-done((f32[512,256]{1,0:T(8,128)}, f32[512,256]{1,0:T(8,128)}, u32[]{:S(2)}, u32[]{:S(2)}) %collective-permute-start.7) | collective-permute-done | bytes 524320 | tf_op jit(solution)/shard_map/ppermute | solution.py:292
  56.5 1.7 %collective-permute-start.10 = (f32[1024,256]{1,0:T(8,128)}, f32[1024,256]{1,0:T(8,128)}, u32[]{:S(2)}, u32[]{:S(2)}) collective-permute-start(f32[1024,256]{1,0:T(8,128)} %get-tuple-element.66.swap), channel_id=1, source_target_pairs={{1,2},{2,1},{5,6},{6,5},{9,10},{10,9},{13,14},{14,13},{17,18},{18,... | collective-permute-start | bytes 3145736 | tf_op jit(solution)/shard_map/ppermute | solution.py:50
  58.2 1.2 broadcast_select_fusion.refs_0_
  59.4 5.9 %collective-permute-start.11 = (f32[512,512]{1,0:T(8,128)}, f32[512,512]{1,0:T(8,128)}, u32[]{:S(2)}, u32[]{:S(2)}) collective-permute-start(f32[512,512]{1,0:T(8,128)} %broadcast_select_fusion.refs_0_), channel_id=1, source_target_pairs={{0,1},{3,2},{4,5},{7,6},{8,9},{11,10},{12,13},{15,14},{16,17},{19,... | collective-permute-start | bytes 3145736 | tf_op jit(solution)/shard_map/ppermute | solution.py:50
  65.3 1.3 collective-permute-start.14
  66.6 3.0 %shard_map.82 = (bf16[512,512]{1,0:T(8,128)(2,1)}, bf16[512,512]{1,0:T(8,128)(2,1)}, bf16[512,512]{1,0:T(8,128)(2,1)}, bf16[512,512]{1,0:T(8,128)(2,1)}) custom-call(f32[512,512]{1,0:T(8,128)} %one, f32[512,512]{1,0:T(8,128)} %two), custom_call_target="tpu_custom_call" | custom-call | tf_op jit(solution)/shard_map/pallas_call | solution.py:108
  69.6 1.0 slice_select_fusion.2
  71.4 1.0 copy-done.18
  72.4 1.0 slice_select_fusion.1
  73.5 1.3 collective-permute-start.12
  74.8 2.5 %collective-permute-done.12 = f32[256,512]{1,0:T(8,128)S(1)} collective-permute-done((f32[256,512]{1,0:T(8,128)S(1)}, f32[256,512]{1,0:T(8,128)S(1)}, u32[]{:S(2)}, u32[]{:S(2)}) %collective-permute-start.12) | collective-permute-done | bytes 524320 | tf_op jit(solution)/shard_map/ppermute | solution.py:54
  77.4 6.2 %collective-permute-start.13 = (f32[256,512]{1,0:T(8,128)S(1)}, f32[256,512]{1,0:T(8,128)S(1)}, u32[]{:S(2)}, u32[]{:S(2)}) collective-permute-start(f32[256,512]{1,0:T(8,128)S(1)} %slice_select_fusion), channel_id=1, source_target_pairs={{0,8},{1,9},{2,10},{3,11},{4,20},{5,21},{6,22},{7,23}} | collective-permute-start | bytes 1572872 | tf_op jit(solution)/shard_map/ppermute | solution.py:54
  83.6 2.2 %pad_maximum_fusion.2 = f32[512,512]{1,0:T(8,128)} fusion(f32[512,256]{1,0:T(8,128)} %get-tuple-element.75.near_end.c, f32[512,256]{1,0:T(8,128)S(1)} %copy-done.1), kind=kLoop, calls=%fused_computation.3 | loop fusion | flops 262144 | bytes 2097152 | tf_op jit(solution)/shard_map/concatenate | solution.py:313
  85.8 1.6 %collective-permute-start.17 = (f32[512,512]{1,0:T(8,128)}, f32[512,512]{1,0:T(8,128)}, u32[]{:S(2)}, u32[]{:S(2)}) collective-permute-start(f32[512,512]{1,0:T(8,128)} %pad_maximum_fusion.2), channel_id=1, source_target_pairs={{1,2},{2,1},{5,6},{6,5},{9,10},{10,9},{13,14},{14,13},{17,18},{18,... | collective-permute-start | bytes 3145736 | tf_op jit(solution)/shard_map/ppermute | solution.py:50
  87.4 2.8 %collective-permute-done.13.refs_3_ = f32[256,512]{1,0:T(8,128)S(1)} collective-permute-done((f32[256,512]{1,0:T(8,128)S(1)}, f32[256,512]{1,0:T(8,128)S(1)}, u32[]{:S(2)}, u32[]{:S(2)}) %collective-permute-start.13) | collective-permute-done | bytes 524320 | tf_op jit(solution)/shard_map/ppermute | solution.py:54
  91.0 1.0 copy-done.14
  92.3 4.5 %collective-permute-start.15 = (f32[256,512]{1,0:T(8,128)S(1)}, f32[256,512]{1,0:T(8,128)S(1)}, u32[]{:S(2)}, u32[]{:S(2)}) collective-permute-start(f32[256,512]{1,0:T(8,128)S(1)} %broadcast_select_fusion.3), channel_id=1, source_target_pairs={{8,24},{9,25},{10,26},{11,27},{20,28},{21,29},{22,30},{23,31},{0,1... | collective-permute-start | bytes 1572872 | tf_op jit(solution)/shard_map/ppermute | solution.py:54
  96.9 1.3 collective-permute-start.21
  98.2 5.2 %collective-permute-done.15.refs_2_ = f32[256,512]{1,0:T(8,128)S(1)} collective-permute-done((f32[256,512]{1,0:T(8,128)S(1)}, f32[256,512]{1,0:T(8,128)S(1)}, u32[]{:S(2)}, u32[]{:S(2)}) %collective-permute-start.15) | collective-permute-done | bytes 524320 | tf_op jit(solution)/shard_map/ppermute | solution.py:54
  104.3 1.0 copy-done.30
  105.3 1.0 copy-done.12
  107.3 1.2 collective-permute-done.18.refs_3_
  109.4 6.8 %shard_map.83 = (bf16[1024,512]{1,0:T(8,128)(2,1)}, bf16[1024,512]{1,0:T(8,128)(2,1)}) custom-call(s32[5]{0:T(128)} %convert_element_type.3.place, f32[512,512]{1,0:T(8,128)} %get-tuple-element.71.refs_0_, f32[512,512]{1,0:T(8,128)} %get-tuple-element.76.refs_1_, f32[256,512]{1,0:T(8,128)} %copy-done.25, f32[256,512]{1,0:T(8,128)} %copy-done.31, ...), custom_call_target="tpu_custom_call" | custom-call | flops 3000000000 | tf_op jit(solution)/shard_map/pallas_call | solution.py:120
  116.2 4.7 %shard_map.85 = f32[512,512]{1,0:T(8,128)} custom-call(f32[512,256]{1,0:T(8,128)} %get-tuple-element.75.near_end.c, f32[512,256]{1,0:T(8,128)} %get-tuple-element.74.own, f32[512,512]{1,0:T(8,128)} %get-tuple-element.86.both, bf16[1024,512]{1,0:T(8,128)(2,1)} %get-tuple-element.87.high, bf16[1024,512]{1,0:T(8,128)(2,1)} %get-tuple-element.88.low), custom_call_target="tpu_custom_call" | custom-call | flops 2000000000 | tf_op jit(solution)/shard_map/pallas_call | solution.py:136
  120.9 1.5 collective-permute-start.19
  122.5 6.8 %shard_map.86 = (bf16[1024,512]{1,0:T(8,128)(2,1)}, bf16[1024,512]{1,0:T(8,128)(2,1)}) custom-call(s32[5]{0:T(128)} %convert_element_type.3.place, f32[512,512]{1,0:T(8,128)} %broadcast_select_fusion.refs_0_, f32[512,512]{1,0:T(8,128)} %collective-permute-done.20.refs_1_, f32[256,512]{1,0:T(8,128)} %copy-done.25, f32[256,512]{1,0:T(8,128)} %copy-done.31, ...), custom_call_target="tpu_custom_call" | custom-call | flops 3000000000 | tf_op jit(solution)/shard_map/pallas_call | solution.py:120
  129.3 5.4 %shard_map.90.refs_2_ = f32[2048,512]{1,0:T(8,128)} custom-call(s32[5]{0:T(128)} %convert_element_type.3.place, f32[2048,512]{1,0:T(8,128)} %top.5, bf16[1024,512]{1,0:T(8,128)(2,1)} %get-tuple-element.92.high, bf16[1024,512]{1,0:T(8,128)(2,1)} %get-tuple-element.93.low, f32[512,256]{1,0:T(8,128)} %copy-done.6, f32[512,256]{1,0:T(8,128)} %get-tuple-element.60.swap, ...), custom_call_target="tpu_custom_call" | custom-call | flops 3000000000 | tf_op jit(solution)/shard_map/pallas_call | solution.py:169
  134.7 8.1 %shard_map.92.kept = f32[2048,512]{1,0:T(8,128)} custom-call(s32[5]{0:T(128)} %convert_element_type.3.place, f32[2048,512]{1,0:T(8,128)} %top.5, bf16[1024,512]{1,0:T(8,128)(2,1)} %get-tuple-element.92.high, bf16[1024,512]{1,0:T(8,128)(2,1)} %get-tuple-element.93.low, f32[1024,256]{1,0:T(8,128)} %pad_maximum_fusion.own, ...), custom_call_target="tpu_custom_call", output_to_operand_aliasing={{}: (10, {})} | custom-call | flops 3000000000 | tf_op jit(solution)/shard_map/pallas_call | solution.py:169
  142.8 5.6 %collective-permute-done.19.returned = f32[512,512]{1,0:T(8,128)} collective-permute-done((f32[512,512]{1,0:T(8,128)}, f32[512,512]{1,0:T(8,128)}, u32[]{:S(2)}, u32[]{:S(2)}) %collective-permute-start.19) | collective-permute-done | bytes 1048608 | tf_op jit(solution)/shard_map/ppermute | solution.py:50
  148.5 3.7 %shard_map.93 = f32[2048,512]{1,0:T(8,128)} custom-call(s32[5]{0:T(128)} %convert_element_type.3.place, f32[2048,512]{1,0:T(8,128)} %top.5, f32[512,512]{1,0:T(8,128)} %collective-permute-done.19.returned, f32[512,256]{1,0:T(8,128)} %get-tuple-element.75.near_end.c, f32[512,256]{1,0:T(8,128)} %get-tuple-element.74.own, ...), custom_call_target="tpu_custom_call", output_to_operand_aliasing={{}: (8, {})} | custom-call | flops 2000000000 | tf_op jit(solution)/shard_map/pallas_call | solution.py:200
  (124 shorter events, 10.3 us)
Async XLA Ops:
  1.4 6.6 %collective-permute-start = (f32[256,512]{1,0:T(8,128)S(1)}, f32[256,512]{1,0:T(8,128)S(1)}, u32[]{:S(2)}, u32[]{:S(2)}) collective-permute-start(f32[256,512]{1,0:T(8,128)S(1)} %get-tuple-element.100), channel_id=1, source_target_pairs={{0,4},{1,5},{2,6},{3,7},{4,0},{5,1},{6,2},{7,3}} | collective-permute-start | bytes 1572872 | tf_op jit(solution)/shard_map/ppermute | solution.py:54
  4.4 1.2 copy-start.15
  4.4 1.5 %copy-start.16 = (f32[2048,128]{1,0:T(8,128)S(1)}, f32[2048,128]{1,0:T(8,128)}, u32[]{:S(2)}) copy-start(f32[2048,128]{1,0:T(8,128)} %param.6) | copy-start | bytes 3145732
  4.4 2.3 %slice-start = ((f32[2048,128]{1,0:T(8,128)}), f32[1024,128]{1,0:T(8,128)S(1)}, s32[]{:S(2)}) async-start(f32[2048,128]{1,0:T(8,128)} %param.7), calls=%async_computation | async-start | bytes 1048576 | tf_op jit(solution)/shard_map/slice | solution.py:252
  4.4 2.4 %slice-start.1 = ((f32[2048,128]{1,0:T(8,128)}), f32[1024,128]{1,0:T(8,128)S(1)}, s32[]{:S(2)}) async-start(f32[2048,128]{1,0:T(8,128)} %param.6), calls=%async_computation.1 | async-start | bytes 1048576 | tf_op jit(solution)/shard_map/slice | solution.py:252
  6.7 8.8 %copy-start.6 = (f32[512,256]{1,0:T(8,128)}, f32[512,256]{1,0:T(8,128)S(1)}, u32[]{:S(2)}) copy-start(f32[512,256]{1,0:T(8,128)S(1)} %pad_maximum_fusion.3.own) | copy-start | bytes 1572868
  8.0 16.2 %collective-permute-start.1 = (f32[512,256]{1,0:T(8,128)S(1)}, f32[512,256]{1,0:T(8,128)}, u32[]{:S(2)}, u32[]{:S(2)}) collective-permute-start(f32[512,256]{1,0:T(8,128)S(1)} %pad_maximum_fusion.3.own), channel_id=1, source_target_pairs={{4,5},{7,6},{5,4},{6,7},{8,9},{11,10},{9,8},{10,11},{12,13},{15,14... | collective-permute-start | bytes 1572872 | tf_op jit(solution)/shard_map/ppermute | solution.py:50
  9.4 14.7 %collective-permute-start.2 = (f32[512,256]{1,0:T(8,128)S(1)}, f32[512,256]{1,0:T(8,128)S(1)}, u32[]{:S(2)}, u32[]{:S(2)}) collective-permute-start(f32[512,256]{1,0:T(8,128)S(1)} %pad_maximum_fusion.3.own), channel_id=1, source_target_pairs={{5,6},{6,5},{9,10},{10,9},{13,14},{14,13},{17,18},{18,17},{21,22},... | collective-permute-start | bytes 1572872 | tf_op jit(solution)/shard_map/ppermute | solution.py:50
  10.3 5.3 %copy-start.2 = (f32[512,512]{1,0:T(8,128)}, f32[512,512]{1,0:T(8,128)S(1)}, u32[]{:S(2)}) copy-start(f32[512,512]{1,0:T(8,128)S(1)} %maximum_select_fusion) | copy-start | bytes 3145732
  10.3 17.5 %collective-permute-start.3 = (f32[512,512]{1,0:T(8,128)S(1)}, f32[512,512]{1,0:T(8,128)S(1)}, u32[]{:S(2)}, u32[]{:S(2)}) collective-permute-start(f32[512,512]{1,0:T(8,128)S(1)} %maximum_select_fusion), channel_id=1, source_target_pairs={{0,8},{1,9},{2,10},{3,11},{4,20},{5,21},{6,22},{7,23}} | collective-permute-start | bytes 3145736 | tf_op jit(solution)/shard_map/ppermute | solution.py:54
  18.1 28.8 %collective-permute-start.4 = (f32[1024,256]{1,0:T(8,128)}, f32[1024,256]{1,0:T(8,128)}, u32[]{:S(2)}, u32[]{:S(2)}) collective-permute-start(f32[1024,256]{1,0:T(8,128)} %pad_maximum_fusion.own), channel_id=1, source_target_pairs={{0,1},{3,2},{1,0},{2,3},{4,5},{7,6},{5,4},{6,7},{8,9},{11,10},{9,8... | collective-permute-start | bytes 3145736 | tf_op jit(solution)/shard_map/ppermute | solution.py:50
  22.4 24.4 %collective-permute-start.5 = (f32[1024,256]{1,0:T(8,128)}, f32[1024,256]{1,0:T(8,128)}, u32[]{:S(2)}, u32[]{:S(2)}) collective-permute-start(f32[1024,256]{1,0:T(8,128)} %pad_maximum_fusion.own), channel_id=1, source_target_pairs={{1,2},{2,1},{5,6},{6,5},{9,10},{10,9},{13,14},{14,13},{17,18},{18,... | collective-permute-start | bytes 3145736 | tf_op jit(solution)/shard_map/ppermute | solution.py:50
  24.1 3.7 %copy-start.8 = (f32[512,256]{1,0:T(8,128)}, f32[512,256]{1,0:T(8,128)S(1)}, u32[]{:S(2)}) copy-start(f32[512,256]{1,0:T(8,128)S(1)} %collective-permute-done.2.refs_2_) | copy-start | bytes 1572868
  28.8 1.2 copy-start.3
  28.8 1.5 %copy-start.20 = (f32[512,512]{1,0:T(8,128)S(1)}, f32[512,512]{1,0:T(8,128)}, u32[]{:S(2)}) copy-start(f32[512,512]{1,0:T(8,128)} %get-tuple-element.56) | copy-start | bytes 3145732
  30.5 1.7 %copy-start.4 = (f32[512,512]{1,0:T(8,128)}, f32[512,512]{1,0:T(8,128)S(1)}, u32[]{:S(2)}) copy-start(f32[512,512]{1,0:T(8,128)S(1)} %broadcast_select_fusion.1) | copy-start | bytes 3145732
  30.6 1.7 %copy-start = (f32[512,256]{1,0:T(8,128)S(1)}, f32[512,256]{1,0:T(8,128)}, u32[]{:S(2)}) copy-start(f32[512,256]{1,0:T(8,128)} %get-tuple-element.74.own) | copy-start | bytes 1572868
  30.6 1.7 %copy-start.9 = (f32[512,256]{1,0:T(8,128)S(1)}, f32[512,256]{1,0:T(8,128)}, u32[]{:S(2)}) copy-start(f32[512,256]{1,0:T(8,128)} %get-tuple-element.59.mid) | copy-start | bytes 1572868
  30.6 11.1 %copy-start.7 = (f32[512,256]{1,0:T(8,128)S(1)}, f32[512,256]{1,0:T(8,128)}, u32[]{:S(2)}) copy-start(f32[512,256]{1,0:T(8,128)} %copy-done.6) | copy-start | bytes 1572868
  30.6 16.3 %collective-permute-start.6 = (f32[512,512]{1,0:T(8,128)S(1)}, f32[512,512]{1,0:T(8,128)S(1)}, u32[]{:S(2)}, u32[]{:S(2)}) collective-permute-start(f32[512,512]{1,0:T(8,128)S(1)} %broadcast_select_fusion.1), channel_id=1, source_target_pairs={{8,24},{9,25},{10,26},{11,27},{20,28},{21,29},{22,30},{23,31},{0,1... | collective-permute-start | bytes 3145736 | tf_op jit(solution)/shard_map/ppermute | solution.py:54
  33.1 22.5 %collective-permute-start.7 = (f32[512,256]{1,0:T(8,128)}, f32[512,256]{1,0:T(8,128)}, u32[]{:S(2)}, u32[]{:S(2)}) collective-permute-start(f32[512,256]{1,0:T(8,128)} %broadcast_select_fusion.4), channel_id=1, source_target_pairs={{5,4},{6,7},{9,8},{10,11},{13,12},{14,15},{17,16},{18,19},{21,20},... | collective-permute-start | bytes 1572872 | tf_op jit(solution)/shard_map/ppermute | solution.py:292
  40.2 15.5 %collective-permute-start.8 = (f32[512,256]{1,0:T(8,128)}, f32[512,256]{1,0:T(8,128)}, u32[]{:S(2)}, u32[]{:S(2)}) collective-permute-start(f32[512,256]{1,0:T(8,128)} %get-tuple-element.60.swap), channel_id=1, source_target_pairs={{5,6},{6,5},{9,10},{10,9},{13,14},{14,13},{17,18},{18,17},{21,22},... | collective-permute-start | bytes 1572872 | tf_op jit(solution)/shard_map/ppermute | solution.py:50
  55.6 2.6 %copy-start.5 = (f32[512,512]{1,0:T(8,128)S(1)}, f32[512,512]{1,0:T(8,128)}, u32[]{:S(2)}) copy-start(f32[512,512]{1,0:T(8,128)} %copy-done.4) | copy-start | bytes 3145732
  55.6 2.6 %copy-start.22 = (f32[512,512]{1,0:T(8,128)S(1)}, f32[512,512]{1,0:T(8,128)}, u32[]{:S(2)}) copy-start(f32[512,512]{1,0:T(8,128)} %get-tuple-element.62) | copy-start | bytes 3145732
  55.7 13.9 %copy-start.10 = (f32[512,256]{1,0:T(8,128)S(1)}, f32[512,256]{1,0:T(8,128)}, u32[]{:S(2)}) copy-start(f32[512,256]{1,0:T(8,128)} %get-tuple-element.59.mid) | copy-start | bytes 1572868
  55.7 14.9 %collective-permute-start.9 = (f32[512,256]{1,0:T(8,128)}, f32[512,256]{1,0:T(8,128)S(1)}, u32[]{:S(2)}, u32[]{:S(2)}) collective-permute-start(f32[512,256]{1,0:T(8,128)} %get-tuple-element.64.far), channel_id=1, source_target_pairs={{5,4},{6,7},{9,8},{10,11},{13,12},{14,15},{17,16},{18,19},{21,20},... | collective-permute-start | bytes 1572872 | tf_op jit(solution)/shard_map/ppermute | solution.py:50
  56.5 30.9 %collective-permute-start.10 = (f32[1024,256]{1,0:T(8,128)}, f32[1024,256]{1,0:T(8,128)}, u32[]{:S(2)}, u32[]{:S(2)}) collective-permute-start(f32[1024,256]{1,0:T(8,128)} %get-tuple-element.66.swap), channel_id=1, source_target_pairs={{1,2},{2,1},{5,6},{6,5},{9,10},{10,9},{13,14},{14,13},{17,18},{18,... | collective-permute-start | bytes 3145736 | tf_op jit(solution)/shard_map/ppermute | solution.py:50
  59.4 28.0 %collective-permute-start.11 = (f32[512,512]{1,0:T(8,128)}, f32[512,512]{1,0:T(8,128)}, u32[]{:S(2)}, u32[]{:S(2)}) collective-permute-start(f32[512,512]{1,0:T(8,128)} %broadcast_select_fusion.refs_0_), channel_id=1, source_target_pairs={{0,1},{3,2},{4,5},{7,6},{8,9},{11,10},{12,13},{15,14},{16,17},{19,... | collective-permute-start | bytes 3145736 | tf_op jit(solution)/shard_map/ppermute | solution.py:50
  65.3 32.9 %collective-permute-start.14 = (f32[1024,256]{1,0:T(8,128)}, f32[1024,256]{1,0:T(8,128)}, u32[]{:S(2)}, u32[]{:S(2)}) collective-permute-start(f32[1024,256]{1,0:T(8,128)} %get-tuple-element.69.mid), channel_id=1, source_target_pairs={{1,0},{2,3},{5,4},{6,7},{9,8},{10,11},{13,12},{14,15},{17,16},{18,... | collective-permute-start | bytes 3145736 | tf_op jit(solution)/shard_map/ppermute | solution.py:50
  71.3 1.0 copy-start.18
  71.4 2.0 %copy-start.23 = (f32[512,128]{1,0:T(8,128)S(1)}, f32[512,128]{1,0:T(8,128)}, u32[]{:S(2)}) copy-start(f32[512,128]{1,0:T(8,128)} %get-tuple-element.102) | copy-start | bytes 786436
  71.4 2.0 %copy-start.24 = (f32[512,128]{1,0:T(8,128)S(1)}, f32[512,128]{1,0:T(8,128)}, u32[]{:S(2)}) copy-start(f32[512,128]{1,0:T(8,128)} %get-tuple-element.103) | copy-start | bytes 786436
  73.5 3.8 %collective-permute-start.12 = (f32[256,512]{1,0:T(8,128)S(1)}, f32[256,512]{1,0:T(8,128)S(1)}, u32[]{:S(2)}, u32[]{:S(2)}) collective-permute-start(f32[256,512]{1,0:T(8,128)S(1)} %slice.69), channel_id=1, source_target_pairs={{4,0},{5,1},{6,2},{7,3}} | collective-permute-start | bytes 1572872 | tf_op jit(solution)/shard_map/ppermute | solution.py:54
  77.4 6.2 %copy-start.13 = (f32[256,512]{1,0:T(8,128)}, f32[256,512]{1,0:T(8,128)S(1)}, u32[]{:S(2)}) copy-start(f32[256,512]{1,0:T(8,128)S(1)} %slice_select_fusion) | copy-start | bytes 1572868
  77.4 6.2 %copy-start.1 = (f32[512,256]{1,0:T(8,128)S(1)}, f32[512,256]{1,0:T(8,128)}, u32[]{:S(2)}) copy-start(f32[512,256]{1,0:T(8,128)} %get-tuple-element.74.own) | copy-start | bytes 1572868
  77.4 12.8 %collective-permute-start.13 = (f32[256,512]{1,0:T(8,128)S(1)}, f32[256,512]{1,0:T(8,128)S(1)}, u32[]{:S(2)}, u32[]{:S(2)}) collective-permute-start(f32[256,512]{1,0:T(8,128)S(1)} %slice_select_fusion), channel_id=1, source_target_pairs={{0,8},{1,9},{2,10},{3,11},{4,20},{5,21},{6,22},{7,23}} | collective-permute-start | bytes 1572872 | tf_op jit(solution)/shard_map/ppermute | solution.py:54
  85.8 30.4 %collective-permute-start.17 = (f32[512,512]{1,0:T(8,128)}, f32[512,512]{1,0:T(8,128)}, u32[]{:S(2)}, u32[]{:S(2)}) collective-permute-start(f32[512,512]{1,0:T(8,128)} %pad_maximum_fusion.2), channel_id=1, source_target_pairs={{1,2},{2,1},{5,6},{6,5},{9,10},{10,9},{13,14},{14,13},{17,18},{18,... | collective-permute-start | bytes 3145736 | tf_op jit(solution)/shard_map/ppermute | solution.py:50
  91.0 1.0 copy-start.14
  91.0 1.2 copy-start.29
  92.3 4.6 %copy-start.11 = (f32[256,512]{1,0:T(8,128)}, f32[256,512]{1,0:T(8,128)S(1)}, u32[]{:S(2)}) copy-start(f32[256,512]{1,0:T(8,128)S(1)} %broadcast_select_fusion.3) | copy-start | bytes 1572868
  92.3 11.1 %collective-permute-start.15 = (f32[256,512]{1,0:T(8,128)S(1)}, f32[256,512]{1,0:T(8,128)S(1)}, u32[]{:S(2)}, u32[]{:S(2)}) collective-permute-start(f32[256,512]{1,0:T(8,128)S(1)} %broadcast_select_fusion.3), channel_id=1, source_target_pairs={{8,24},{9,25},{10,26},{11,27},{20,28},{21,29},{22,30},{23,31},{0,1... | collective-permute-start | bytes 1572872 | tf_op jit(solution)/shard_map/ppermute | solution.py:54
  96.8 6.7 %collective-permute-start.16 = (f32[512,512]{1,0:T(8,128)}, f32[512,512]{1,0:T(8,128)S(1)}, u32[]{:S(2)}, u32[]{:S(2)}) collective-permute-start(f32[512,512]{1,0:T(8,128)} %get-tuple-element.71.refs_0_), channel_id=1, source_target_pairs={{0,4},{1,5},{2,6},{3,7},{4,0},{5,1},{6,2},{7,3},{8,12},{9,13},{10,... | collective-permute-start | bytes 3145736 | tf_op jit(solution)/shard_map/ppermute | solution.py:54
  96.9 37.8 %collective-permute-start.21 = (f32[1024,256]{1,0:T(8,128)}, f32[1024,256]{1,0:T(8,128)}, u32[]{:S(2)}, u32[]{:S(2)}) collective-permute-start(f32[1024,256]{1,0:T(8,128)} %get-tuple-element.94.far), channel_id=1, source_target_pairs={{1,0},{2,3},{5,4},{6,7},{9,8},{10,11},{13,12},{14,15},{17,16},{18,... | collective-permute-start | bytes 3145736 | tf_op jit(solution)/shard_map/ppermute | solution.py:50
  105.3 1.0 copy-start.12
  105.3 1.2 copy-start.27
  106.6 2.0 %collective-permute-start.18 = (f32[256,512]{1,0:T(8,128)S(1)}, f32[256,512]{1,0:T(8,128)S(1)}, u32[]{:S(2)}, u32[]{:S(2)}) collective-permute-start(f32[256,512]{1,0:T(8,128)S(1)} %broadcast_select_fusion.2.refs_2_), channel_id=1, source_target_pairs={{0,4},{1,5},{2,6},{3,7},{4,0},{5,1},{6,2},{7,3},{8,12},{9,13},{10,... | collective-permute-start | bytes 1572872 | tf_op jit(solution)/shard_map/ppermute | solution.py:54
  107.3 15.1 %collective-permute-start.20 = (f32[512,512]{1,0:T(8,128)}, f32[512,512]{1,0:T(8,128)}, u32[]{:S(2)}, u32[]{:S(2)}) collective-permute-start(f32[512,512]{1,0:T(8,128)} %broadcast_select_fusion.refs_0_), channel_id=1, source_target_pairs={{0,4},{1,5},{2,6},{3,7},{4,0},{5,1},{6,2},{7,3},{8,12},{9,13},{10,... | collective-permute-start | bytes 3145736 | tf_op jit(solution)/shard_map/ppermute | solution.py:54
  120.9 27.5 %collective-permute-start.19 = (f32[512,512]{1,0:T(8,128)}, f32[512,512]{1,0:T(8,128)}, u32[]{:S(2)}, u32[]{:S(2)}) collective-permute-start(f32[512,512]{1,0:T(8,128)} %shard_map.85), channel_id=1, source_target_pairs={{1,0},{2,3},{5,4},{6,7},{9,8},{10,11},{13,12},{14,15},{17,16},{18,... | collective-permute-start | bytes 3145736 | tf_op jit(solution)/shard_map/ppermute | solution.py:50
  (8 other events, 7.0 us)

commit v5 on v4

--- a/solution.py
+++ b/solution.py
@@ -8,7 +8,8 @@
 from jax.sharding import PartitionSpec as P
 
 STAGE_FLOPS = 4 * 10**10
-FILLERS = 3
+FILLERS = 2
+STAGE_BYTES = 2**20
 
 
 def product(left, right):
@@ -71,7 +72,7 @@
 
 
 TILE = 256
-VMEM_BYTES = 56 * 2**20
+VMEM_BYTES = 32 * 2**20
 SMEM = pl.BlockSpec(memory_space=pltpu.SMEM)
 
 
@@ -106,7 +107,9 @@
 
 def split_inverses(one, two):
     return pl.pallas_call(
-        split_kernel, out_shape=[jax.ShapeDtypeStruct(one.shape, jnp.bfloat16)] * 4
+        split_kernel,
+        out_shape=[jax.ShapeDtypeStruct(one.shape, jnp.bfloat16)] * 4,
+        compiler_params=pltpu.CompilerParams(vmem_limit_bytes=16 * 2**20),
     )(one, two)
 
 
@@ -181,35 +184,42 @@
     )(place, top, *solved, *group, *out)
 
 
-def finish_kernel(place, top, returned, near_end, own, both, high, low, kept, out):
-    @pl.when(place[2] == 1)
-    def _():
-        out[...] = top[...] - returned[...]
-
+def update_last_kernel(place, top, near_end, own, both, high, low, kept, out):
     @pl.when(place[2] == 0)
     def _():
         panels = jnp.concatenate([near_end[...], own[...], both[...]], axis=1)
         out[...] = top[...] - three_pass(split(panels), (high[...], low[...]))
 
 
-def finish(place, top, returned, last, solved, out):
-    width, count = top.shape[1], returned.shape[0] // TILE
+def finish_kernel(place, top, returned, kept, out):
+    out[...] = jnp.where(place[2] == 1, top[...] - returned[...], kept[...])
+
+
+def last_call(body, place, top, parts, fixed, out, block_of_out, flops):
+    width, count = top.shape[1], parts[0].shape[0] // TILE
     first = top.shape[0] // TILE - count
     tile = pl.BlockSpec((TILE, width), lambda i: (first + i, 0))
-    parts = (returned, *last)
-    return pl.pallas_call(
-        finish_kernel,
+    return pl.pallas_call(
+        body,
         grid=(count,),
         out_shape=jax.ShapeDtypeStruct(top.shape, top.dtype),
         in_specs=[SMEM, tile]
         + [pl.BlockSpec((TILE, v.shape[1]), lambda i: (i, 0)) for v in parts]
-        + [pl.BlockSpec(v.shape, lambda i: (0, 0)) for v in solved]
-        + [pl.BlockSpec(memory_space=pl.ANY)],
+        + [pl.BlockSpec(v.shape, lambda i: (0, 0)) for v in fixed]
+        + [tile if block_of_out else pl.BlockSpec(memory_space=pl.ANY)],
         out_specs=tile,
-        input_output_aliases={8: 0},
+        input_output_aliases={2 + len(parts) + len(fixed): 0},
         compiler_params=pltpu.CompilerParams(vmem_limit_bytes=VMEM_BYTES),
-        cost_estimate=pl.CostEstimate(flops=2 * 10**9, bytes_accessed=0, transcendentals=0),
-    )(place, top, *parts, *solved, out)
+        cost_estimate=pl.CostEstimate(flops=flops, bytes_accessed=0, transcendentals=0),
+    )(place, top, *parts, *fixed, out)
+
+
+def update_last(place, top, last, solved, out):
+    return last_call(update_last_kernel, place, top, last, solved, out, False, 2 * 10**9)
+
+
+def finish(place, top, returned, out):
+    return last_call(finish_kernel, place, top, (returned,), (), out, True, 10**9)
 
 
 def nothing(*refs):
@@ -224,7 +234,7 @@
         in_specs=anywhere,
         out_specs=anywhere,
         input_output_aliases={i: i for i in range(len(values))},
-        compiler_params=pltpu.CompilerParams(vmem_limit_bytes=VMEM_BYTES),
+        compiler_params=pltpu.CompilerParams(vmem_limit_bytes=STAGE_BYTES),
         cost_estimate=pl.CostEstimate(flops=STAGE_FLOPS, bytes_accessed=0, transcendentals=0),
     )(*values)
 
@@ -271,9 +281,10 @@
 
     lead_own, rest_own, last_own = both(0, block), both(block, raw), both(raw, rows)
     top = test_kernel[:block]
-    given = along_row(jnp.where(even, top[half:], top[:half]), ((0, 1), (1, 0)), ALL_COLS)
+    given, lead_own = tied((jnp.where(even, top[half:], top[:half]), lead_own))
+    given = along_row(given, ((0, 1), (1, 0)), ALL_COLS)
     token = jnp.zeros((8, 128), jnp.float32)
-    given, lead_own, rest_own = tied((given, lead_own, rest_own))
+    given, rest_own = tied((given, rest_own))
 
     mine = jnp.where(
         even,
@@ -296,13 +307,13 @@
     token, rest_swap, rest_mid, got = stage(token, rest_swap, rest_mid, got)
 
     mine = far_or(got, mine)
-    token, crossed, lead_far = stage(token, crossed, lead_far)
-
-    lead_cc = along_col(lead_far, MID_END, most)
     hop = along_col(mine, END_MID, every)
-    rest_c = along_col(rest_mid, MID_END, every)
     rest_far = along_col(rest_swap, MID_MID, every)
     inverses = split_inverses(*tied((first_inverse, second_inverse, token))[:2])
+    token, crossed, lead_far = stage(token, crossed, lead_far)
+
+    lead_cc = along_col(lead_far, MID_END, most)
+    rest_c = along_col(rest_mid, MID_END, every)
     token, lead_cc = stage(token, lead_cc)
 
     slabs = [v[:, :slab] for v in (lead_own, lead_swap, lead_mid, lead_far, crossed, lead_cc)]
@@ -339,7 +350,8 @@
 
     rest = (rest_own, rest_swap, rest_mid, rest_far, rest_c, rest_cc)
     out = update_raw(place, test_kernel, solved, rest, block, False, out)
-    return finish(place, test_kernel, returned, last, solved, out)
+    out = update_last(place, test_kernel, last, solved, out)
+    return finish(place, test_kernel, returned, out)
 
 
 def solution(mesh):

time: 153 us -> 143 us (0.935)
  waiting for transfers between devices: 32.3 us -> 47.8 us
  Pallas kernels: 38.6 us -> 24.9 us
  local copies, waits for them, and re-layouts: 14.9 us -> 6.85 us
  other arithmetic: 13.6 us -> 7.04 us
  starting transfers between devices: 52.1 us -> 55.1 us
    ppermute x12, waiting for transfers between devices: 9.08 us -> 24.7 us  [along_col(): return lax.ppermute(value, AXES, pairs_of(pairs, rows))]
    unnamed x64 -> x44, local copies, waits for them, and re-layouts: 13.4 us -> 4.27 us
    pallas_call x2, Pallas kernels: 13.7 us -> 7.3 us  [solve(): pl.pallas_call(solve_kernel, out_shape=[part, part], in_specs=[SMEM] + [p...]
    ppermute x9, starting transfers between devices: 21.3 us -> 27.3 us  [along_row(): lax.ppermute(value, AXES, [(a * COLS + c, b * COLS + c) for a, b in pairs...]
    pallas_call x2, Pallas kernels: 13.5 us -> 10.1 us  [update_raw(): pl.pallas_call(functools.partial(update_raw_kernel, blocks), grid=(group[...]
    concatenate x3, other arithmetic: 3.02 us -> 0.14 us  [both(): jnp.concatenate([first_panel[low:high], second_panel[low:high]], axis=1)]
    select_n x3, other arithmetic: 3.72 us -> 0.9 us  [ordered(): return jnp.concatenate([jnp.where(end, a, b) for a, b in pairs], axis=1)]
    pallas_call x1, Pallas kernels: 2.95 us -> 0.28 us  [split_inverses(): pl.pallas_call(split_kernel, out_shape=[jax.ShapeDtypeStruct(one.shape, j...]
  transfers between devices with their start and end apart: 22 -> 22, of which waited for: 8 -> 11; matrix products, arithmetic and copies ran while one was open for 9% -> 4% of each run, Pallas kernels for 23% -> 16%
where the time goes in v5:
time: 143 us; the launch traced here: 142 us
  starting transfers between devices  55.1 us (39%)
  waiting for transfers between devices  47.8 us (33%)
  Pallas kernels  24.9 us (17%)
  other arithmetic  7.04 us (5%)
  local copies, waits for them, and re-layouts  6.85 us (5%)
    ppermute x9, starting transfers between devices, along_row(): lax.ppermute(value, AXES, [(a * COLS + c, b * COLS + c) for a, b in pairs...  27.3 us
    ppermute x12, waiting for transfers between devices, along_col(): return lax.ppermute(value, AXES, pairs_of(pairs, rows))  24.7 us
    ppermute x12, starting transfers between devices, along_col(): return lax.ppermute(value, AXES, pairs_of(pairs, rows))  21.5 us
    ppermute x9, waiting for transfers between devices, along_row(): lax.ppermute(value, AXES, [(a * COLS + c, b * COLS + c) for a, b in pairs...  15.3 us
    pallas_call x2, Pallas kernels, update_raw(): pl.pallas_call(functools.partial(update_raw_kernel, blocks), grid=(group[...  10.1 us
    ppermute x1, waiting for transfers between devices, four(): lax.ppermute(jnp.where(end, last_own, lead_mid), AXES, pairs_of(MID_END,...  7.68 us
    pallas_call x2, Pallas kernels, solve(): pl.pallas_call(solve_kernel, out_shape=[part, part], in_specs=[SMEM] + [p...  7.3 us
    ppermute x1, starting transfers between devices, four(): lax.ppermute(jnp.where(end, last_own, lead_mid), AXES, pairs_of(MID_END,...  6.3 us
  transfers between devices with their start and end apart: 22, of which 11 were waited for; matrix products, arithmetic and copies ran while one was open for 4% of the time, Pallas kernels for 16%

profile of v5, /device:TPU:0, one launch (start us, length us, event | category | flops | bytes accessed | tf_op | source)
XLA Modules:
  0.0 142.4 jit_solution(10832816688307102145)
XLA Ops:
  0.0 1.3 fusion
  1.3 1.3 fusion.1
  2.7 0.7 collective-permute-start
  3.4 0.7 collective-permute-start.1
  4.1 5.7 %collective-permute-start.2 = (f32[256,512]{1,0:T(8,128)S(1)}, f32[256,512]{1,0:T(8,128)S(1)}, u32[]{:S(2)}, u32[]{:S(2)}) collective-permute-start(f32[256,512]{1,0:T(8,128)S(1)} %get-tuple-element.54), channel_id=1, source_target_pairs={{0,4},{1,5},{2,6},{3,7},{4,0},{5,1},{6,2},{7,3}} | collective-permute-start | bytes 1572872 | tf_op jit(solution)/shard_map/ppermute | solution.py:55
  9.8 1.0 slice-done
  11.3 1.1 maximum_select_fusion
  12.4 3.4 %collective-permute-start.3 = (f32[512,512]{1,0:T(8,128)}, f32[512,512]{1,0:T(8,128)}, u32[]{:S(2)}, u32[]{:S(2)}) collective-permute-start(f32[512,512]{1,0:T(8,128)} %maximum_select_fusion), channel_id=1, source_target_pairs={{0,8},{1,9},{2,10},{3,11},{4,20},{5,21},{6,22},{7,23}} | collective-permute-start | bytes 3145736 | tf_op jit(solution)/shard_map/ppermute | solution.py:55
  16.0 4.4 %collective-permute-start.4 = (f32[1024,256]{1,0:T(8,128)S(1)}, f32[1024,256]{1,0:T(8,128)}, u32[]{:S(2)}, u32[]{:S(2)}) collective-permute-start(f32[1024,256]{1,0:T(8,128)S(1)} %pad_maximum_fusion.own), channel_id=1, source_target_pairs={{0,1},{3,2},{1,0},{2,3},{4,5},{7,6},{5,4},{6,7},{8,9},{11,10},{9,8... | collective-permute-start | bytes 3145736 | tf_op jit(solution)/shard_map/ppermute | solution.py:51
  20.4 1.7 %collective-permute-start.5 = (f32[1024,256]{1,0:T(8,128)S(1)}, f32[1024,256]{1,0:T(8,128)}, u32[]{:S(2)}, u32[]{:S(2)}) collective-permute-start(f32[1024,256]{1,0:T(8,128)S(1)} %pad_maximum_fusion.own), channel_id=1, source_target_pairs={{1,2},{2,1},{5,6},{6,5},{9,10},{10,9},{13,14},{14,13},{17,18},{18,... | collective-permute-start | bytes 3145736 | tf_op jit(solution)/shard_map/ppermute | solution.py:51
  22.1 5.4 %collective-permute-done.3.refs_3_ = f32[512,512]{1,0:T(8,128)} collective-permute-done((f32[512,512]{1,0:T(8,128)}, f32[512,512]{1,0:T(8,128)}, u32[]{:S(2)}, u32[]{:S(2)}) %collective-permute-start.3) | collective-permute-done | bytes 1048608 | tf_op jit(solution)/shard_map/ppermute | solution.py:55
  27.5 1.8 %broadcast_select_fusion.1 = f32[512,512]{1,0:T(8,128)S(1)} fusion(f32[512,512]{1,0:T(8,128)} %get-tuple-element.58, f32[512,512]{1,0:T(8,128)} %maximum_select_fusion, pred[]{:T(512)S(6)} %or.16), kind=kLoop, calls=%fused_computation.8 | loop fusion | flops 262144 | bytes 3145729 | tf_op jit(solution)/shard_map/jit(_where)/select_n | solution.py:271
  29.3 1.5 %collective-permute-start.6 = (f32[512,512]{1,0:T(8,128)S(1)}, f32[512,512]{1,0:T(8,128)S(1)}, u32[]{:S(2)}, u32[]{:S(2)}) collective-permute-start(f32[512,512]{1,0:T(8,128)S(1)} %broadcast_select_fusion.1), channel_id=1, source_target_pairs={{8,24},{9,25},{10,26},{11,27},{20,28},{21,29},{22,30},{23,31},{0,1... | collective-permute-start | bytes 3145736 | tf_op jit(solution)/shard_map/ppermute | solution.py:55
  30.9 6.3 %collective-permute-start.7 = (f32[512,256]{1,0:T(8,128)S(1)}, f32[512,256]{1,0:T(8,128)S(1)}, u32[]{:S(2)}, u32[]{:S(2)}) collective-permute-start(f32[512,256]{1,0:T(8,128)S(1)} %broadcast_select_fusion.4), channel_id=1, source_target_pairs={{5,4},{6,7},{9,8},{10,11},{13,12},{14,15},{17,16},{18,19},{21,20},... | collective-permute-start | bytes 1572872 | tf_op jit(solution)/shard_map/ppermute | solution.py:303
  37.2 0.7 collective-permute-start.8
  37.9 0.8 slice_select_fusion.4
  38.8 5.8 %collective-permute-done.4.refs_1_ = f32[1024,256]{1,0:T(8,128)} collective-permute-done((f32[1024,256]{1,0:T(8,128)S(1)}, f32[1024,256]{1,0:T(8,128)}, u32[]{:S(2)}, u32[]{:S(2)}) %collective-permute-start.4) | collective-permute-done | bytes 1048608 | tf_op jit(solution)/shard_map/ppermute | solution.py:51
  44.6 1.0 copy-done.16
  45.6 7.7 %collective-permute-done.7.refs_1_ = f32[512,256]{1,0:T(8,128)S(1)} collective-permute-done((f32[512,256]{1,0:T(8,128)S(1)}, f32[512,256]{1,0:T(8,128)S(1)}, u32[]{:S(2)}, u32[]{:S(2)}) %collective-permute-start.7) | collective-permute-done | bytes 524320 | tf_op jit(solution)/shard_map/ppermute | solution.py:303
  53.3 0.8 collective-permute-start.9
  54.1 1.8 %collective-permute-start.10 = (f32[1024,256]{1,0:T(8,128)}, f32[1024,256]{1,0:T(8,128)}, u32[]{:S(2)}, u32[]{:S(2)}) collective-permute-start(f32[1024,256]{1,0:T(8,128)} %get-tuple-element.68.swap), channel_id=1, source_target_pairs={{1,2},{2,1},{5,6},{6,5},{9,10},{10,9},{13,14},{14,13},{17,18},{18,... | collective-permute-start | bytes 3145736 | tf_op jit(solution)/shard_map/ppermute | solution.py:51
  56.2 5.0 %collective-permute-start.11 = (f32[512,512]{1,0:T(8,128)S(1)}, f32[512,512]{1,0:T(8,128)S(1)}, u32[]{:S(2)}, u32[]{:S(2)}) collective-permute-start(f32[512,512]{1,0:T(8,128)S(1)} %broadcast_select_fusion.refs_0_), channel_id=1, source_target_pairs={{0,1},{3,2},{4,5},{7,6},{8,9},{11,10},{12,13},{15,14},{16,17},{19,... | collective-permute-start | bytes 3145736 | tf_op jit(solution)/shard_map/ppermute | solution.py:51
  61.2 1.3 collective-permute-start.14
  62.5 0.3 shard_map.75
  63.0 0.9 copy-done.20
  64.0 1.3 collective-permute-start.12
  65.3 2.5 %collective-permute-done.12 = f32[256,512]{1,0:T(8,128)S(1)} collective-permute-done((f32[256,512]{1,0:T(8,128)S(1)}, f32[256,512]{1,0:T(8,128)S(1)}, u32[]{:S(2)}, u32[]{:S(2)}) %collective-permute-start.12) | collective-permute-done | bytes 524320 | tf_op jit(solution)/shard_map/ppermute | solution.py:55
  67.9 9.1 %collective-permute-start.13 = (f32[256,512]{1,0:T(8,128)S(1)}, f32[256,512]{1,0:T(8,128)S(1)}, u32[]{:S(2)}, u32[]{:S(2)}) collective-permute-start(f32[256,512]{1,0:T(8,128)S(1)} %slice_select_fusion), channel_id=1, source_target_pairs={{0,8},{1,9},{2,10},{3,11},{4,20},{5,21},{6,22},{7,23}} | collective-permute-start | bytes 1572872 | tf_op jit(solution)/shard_map/ppermute | solution.py:55
  77.0 1.1 pad_maximum_fusion.2
  78.2 1.6 %collective-permute-start.17 = (f32[512,512]{1,0:T(8,128)}, f32[512,512]{1,0:T(8,128)}, u32[]{:S(2)}, u32[]{:S(2)}) collective-permute-start(f32[512,512]{1,0:T(8,128)} %pad_maximum_fusion.2), channel_id=1, source_target_pairs={{1,2},{2,1},{5,6},{6,5},{9,10},{10,9},{13,14},{14,13},{17,18},{18,... | collective-permute-start | bytes 3145736 | tf_op jit(solution)/shard_map/ppermute | solution.py:51
  79.8 2.6 %collective-permute-done.11.refs_2_ = f32[512,512]{1,0:T(8,128)S(1)} collective-permute-done((f32[512,512]{1,0:T(8,128)S(1)}, f32[512,512]{1,0:T(8,128)S(1)}, u32[]{:S(2)}, u32[]{:S(2)}) %collective-permute-start.11) | collective-permute-done | bytes 1048608 | tf_op jit(solution)/shard_map/ppermute | solution.py:51
  82.4 1.2 collective-permute-done.13.refs_3_
  83.7 6.2 %collective-permute-start.15 = (f32[256,512]{1,0:T(8,128)S(1)}, f32[256,512]{1,0:T(8,128)S(1)}, u32[]{:S(2)}, u32[]{:S(2)}) collective-permute-start(f32[256,512]{1,0:T(8,128)S(1)} %broadcast_select_fusion.3), channel_id=1, source_target_pairs={{8,24},{9,25},{10,26},{11,27},{20,28},{21,29},{22,30},{23,31},{0,1... | collective-permute-start | bytes 1572872 | tf_op jit(solution)/shard_map/ppermute | solution.py:55
  90.0 1.3 collective-permute-start.21
  91.3 5.2 %collective-permute-done.15.refs_2_ = f32[256,512]{1,0:T(8,128)S(1)} collective-permute-done((f32[256,512]{1,0:T(8,128)S(1)}, f32[256,512]{1,0:T(8,128)S(1)}, u32[]{:S(2)}, u32[]{:S(2)}) %collective-permute-start.15) | collective-permute-done | bytes 524320 | tf_op jit(solution)/shard_map/ppermute | solution.py:55
  96.8 1.1 copy-done.15
  97.9 0.8 collective-permute-done.18.refs_3_
  98.7 3.7 %shard_map.76 = (bf16[1024,512]{1,0:T(8,128)(2,1)S(1)}, bf16[1024,512]{1,0:T(8,128)(2,1)S(1)}) custom-call(s32[5]{0:T(128)S(1)} %convert_element_type.3.place, f32[512,512]{1,0:T(8,128)S(1)} %get-tuple-element.73.refs_0_, f32[512,512]{1,0:T(8,128)S(1)} %get-tuple-element.78.refs_1_, f32[256,512]{1,0:T(8,128)S(1)} %broadcast_select_fusion.2.refs_2_, ...), custom_call_target="tpu_custom_call" | custom-call | flops 3000000000 | tf_op jit(solution)/shard_map/pallas_call | solution.py:123
  102.4 1.0 copy-done.3
  103.6 3.1 %shard_map.78 = f32[512,512]{1,0:T(8,128)S(1)} custom-call(f32[512,256]{1,0:T(8,128)S(1)} %copy-done.5, f32[512,256]{1,0:T(8,128)S(1)} %copy-done.3, f32[512,512]{1,0:T(8,128)} %get-tuple-element.88.both, bf16[1024,512]{1,0:T(8,128)(2,1)S(1)} %get-tuple-element.89.high, bf16[1024,512]{1,0:T(8,128)(2,1)S(1)} %get-tuple-element.90.low), custom_call_target="tpu_custom_call" | custom-call | flops 2000000000 | tf_op jit(solution)/shard_map/pallas_call | solution.py:139
  106.6 1.5 %collective-permute-start.19 = (f32[512,512]{1,0:T(8,128)S(1)}, f32[512,512]{1,0:T(8,128)S(1)}, u32[]{:S(2)}, u32[]{:S(2)}) collective-permute-start(f32[512,512]{1,0:T(8,128)S(1)} %shard_map.78), channel_id=1, source_target_pairs={{1,0},{2,3},{5,4},{6,7},{9,8},{10,11},{13,12},{14,15},{17,16},{18,... | collective-permute-start | bytes 3145736 | tf_op jit(solution)/shard_map/ppermute | solution.py:51
  108.2 3.6 %shard_map.79 = (bf16[1024,512]{1,0:T(8,128)(2,1)S(1)}, bf16[1024,512]{1,0:T(8,128)(2,1)S(1)}) custom-call(s32[5]{0:T(128)S(1)} %convert_element_type.3.place, f32[512,512]{1,0:T(8,128)S(1)} %copy-done.15, f32[512,512]{1,0:T(8,128)S(1)} %collective-permute-done.20.refs_1_, f32[256,512]{1,0:T(8,128)S(1)} %broadcast_select_fusion.2.refs_2_, ...), custom_call_target="tpu_custom_call" | custom-call | flops 3000000000 | tf_op jit(solution)/shard_map/pallas_call | solution.py:123
  111.8 3.5 %shard_map.82.refs_2_ = f32[2048,512]{1,0:T(8,128)} custom-call(s32[5]{0:T(128)S(1)} %convert_element_type.3.place, f32[2048,512]{1,0:T(8,128)S(1)} %copy-done, bf16[1024,512]{1,0:T(8,128)(2,1)S(1)} %get-tuple-element.94.high, bf16[1024,512]{1,0:T(8,128)(2,1)S(1)} %get-tuple-element.95.low, f32[512,256]{1,0:T(8,128)S(1)} %copy-done.8, ...), custom_call_target="tpu_custom_call" | custom-call | flops 3000000000 | tf_op jit(solution)/shard_map/pallas_call | solution.py:172
  115.4 2.8 %collective-permute-done.21.refs_1_ = f32[1024,256]{1,0:T(8,128)} collective-permute-done((f32[1024,256]{1,0:T(8,128)}, f32[1024,256]{1,0:T(8,128)}, u32[]{:S(2)}, u32[]{:S(2)}) %collective-permute-start.21) | collective-permute-done | bytes 1048608 | tf_op jit(solution)/shard_map/ppermute | solution.py:51
  118.2 6.6 %shard_map.84.kept = f32[2048,512]{1,0:T(8,128)} custom-call(s32[5]{0:T(128)S(1)} %convert_element_type.3.place, f32[2048,512]{1,0:T(8,128)S(1)} %copy-done, bf16[1024,512]{1,0:T(8,128)(2,1)S(1)} %get-tuple-element.94.high, bf16[1024,512]{1,0:T(8,128)(2,1)S(1)} %get-tuple-element.95.low, ...), custom_call_target="tpu_custom_call", output_to_operand_aliasing={{}: (10, {})} | custom-call | flops 3000000000 | tf_op jit(solution)/shard_map/pallas_call | solution.py:172
  124.8 2.0 %shard_map.85.kept = f32[2048,512]{1,0:T(8,128)} custom-call(s32[5]{0:T(128)S(1)} %convert_element_type.3.place, f32[2048,512]{1,0:T(8,128)S(1)} %copy-done, f32[512,256]{1,0:T(8,128)S(1)} %copy-done.5, f32[512,256]{1,0:T(8,128)S(1)} %copy-done.3, f32[512,512]{1,0:T(8,128)} %get-tuple-element.88.both, ...), custom_call_target="tpu_custom_call", output_to_operand_aliasing={{}: (7, {})} | custom-call | flops 2000000000 | tf_op jit(solution)/shard_map/pallas_call | solution.py:202
  126.9 13.4 %collective-permute-done.19.returned = f32[512,512]{1,0:T(8,128)S(1)} collective-permute-done((f32[512,512]{1,0:T(8,128)S(1)}, f32[512,512]{1,0:T(8,128)S(1)}, u32[]{:S(2)}, u32[]{:S(2)}) %collective-permute-start.19) | collective-permute-done | bytes 1048608 | tf_op jit(solution)/shard_map/ppermute | solution.py:51
  140.3 2.1 %shard_map.86 = f32[2048,512]{1,0:T(8,128)} custom-call(s32[5]{0:T(128)S(1)} %convert_element_type.3.place, f32[2048,512]{1,0:T(8,128)S(1)} %copy-done, f32[512,512]{1,0:T(8,128)S(1)} %collective-permute-done.19.returned, f32[2048,512]{1,0:T(8,128)} %shard_map.85.kept), custom_call_target="tpu_custom_call", output_to_operand_aliasing={{}: (3, {})} | custom-call | flops 1000000000 | tf_op jit(solution)/shard_map/pallas_call | solution.py:202
  (97 shorter events, 1.9 us)
Async XLA Ops:
  2.7 7.2 %copy-start.6 = (f32[512,256]{1,0:T(8,128)}, f32[512,256]{1,0:T(8,128)S(1)}, u32[]{:S(2)}) copy-start(f32[512,256]{1,0:T(8,128)S(1)} %pad_maximum_fusion.3.own) | copy-start | bytes 1572868
  2.7 19.4 %collective-permute-start = (f32[512,256]{1,0:T(8,128)S(1)}, f32[512,256]{1,0:T(8,128)S(1)}, u32[]{:S(2)}, u32[]{:S(2)}) collective-permute-start(f32[512,256]{1,0:T(8,128)S(1)} %pad_maximum_fusion.3.own), channel_id=1, source_target_pairs={{4,5},{7,6},{5,4},{6,7},{8,9},{11,10},{9,8},{10,11},{12,13},{15,14... | collective-permute-start | bytes 1572872 | tf_op jit(solution)/shard_map/ppermute | solution.py:51
  3.4 18.7 %collective-permute-start.1 = (f32[512,256]{1,0:T(8,128)S(1)}, f32[512,256]{1,0:T(8,128)S(1)}, u32[]{:S(2)}, u32[]{:S(2)}) collective-permute-start(f32[512,256]{1,0:T(8,128)S(1)} %pad_maximum_fusion.3.own), channel_id=1, source_target_pairs={{5,6},{6,5},{9,10},{10,9},{13,14},{14,13},{17,18},{18,17},{21,22},... | collective-permute-start | bytes 1572872 | tf_op jit(solution)/shard_map/ppermute | solution.py:51
  4.1 7.2 %collective-permute-start.2 = (f32[256,512]{1,0:T(8,128)S(1)}, f32[256,512]{1,0:T(8,128)S(1)}, u32[]{:S(2)}, u32[]{:S(2)}) collective-permute-start(f32[256,512]{1,0:T(8,128)S(1)} %get-tuple-element.54), channel_id=1, source_target_pairs={{0,4},{1,5},{2,6},{3,7},{4,0},{5,1},{6,2},{7,3}} | collective-permute-start | bytes 1572872 | tf_op jit(solution)/shard_map/ppermute | solution.py:55
  9.8 1.0 slice-start
  9.8 1.2 slice-start.1
  12.4 15.0 %collective-permute-start.3 = (f32[512,512]{1,0:T(8,128)}, f32[512,512]{1,0:T(8,128)}, u32[]{:S(2)}, u32[]{:S(2)}) collective-permute-start(f32[512,512]{1,0:T(8,128)} %maximum_select_fusion), channel_id=1, source_target_pairs={{0,8},{1,9},{2,10},{3,11},{4,20},{5,21},{6,22},{7,23}} | collective-permute-start | bytes 3145736 | tf_op jit(solution)/shard_map/ppermute | solution.py:55
  16.0 28.6 %collective-permute-start.4 = (f32[1024,256]{1,0:T(8,128)S(1)}, f32[1024,256]{1,0:T(8,128)}, u32[]{:S(2)}, u32[]{:S(2)}) collective-permute-start(f32[1024,256]{1,0:T(8,128)S(1)} %pad_maximum_fusion.own), channel_id=1, source_target_pairs={{0,1},{3,2},{1,0},{2,3},{4,5},{7,6},{5,4},{6,7},{8,9},{11,10},{9,8... | collective-permute-start | bytes 3145736 | tf_op jit(solution)/shard_map/ppermute | solution.py:51
  20.4 24.2 %collective-permute-start.5 = (f32[1024,256]{1,0:T(8,128)S(1)}, f32[1024,256]{1,0:T(8,128)}, u32[]{:S(2)}, u32[]{:S(2)}) collective-permute-start(f32[1024,256]{1,0:T(8,128)S(1)} %pad_maximum_fusion.own), channel_id=1, source_target_pairs={{1,2},{2,1},{5,6},{6,5},{9,10},{10,9},{13,14},{14,13},{17,18},{18,... | collective-permute-start | bytes 3145736 | tf_op jit(solution)/shard_map/ppermute | solution.py:51
  27.5 3.4 %copy-start.1 = (f32[512,256]{1,0:T(8,128)}, f32[512,256]{1,0:T(8,128)S(1)}, u32[]{:S(2)}) copy-start(f32[512,256]{1,0:T(8,128)S(1)} %get-tuple-element.76.own) | copy-start | bytes 1572868
  27.5 3.4 %copy-start.9 = (f32[512,256]{1,0:T(8,128)}, f32[512,256]{1,0:T(8,128)S(1)}, u32[]{:S(2)}) copy-start(f32[512,256]{1,0:T(8,128)S(1)} %get-tuple-element.61.mid) | copy-start | bytes 1572868
  29.3 1.5 %copy-start.18 = (f32[512,512]{1,0:T(8,128)}, f32[512,512]{1,0:T(8,128)S(1)}, u32[]{:S(2)}) copy-start(f32[512,512]{1,0:T(8,128)S(1)} %broadcast_select_fusion.1) | copy-start | bytes 3145732
  29.3 8.6 %copy-start.7 = (f32[512,256]{1,0:T(8,128)S(1)}, f32[512,256]{1,0:T(8,128)}, u32[]{:S(2)}) copy-start(f32[512,256]{1,0:T(8,128)} %copy-done.6) | copy-start | bytes 1572868
  29.3 15.3 %collective-permute-start.6 = (f32[512,512]{1,0:T(8,128)S(1)}, f32[512,512]{1,0:T(8,128)S(1)}, u32[]{:S(2)}, u32[]{:S(2)}) collective-permute-start(f32[512,512]{1,0:T(8,128)S(1)} %broadcast_select_fusion.1), channel_id=1, source_target_pairs={{8,24},{9,25},{10,26},{11,27},{20,28},{21,29},{22,30},{23,31},{0,1... | collective-permute-start | bytes 3145736 | tf_op jit(solution)/shard_map/ppermute | solution.py:55
  30.9 22.3 %collective-permute-start.7 = (f32[512,256]{1,0:T(8,128)S(1)}, f32[512,256]{1,0:T(8,128)S(1)}, u32[]{:S(2)}, u32[]{:S(2)}) collective-permute-start(f32[512,256]{1,0:T(8,128)S(1)} %broadcast_select_fusion.4), channel_id=1, source_target_pairs={{5,4},{6,7},{9,8},{10,11},{13,12},{14,15},{17,16},{18,19},{21,20},... | collective-permute-start | bytes 1572872 | tf_op jit(solution)/shard_map/ppermute | solution.py:303
  37.2 16.0 %collective-permute-start.8 = (f32[512,256]{1,0:T(8,128)S(1)}, f32[512,256]{1,0:T(8,128)S(1)}, u32[]{:S(2)}, u32[]{:S(2)}) collective-permute-start(f32[512,256]{1,0:T(8,128)S(1)} %get-tuple-element.62.swap), channel_id=1, source_target_pairs={{5,6},{6,5},{9,10},{10,9},{13,14},{14,13},{17,18},{18,17},{21,22},... | collective-permute-start | bytes 1572872 | tf_op jit(solution)/shard_map/ppermute | solution.py:51
  44.6 1.0 copy-start.16
  53.3 23.8 %copy-start.4 = (f32[512,256]{1,0:T(8,128)}, f32[512,256]{1,0:T(8,128)S(1)}, u32[]{:S(2)}) copy-start(f32[512,256]{1,0:T(8,128)S(1)} %get-tuple-element.77.near_end.c) | copy-start | bytes 1572868
  53.3 2.7 %copy-start.17 = (f32[512,512]{1,0:T(8,128)S(1)}, f32[512,512]{1,0:T(8,128)}, u32[]{:S(2)}) copy-start(f32[512,512]{1,0:T(8,128)} %copy-done.16) | copy-start | bytes 3145732
  53.3 2.7 %copy-start.19 = (f32[512,512]{1,0:T(8,128)S(1)}, f32[512,512]{1,0:T(8,128)}, u32[]{:S(2)}) copy-start(f32[512,512]{1,0:T(8,128)} %copy-done.18) | copy-start | bytes 3145732
  53.3 9.2 %copy-start.12 = (f32[512,512]{1,0:T(8,128)S(1)}, f32[512,512]{1,0:T(8,128)}, u32[]{:S(2)}) copy-start(f32[512,512]{1,0:T(8,128)} %one) | copy-start | bytes 3145732
  53.3 9.2 %copy-start.13 = (f32[512,512]{1,0:T(8,128)S(1)}, f32[512,512]{1,0:T(8,128)}, u32[]{:S(2)}) copy-start(f32[512,512]{1,0:T(8,128)} %two) | copy-start | bytes 3145732
  53.3 9.5 %copy-start.10 = (f32[512,256]{1,0:T(8,128)S(1)}, f32[512,256]{1,0:T(8,128)}, u32[]{:S(2)}) copy-start(f32[512,256]{1,0:T(8,128)} %copy-done.9) | copy-start | bytes 1572868
  53.3 9.6 %collective-permute-start.9 = (f32[512,256]{1,0:T(8,128)S(1)}, f32[512,256]{1,0:T(8,128)S(1)}, u32[]{:S(2)}, u32[]{:S(2)}) collective-permute-start(f32[512,256]{1,0:T(8,128)S(1)} %get-tuple-element.66.far), channel_id=1, source_target_pairs={{5,4},{6,7},{9,8},{10,11},{13,12},{14,15},{17,16},{18,19},{21,20},... | collective-permute-start | bytes 1572872 | tf_op jit(solution)/shard_map/ppermute | solution.py:51
  54.1 25.7 %collective-permute-start.10 = (f32[1024,256]{1,0:T(8,128)}, f32[1024,256]{1,0:T(8,128)}, u32[]{:S(2)}, u32[]{:S(2)}) collective-permute-start(f32[1024,256]{1,0:T(8,128)} %get-tuple-element.68.swap), channel_id=1, source_target_pairs={{1,2},{2,1},{5,6},{6,5},{9,10},{10,9},{13,14},{14,13},{17,18},{18,... | collective-permute-start | bytes 3145736 | tf_op jit(solution)/shard_map/ppermute | solution.py:51
  56.2 6.7 %copy-start.14 = (f32[512,512]{1,0:T(8,128)}, f32[512,512]{1,0:T(8,128)S(1)}, u32[]{:S(2)}) copy-start(f32[512,512]{1,0:T(8,128)S(1)} %broadcast_select_fusion.refs_0_) | copy-start | bytes 3145732
  56.2 26.3 %collective-permute-start.11 = (f32[512,512]{1,0:T(8,128)S(1)}, f32[512,512]{1,0:T(8,128)S(1)}, u32[]{:S(2)}, u32[]{:S(2)}) collective-permute-start(f32[512,512]{1,0:T(8,128)S(1)} %broadcast_select_fusion.refs_0_), channel_id=1, source_target_pairs={{0,1},{3,2},{4,5},{7,6},{8,9},{11,10},{12,13},{15,14},{16,17},{19,... | collective-permute-start | bytes 3145736 | tf_op jit(solution)/shard_map/ppermute | solution.py:51
  61.2 30.1 %collective-permute-start.14 = (f32[1024,256]{1,0:T(8,128)}, f32[1024,256]{1,0:T(8,128)}, u32[]{:S(2)}, u32[]{:S(2)}) collective-permute-start(f32[1024,256]{1,0:T(8,128)} %get-tuple-element.71.mid), channel_id=1, source_target_pairs={{1,0},{2,3},{5,4},{6,7},{9,8},{10,11},{13,12},{14,15},{17,16},{18,... | collective-permute-start | bytes 3145736 | tf_op jit(solution)/shard_map/ppermute | solution.py:51
  62.9 1.0 copy-start.20
  62.9 1.0 copy-start.21
  64.0 3.8 %collective-permute-start.12 = (f32[256,512]{1,0:T(8,128)S(1)}, f32[256,512]{1,0:T(8,128)S(1)}, u32[]{:S(2)}, u32[]{:S(2)}) collective-permute-start(f32[256,512]{1,0:T(8,128)S(1)} %slice.69), channel_id=1, source_target_pairs={{4,0},{5,1},{6,2},{7,3}} | collective-permute-start | bytes 1572872 | tf_op jit(solution)/shard_map/ppermute | solution.py:55
  67.9 9.1 %copy-start.2 = (f32[512,256]{1,0:T(8,128)S(1)}, f32[512,256]{1,0:T(8,128)}, u32[]{:S(2)}) copy-start(f32[512,256]{1,0:T(8,128)} %copy-done.1) | copy-start | bytes 1572868
  67.9 15.7 %collective-permute-start.13 = (f32[256,512]{1,0:T(8,128)S(1)}, f32[256,512]{1,0:T(8,128)S(1)}, u32[]{:S(2)}, u32[]{:S(2)}) collective-permute-start(f32[256,512]{1,0:T(8,128)S(1)} %slice_select_fusion), channel_id=1, source_target_pairs={{0,8},{1,9},{2,10},{3,11},{4,20},{5,21},{6,22},{7,23}} | collective-permute-start | bytes 1572872 | tf_op jit(solution)/shard_map/ppermute | solution.py:55
  78.2 24.2 %collective-permute-start.17 = (f32[512,512]{1,0:T(8,128)}, f32[512,512]{1,0:T(8,128)}, u32[]{:S(2)}, u32[]{:S(2)}) collective-permute-start(f32[512,512]{1,0:T(8,128)} %pad_maximum_fusion.2), channel_id=1, source_target_pairs={{1,2},{2,1},{5,6},{6,5},{9,10},{10,9},{13,14},{14,13},{17,18},{18,... | collective-permute-start | bytes 3145736 | tf_op jit(solution)/shard_map/ppermute | solution.py:51
  83.7 12.9 %collective-permute-start.15 = (f32[256,512]{1,0:T(8,128)S(1)}, f32[256,512]{1,0:T(8,128)S(1)}, u32[]{:S(2)}, u32[]{:S(2)}) collective-permute-start(f32[256,512]{1,0:T(8,128)S(1)} %broadcast_select_fusion.3), channel_id=1, source_target_pairs={{8,24},{9,25},{10,26},{11,27},{20,28},{21,29},{22,30},{23,31},{0,1... | collective-permute-start | bytes 1572872 | tf_op jit(solution)/shard_map/ppermute | solution.py:55
  90.0 6.7 %collective-permute-start.16 = (f32[512,512]{1,0:T(8,128)S(1)}, f32[512,512]{1,0:T(8,128)S(1)}, u32[]{:S(2)}, u32[]{:S(2)}) collective-permute-start(f32[512,512]{1,0:T(8,128)S(1)} %get-tuple-element.73.refs_0_), channel_id=1, source_target_pairs={{0,4},{1,5},{2,6},{3,7},{4,0},{5,1},{6,2},{7,3},{8,12},{9,13},{10,... | collective-permute-start | bytes 3145736 | tf_op jit(solution)/shard_map/ppermute | solution.py:55
  90.0 28.2 %collective-permute-start.21 = (f32[1024,256]{1,0:T(8,128)}, f32[1024,256]{1,0:T(8,128)}, u32[]{:S(2)}, u32[]{:S(2)}) collective-permute-start(f32[1024,256]{1,0:T(8,128)} %get-tuple-element.96.far), channel_id=1, source_target_pairs={{1,0},{2,3},{5,4},{6,7},{9,8},{10,11},{13,12},{14,15},{17,16},{18,... | collective-permute-start | bytes 3145736 | tf_op jit(solution)/shard_map/ppermute | solution.py:51
  96.7 1.2 copy-start.15
  96.7 2.0 %collective-permute-start.18 = (f32[256,512]{1,0:T(8,128)S(1)}, f32[256,512]{1,0:T(8,128)S(1)}, u32[]{:S(2)}, u32[]{:S(2)}) collective-permute-start(f32[256,512]{1,0:T(8,128)S(1)} %broadcast_select_fusion.2.refs_2_), channel_id=1, source_target_pairs={{0,4},{1,5},{2,6},{3,7},{4,0},{5,1},{6,2},{7,3},{8,12},{9,13},{10,... | collective-permute-start | bytes 1572872 | tf_op jit(solution)/shard_map/ppermute | solution.py:55
  97.9 10.2 %collective-permute-start.20 = (f32[512,512]{1,0:T(8,128)S(1)}, f32[512,512]{1,0:T(8,128)S(1)}, u32[]{:S(2)}, u32[]{:S(2)}) collective-permute-start(f32[512,512]{1,0:T(8,128)S(1)} %copy-done.15), channel_id=1, source_target_pairs={{0,4},{1,5},{2,6},{3,7},{4,0},{5,1},{6,2},{7,3},{8,12},{9,13},{10,... | collective-permute-start | bytes 3145736 | tf_op jit(solution)/shard_map/ppermute | solution.py:55
  102.4 1.0 copy-start.3
  102.4 1.2 copy-start.5
  106.6 33.6 %collective-permute-start.19 = (f32[512,512]{1,0:T(8,128)S(1)}, f32[512,512]{1,0:T(8,128)S(1)}, u32[]{:S(2)}, u32[]{:S(2)}) collective-permute-start(f32[512,512]{1,0:T(8,128)S(1)} %shard_map.78), channel_id=1, source_target_pairs={{1,0},{2,3},{5,4},{6,7},{9,8},{10,11},{13,12},{14,15},{17,16},{18,... | collective-permute-start | bytes 3145736 | tf_op jit(solution)/shard_map/ppermute | solution.py:51
  108.1 3.7 %copy-start = (f32[2048,512]{1,0:T(8,128)S(1)}, f32[2048,512]{1,0:T(8,128)}, u32[]{:S(2)}) copy-start(f32[2048,512]{1,0:T(8,128)} %top.7) | copy-start | bytes 12582916
  108.1 3.7 %copy-start.8 = (f32[512,256]{1,0:T(8,128)S(1)}, f32[512,256]{1,0:T(8,128)}, u32[]{:S(2)}) copy-start(f32[512,256]{1,0:T(8,128)} %copy-done.6) | copy-start | bytes 1572868
  108.2 3.7 %copy-start.11 = (f32[512,256]{1,0:T(8,128)S(1)}, f32[512,256]{1,0:T(8,128)}, u32[]{:S(2)}) copy-start(f32[512,256]{1,0:T(8,128)} %copy-done.9) | copy-start | bytes 1572868

commit v6 on v5

--- a/solution.py
+++ b/solution.py
@@ -7,7 +7,7 @@
 from jax.experimental.pallas import tpu as pltpu
 from jax.sharding import PartitionSpec as P
 
-STAGE_FLOPS = 4 * 10**10
+STAGE_FLOPS = 10**10
 FILLERS = 2
 STAGE_BYTES = 2**20
 
@@ -281,8 +281,8 @@
 
     lead_own, rest_own, last_own = both(0, block), both(block, raw), both(raw, rows)
     top = test_kernel[:block]
-    given, lead_own = tied((jnp.where(even, top[half:], top[:half]), lead_own))
-    given = along_row(given, ((0, 1), (1, 0)), ALL_COLS)
+    top, lead_own = tied((top, lead_own))
+    given = along_row(jnp.where(even, top[half:], top[:half]), ((0, 1), (1, 0)), ALL_COLS)
     token = jnp.zeros((8, 128), jnp.float32)
     given, rest_own = tied((given, rest_own))
 

time: 143 us -> 141 us (0.986)
  waiting for transfers between devices: 47.8 us -> 57 us
  local copies, waits for them, and re-layouts: 6.85 us -> 2.68 us
  other arithmetic: 7.04 us -> 3.67 us
  Pallas kernels: 24.9 us -> 22.3 us
    ppermute x12, waiting for transfers between devices: 24.7 us -> 31.5 us  [along_col(): return lax.ppermute(value, AXES, pairs_of(pairs, rows))]
    unnamed x44 -> x6, local copies, waits for them, and re-layouts: 4.27 us -> 0.01 us
    ppermute x12, starting transfers between devices: 21.5 us -> 19.5 us  [along_col(): return lax.ppermute(value, AXES, pairs_of(pairs, rows))]
  transfers between devices with their start and end apart: 22 -> 22, of which waited for: 11 -> 11; matrix products, arithmetic and copies ran while one was open for 4% -> 3% of each run, Pallas kernels for 16% -> 14%
where the time goes in v6:
time: 141 us; the launch traced here: 140 us
  waiting for transfers between devices  57 us (40%)
  starting transfers between devices  54.2 us (38%)
  Pallas kernels  22.3 us (16%)
  other arithmetic  3.67 us (3%)
  local copies, waits for them, and re-layouts  2.68 us (2%)
    ppermute x12, waiting for transfers between devices, along_col(): return lax.ppermute(value, AXES, pairs_of(pairs, rows))  31.5 us
    ppermute x9, starting transfers between devices, along_row(): lax.ppermute(value, AXES, [(a * COLS + c, b * COLS + c) for a, b in pairs...  28.4 us
    ppermute x12, starting transfers between devices, along_col(): return lax.ppermute(value, AXES, pairs_of(pairs, rows))  19.5 us
    ppermute x9, waiting for transfers between devices, along_row(): lax.ppermute(value, AXES, [(a * COLS + c, b * COLS + c) for a, b in pairs...  16.7 us
    pallas_call x2, Pallas kernels, update_raw(): pl.pallas_call(functools.partial(update_raw_kernel, blocks), grid=(group[...  8.96 us
    ppermute x1, waiting for transfers between devices, four(): lax.ppermute(jnp.where(end, last_own, lead_mid), AXES, pairs_of(MID_END,...  8.74 us
    pallas_call x2, Pallas kernels, solve(): pl.pallas_call(solve_kernel, out_shape=[part, part], in_specs=[SMEM] + [p...  7.36 us
    ppermute x1, starting transfers between devices, four(): lax.ppermute(jnp.where(end, last_own, lead_mid), AXES, pairs_of(MID_END,...  6.3 us
  transfers between devices with their start and end apart: 22, of which 11 were waited for; matrix products, arithmetic and copies ran while one was open for 3% of the time, Pallas kernels for 14%

profile of v6, /device:TPU:0, one launch (start us, length us, event | category | flops | bytes accessed | tf_op | source)
XLA Modules:
  0.0 140.3 jit_solution(1809920915767282263)
XLA Ops:
  0.0 1.3 fusion
  1.4 0.7 collective-permute-start
  2.1 0.7 collective-permute-start.1
  2.8 0.1 fusion.2
  3.0 5.7 %collective-permute-start.2 = (f32[256,512]{1,0:T(8,128)S(1)}, f32[256,512]{1,0:T(8,128)S(1)}, u32[]{:S(2)}, u32[]{:S(2)}) collective-permute-start(f32[256,512]{1,0:T(8,128)S(1)} %get-tuple-element.108), channel_id=1, source_target_pairs={{0,4},{1,5},{2,6},{3,7},{4,0},{5,1},{6,2},{7,3}} | collective-permute-start | bytes 1572872 | tf_op jit(solution)/shard_map/ppermute | solution.py:55
  8.7 1.0 slice-done.1
  9.7 0.2 slice-done.2
  10.0 0.2 collective-permute-done.2
  10.2 1.1 maximum_select_fusion
  11.3 3.4 %collective-permute-start.3 = (f32[512,512]{1,0:T(8,128)}, f32[512,512]{1,0:T(8,128)}, u32[]{:S(2)}, u32[]{:S(2)}) collective-permute-start(f32[512,512]{1,0:T(8,128)} %maximum_select_fusion), channel_id=1, source_target_pairs={{0,8},{1,9},{2,10},{3,11},{4,20},{5,21},{6,22},{7,23}} | collective-permute-start | bytes 3145736 | tf_op jit(solution)/shard_map/ppermute | solution.py:55
  14.7 0.1 stack.23
  14.9 4.4 %collective-permute-start.4 = (f32[1024,256]{1,0:T(8,128)S(1)}, f32[1024,256]{1,0:T(8,128)S(1)}, u32[]{:S(2)}, u32[]{:S(2)}) collective-permute-start(f32[1024,256]{1,0:T(8,128)S(1)} %pad_maximum_fusion.own), channel_id=1, source_target_pairs={{0,1},{3,2},{1,0},{2,3},{4,5},{7,6},{5,4},{6,7},{8,9},{11,10},{9,8... | collective-permute-start | bytes 3145736 | tf_op jit(solution)/shard_map/ppermute | solution.py:51
  19.3 0.7 collective-permute-start.5
  20.1 6.3 %collective-permute-done.3.refs_3_ = f32[512,512]{1,0:T(8,128)} collective-permute-done((f32[512,512]{1,0:T(8,128)}, f32[512,512]{1,0:T(8,128)}, u32[]{:S(2)}, u32[]{:S(2)}) %collective-permute-start.3) | collective-permute-done | bytes 1048608 | tf_op jit(solution)/shard_map/ppermute | solution.py:55
  26.4 1.4 %broadcast_select_fusion.1 = f32[512,512]{1,0:T(8,128)S(1)} fusion(f32[512,512]{1,0:T(8,128)} %get-tuple-element.58, f32[512,512]{1,0:T(8,128)} %maximum_select_fusion, pred[]{:T(512)S(6)} %or.16), kind=kLoop, calls=%fused_computation.8 | loop fusion | flops 262144 | bytes 3145729 | tf_op jit(solution)/shard_map/jit(_where)/select_n | solution.py:271
  27.8 1.4 collective-permute-start.6
  29.2 0.7 collective-permute-start.8
  30.0 6.3 %collective-permute-start.7 = (f32[512,256]{1,0:T(8,128)S(1)}, f32[512,256]{1,0:T(8,128)S(1)}, u32[]{:S(2)}, u32[]{:S(2)}) collective-permute-start(f32[512,256]{1,0:T(8,128)S(1)} %broadcast_select_fusion.4), channel_id=1, source_target_pairs={{5,4},{6,7},{9,8},{10,11},{13,12},{14,15},{17,16},{18,19},{21,20},... | collective-permute-start | bytes 1572872 | tf_op jit(solution)/shard_map/ppermute | solution.py:303
  36.3 7.1 %collective-permute-done.4.refs_1_ = f32[1024,256]{1,0:T(8,128)S(1)} collective-permute-done((f32[1024,256]{1,0:T(8,128)S(1)}, f32[1024,256]{1,0:T(8,128)S(1)}, u32[]{:S(2)}, u32[]{:S(2)}) %collective-permute-start.4) | collective-permute-done | bytes 1048608 | tf_op jit(solution)/shard_map/ppermute | solution.py:51
  43.4 8.7 %collective-permute-done.7.refs_1_ = f32[512,256]{1,0:T(8,128)S(1)} collective-permute-done((f32[512,256]{1,0:T(8,128)S(1)}, f32[512,256]{1,0:T(8,128)S(1)}, u32[]{:S(2)}, u32[]{:S(2)}) %collective-permute-start.7) | collective-permute-done | bytes 524320 | tf_op jit(solution)/shard_map/ppermute | solution.py:303
  52.2 0.8 collective-permute-start.9
  53.0 0.7 collective-permute-start.10
  53.8 0.2 broadcast_select_fusion.refs_0_
  54.0 5.9 %collective-permute-start.11 = (f32[512,512]{1,0:T(8,128)S(1)}, f32[512,512]{1,0:T(8,128)S(1)}, u32[]{:S(2)}, u32[]{:S(2)}) collective-permute-start(f32[512,512]{1,0:T(8,128)S(1)} %broadcast_select_fusion.refs_0_), channel_id=1, source_target_pairs={{0,1},{3,2},{4,5},{7,6},{8,9},{11,10},{12,13},{15,14},{16,17},{19,... | collective-permute-start | bytes 3145736 | tf_op jit(solution)/shard_map/ppermute | solution.py:51
  59.9 1.3 collective-permute-start.14
  61.2 0.3 shard_map.75
  61.7 1.3 collective-permute-start.12
  63.0 0.1 pad_maximum_fusion.2
  63.2 0.7 collective-permute-start.17
  63.9 1.6 %collective-permute-done.12 = f32[256,512]{1,0:T(8,128)S(1)} collective-permute-done((f32[256,512]{1,0:T(8,128)S(1)}, f32[256,512]{1,0:T(8,128)S(1)}, u32[]{:S(2)}, u32[]{:S(2)}) %collective-permute-start.12) | collective-permute-done | bytes 524320 | tf_op jit(solution)/shard_map/ppermute | solution.py:55
  65.6 10.6 %collective-permute-start.13 = (f32[256,512]{1,0:T(8,128)S(1)}, f32[256,512]{1,0:T(8,128)S(1)}, u32[]{:S(2)}, u32[]{:S(2)}) collective-permute-start(f32[256,512]{1,0:T(8,128)S(1)} %slice_select_fusion), channel_id=1, source_target_pairs={{0,8},{1,9},{2,10},{3,11},{4,20},{5,21},{6,22},{7,23}} | collective-permute-start | bytes 1572872 | tf_op jit(solution)/shard_map/ppermute | solution.py:55
  76.3 4.9 %collective-permute-done.11.refs_2_ = f32[512,512]{1,0:T(8,128)S(1)} collective-permute-done((f32[512,512]{1,0:T(8,128)S(1)}, f32[512,512]{1,0:T(8,128)S(1)}, u32[]{:S(2)}, u32[]{:S(2)}) %collective-permute-start.11) | collective-permute-done | bytes 1048608 | tf_op jit(solution)/shard_map/ppermute | solution.py:51
  81.1 1.8 %collective-permute-done.13.refs_3_ = f32[256,512]{1,0:T(8,128)S(1)} collective-permute-done((f32[256,512]{1,0:T(8,128)S(1)}, f32[256,512]{1,0:T(8,128)S(1)}, u32[]{:S(2)}, u32[]{:S(2)}) %collective-permute-start.13) | collective-permute-done | bytes 524320 | tf_op jit(solution)/shard_map/ppermute | solution.py:55
  83.0 5.5 %collective-permute-start.15 = (f32[256,512]{1,0:T(8,128)S(1)}, f32[256,512]{1,0:T(8,128)S(1)}, u32[]{:S(2)}, u32[]{:S(2)}) collective-permute-start(f32[256,512]{1,0:T(8,128)S(1)} %broadcast_select_fusion.3), channel_id=1, source_target_pairs={{8,24},{9,25},{10,26},{11,27},{20,28},{21,29},{22,30},{23,31},{0,1... | collective-permute-start | bytes 1572872 | tf_op jit(solution)/shard_map/ppermute | solution.py:55
  88.5 1.3 collective-permute-start.21
  89.8 5.3 %collective-permute-done.15.refs_2_ = f32[256,512]{1,0:T(8,128)S(1)} collective-permute-done((f32[256,512]{1,0:T(8,128)S(1)}, f32[256,512]{1,0:T(8,128)S(1)}, u32[]{:S(2)}, u32[]{:S(2)}) %collective-permute-start.15) | collective-permute-done | bytes 524320 | tf_op jit(solution)/shard_map/ppermute | solution.py:55
  95.3 0.5 collective-permute-start.20
  95.8 1.4 collective-permute-done.18.refs_3_
  97.2 3.7 %shard_map.76 = (bf16[1024,512]{1,0:T(8,128)(2,1)S(1)}, bf16[1024,512]{1,0:T(8,128)(2,1)S(1)}) custom-call(s32[5]{0:T(128)S(1)} %convert_element_type.3.place, f32[512,512]{1,0:T(8,128)S(1)} %get-tuple-element.73.refs_0_, f32[512,512]{1,0:T(8,128)S(1)} %get-tuple-element.78.refs_1_, f32[256,512]{1,0:T(8,128)S(1)} %broadcast_select_fusion.2.refs_2_, ...), custom_call_target="tpu_custom_call" | custom-call | flops 3000000000 | tf_op jit(solution)/shard_map/pallas_call | solution.py:123
  100.9 2.0 %shard_map.78 = f32[512,512]{1,0:T(8,128)S(1)} custom-call(f32[512,256]{1,0:T(8,128)S(1)} %get-tuple-element.77.near_end.c, f32[512,256]{1,0:T(8,128)S(1)} %get-tuple-element.76.own, f32[512,512]{1,0:T(8,128)S(1)} %get-tuple-element.88.both, bf16[1024,512]{1,0:T(8,128)(2,1)S(1)} %get-tuple-element.89.high, bf16[1024,512]{1,0:T(8,128)(2,1)S(1)} %get-tuple-element.90.low), custom_call_target="tpu_custom_call" | custom-call | flops 2000000000 | tf_op jit(solution)/shard_map/pallas_call | solution.py:139
  102.9 1.5 %collective-permute-start.19 = (f32[512,512]{1,0:T(8,128)S(1)}, f32[512,512]{1,0:T(8,128)S(1)}, u32[]{:S(2)}, u32[]{:S(2)}) collective-permute-start(f32[512,512]{1,0:T(8,128)S(1)} %shard_map.78), channel_id=1, source_target_pairs={{1,0},{2,3},{5,4},{6,7},{9,8},{10,11},{13,12},{14,15},{17,16},{18,... | collective-permute-start | bytes 3145736 | tf_op jit(solution)/shard_map/ppermute | solution.py:51
  104.5 3.7 %shard_map.79 = (bf16[1024,512]{1,0:T(8,128)(2,1)S(1)}, bf16[1024,512]{1,0:T(8,128)(2,1)S(1)}) custom-call(s32[5]{0:T(128)S(1)} %convert_element_type.3.place, f32[512,512]{1,0:T(8,128)S(1)} %broadcast_select_fusion.refs_0_, f32[512,512]{1,0:T(8,128)S(1)} %collective-permute-done.20.refs_1_, f32[256,512]{1,0:T(8,128)S(1)} %broadcast_select_fusion.2.refs_2_, ...), custom_call_target="tpu_custom_call" | custom-call | flops 3000000000 | tf_op jit(solution)/shard_map/pallas_call | solution.py:123
  108.2 3.5 %shard_map.82.refs_2_ = f32[2048,512]{1,0:T(8,128)} custom-call(s32[5]{0:T(128)S(1)} %convert_element_type.3.place, f32[2048,512]{1,0:T(8,128)S(1)} %copy-done, bf16[1024,512]{1,0:T(8,128)(2,1)S(1)} %get-tuple-element.94.high, bf16[1024,512]{1,0:T(8,128)(2,1)S(1)} %get-tuple-element.95.low, f32[512,256]{1,0:T(8,128)S(1)} %pad_maximum_fusion.3.own, ...), custom_call_target="tpu_custom_call" | custom-call | flops 3000000000 | tf_op jit(solution)/shard_map/pallas_call | solution.py:172
  111.7 4.7 %collective-permute-done.21.refs_1_ = f32[1024,256]{1,0:T(8,128)S(1)} collective-permute-done((f32[1024,256]{1,0:T(8,128)S(1)}, f32[1024,256]{1,0:T(8,128)S(1)}, u32[]{:S(2)}, u32[]{:S(2)}) %collective-permute-start.21) | collective-permute-done | bytes 1048608 | tf_op jit(solution)/shard_map/ppermute | solution.py:51
  116.4 5.4 %shard_map.84.kept = f32[2048,512]{1,0:T(8,128)} custom-call(s32[5]{0:T(128)S(1)} %convert_element_type.3.place, f32[2048,512]{1,0:T(8,128)S(1)} %copy-done, bf16[1024,512]{1,0:T(8,128)(2,1)S(1)} %get-tuple-element.94.high, bf16[1024,512]{1,0:T(8,128)(2,1)S(1)} %get-tuple-element.95.low, ...), custom_call_target="tpu_custom_call", output_to_operand_aliasing={{}: (10, {})} | custom-call | flops 3000000000 | tf_op jit(solution)/shard_map/pallas_call | solution.py:172
  121.8 1.5 %shard_map.85.kept = f32[2048,512]{1,0:T(8,128)} custom-call(s32[5]{0:T(128)S(1)} %convert_element_type.3.place, f32[2048,512]{1,0:T(8,128)S(1)} %copy-done, f32[512,256]{1,0:T(8,128)S(1)} %get-tuple-element.77.near_end.c, f32[512,256]{1,0:T(8,128)S(1)} %get-tuple-element.76.own, ...), custom_call_target="tpu_custom_call", output_to_operand_aliasing={{}: (7, {})} | custom-call | flops 2000000000 | tf_op jit(solution)/shard_map/pallas_call | solution.py:202
  123.3 14.9 %collective-permute-done.19.returned = f32[512,512]{1,0:T(8,128)S(1)} collective-permute-done((f32[512,512]{1,0:T(8,128)S(1)}, f32[512,512]{1,0:T(8,128)S(1)}, u32[]{:S(2)}, u32[]{:S(2)}) %collective-permute-start.19) | collective-permute-done | bytes 1048608 | tf_op jit(solution)/shard_map/ppermute | solution.py:51
  138.2 2.1 %shard_map.86 = f32[2048,512]{1,0:T(8,128)} custom-call(s32[5]{0:T(128)S(1)} %convert_element_type.3.place, f32[2048,512]{1,0:T(8,128)S(1)} %copy-done, f32[512,512]{1,0:T(8,128)S(1)} %collective-permute-done.19.returned, f32[2048,512]{1,0:T(8,128)} %shard_map.85.kept), custom_call_target="tpu_custom_call", output_to_operand_aliasing={{}: (3, {})} | custom-call | flops 1000000000 | tf_op jit(solution)/shard_map/pallas_call | solution.py:202
  (61 shorter events, 0.8 us)
Async XLA Ops:
  0.0 2.8 %slice-start = ((f32[2048,512]{1,0:T(8,128)}), f32[512,512]{1,0:T(8,128)S(1)}, s32[]{:S(2)}) async-start(f32[2048,512]{1,0:T(8,128)} %top.7), calls=%async_computation | async-start | bytes 2097152 | tf_op jit(solution)/shard_map/slice | solution.py:283
  1.4 18.6 %collective-permute-start = (f32[512,256]{1,0:T(8,128)S(1)}, f32[512,256]{1,0:T(8,128)S(1)}, u32[]{:S(2)}, u32[]{:S(2)}) collective-permute-start(f32[512,256]{1,0:T(8,128)S(1)} %pad_maximum_fusion.3.own), channel_id=1, source_target_pairs={{4,5},{7,6},{5,4},{6,7},{8,9},{11,10},{9,8},{10,11},{12,13},{15,14... | collective-permute-start | bytes 1572872 | tf_op jit(solution)/shard_map/ppermute | solution.py:51
  2.1 18.0 %collective-permute-start.1 = (f32[512,256]{1,0:T(8,128)S(1)}, f32[512,256]{1,0:T(8,128)S(1)}, u32[]{:S(2)}, u32[]{:S(2)}) collective-permute-start(f32[512,256]{1,0:T(8,128)S(1)} %pad_maximum_fusion.3.own), channel_id=1, source_target_pairs={{5,6},{6,5},{9,10},{10,9},{13,14},{14,13},{17,18},{18,17},{21,22},... | collective-permute-start | bytes 1572872 | tf_op jit(solution)/shard_map/ppermute | solution.py:51
  3.0 7.2 %collective-permute-start.2 = (f32[256,512]{1,0:T(8,128)S(1)}, f32[256,512]{1,0:T(8,128)S(1)}, u32[]{:S(2)}, u32[]{:S(2)}) collective-permute-start(f32[256,512]{1,0:T(8,128)S(1)} %get-tuple-element.108), channel_id=1, source_target_pairs={{0,4},{1,5},{2,6},{3,7},{4,0},{5,1},{6,2},{7,3}} | collective-permute-start | bytes 1572872 | tf_op jit(solution)/shard_map/ppermute | solution.py:55
  8.7 1.0 slice-start.1
  8.7 1.2 slice-start.2
  11.3 15.0 %collective-permute-start.3 = (f32[512,512]{1,0:T(8,128)}, f32[512,512]{1,0:T(8,128)}, u32[]{:S(2)}, u32[]{:S(2)}) collective-permute-start(f32[512,512]{1,0:T(8,128)} %maximum_select_fusion), channel_id=1, source_target_pairs={{0,8},{1,9},{2,10},{3,11},{4,20},{5,21},{6,22},{7,23}} | collective-permute-start | bytes 3145736 | tf_op jit(solution)/shard_map/ppermute | solution.py:55
  14.9 28.5 %collective-permute-start.4 = (f32[1024,256]{1,0:T(8,128)S(1)}, f32[1024,256]{1,0:T(8,128)S(1)}, u32[]{:S(2)}, u32[]{:S(2)}) collective-permute-start(f32[1024,256]{1,0:T(8,128)S(1)} %pad_maximum_fusion.own), channel_id=1, source_target_pairs={{0,1},{3,2},{1,0},{2,3},{4,5},{7,6},{5,4},{6,7},{8,9},{11,10},{9,8... | collective-permute-start | bytes 3145736 | tf_op jit(solution)/shard_map/ppermute | solution.py:51
  19.3 24.1 %collective-permute-start.5 = (f32[1024,256]{1,0:T(8,128)S(1)}, f32[1024,256]{1,0:T(8,128)S(1)}, u32[]{:S(2)}, u32[]{:S(2)}) collective-permute-start(f32[1024,256]{1,0:T(8,128)S(1)} %pad_maximum_fusion.own), channel_id=1, source_target_pairs={{1,2},{2,1},{5,6},{6,5},{9,10},{10,9},{13,14},{14,13},{17,18},{18,... | collective-permute-start | bytes 3145736 | tf_op jit(solution)/shard_map/ppermute | solution.py:51
  27.8 15.6 %collective-permute-start.6 = (f32[512,512]{1,0:T(8,128)S(1)}, f32[512,512]{1,0:T(8,128)S(1)}, u32[]{:S(2)}, u32[]{:S(2)}) collective-permute-start(f32[512,512]{1,0:T(8,128)S(1)} %broadcast_select_fusion.1), channel_id=1, source_target_pairs={{8,24},{9,25},{10,26},{11,27},{20,28},{21,29},{22,30},{23,31},{0,1... | collective-permute-start | bytes 3145736 | tf_op jit(solution)/shard_map/ppermute | solution.py:55
  29.2 23.0 %collective-permute-start.8 = (f32[512,256]{1,0:T(8,128)S(1)}, f32[512,256]{1,0:T(8,128)S(1)}, u32[]{:S(2)}, u32[]{:S(2)}) collective-permute-start(f32[512,256]{1,0:T(8,128)S(1)} %get-tuple-element.62.swap), channel_id=1, source_target_pairs={{5,6},{6,5},{9,10},{10,9},{13,14},{14,13},{17,18},{18,17},{21,22},... | collective-permute-start | bytes 1572872 | tf_op jit(solution)/shard_map/ppermute | solution.py:51
  30.0 22.2 %collective-permute-start.7 = (f32[512,256]{1,0:T(8,128)S(1)}, f32[512,256]{1,0:T(8,128)S(1)}, u32[]{:S(2)}, u32[]{:S(2)}) collective-permute-start(f32[512,256]{1,0:T(8,128)S(1)} %broadcast_select_fusion.4), channel_id=1, source_target_pairs={{5,4},{6,7},{9,8},{10,11},{13,12},{14,15},{17,16},{18,19},{21,20},... | collective-permute-start | bytes 1572872 | tf_op jit(solution)/shard_map/ppermute | solution.py:303
  52.2 9.0 %copy-start.1 = (f32[512,512]{1,0:T(8,128)S(1)}, f32[512,512]{1,0:T(8,128)}, u32[]{:S(2)}) copy-start(f32[512,512]{1,0:T(8,128)} %one) | copy-start | bytes 3145732
  52.2 9.1 %copy-start.2 = (f32[512,512]{1,0:T(8,128)S(1)}, f32[512,512]{1,0:T(8,128)}, u32[]{:S(2)}) copy-start(f32[512,512]{1,0:T(8,128)} %two) | copy-start | bytes 3145732
  52.2 9.4 %collective-permute-start.9 = (f32[512,256]{1,0:T(8,128)S(1)}, f32[512,256]{1,0:T(8,128)S(1)}, u32[]{:S(2)}, u32[]{:S(2)}) collective-permute-start(f32[512,256]{1,0:T(8,128)S(1)} %get-tuple-element.66.far), channel_id=1, source_target_pairs={{5,4},{6,7},{9,8},{10,11},{13,12},{14,15},{17,16},{18,19},{21,20},... | collective-permute-start | bytes 1572872 | tf_op jit(solution)/shard_map/ppermute | solution.py:51
  53.0 23.3 %collective-permute-start.10 = (f32[1024,256]{1,0:T(8,128)S(1)}, f32[1024,256]{1,0:T(8,128)S(1)}, u32[]{:S(2)}, u32[]{:S(2)}) collective-permute-start(f32[1024,256]{1,0:T(8,128)S(1)} %get-tuple-element.68.swap), channel_id=1, source_target_pairs={{1,2},{2,1},{5,6},{6,5},{9,10},{10,9},{13,14},{14,13},{17,18},{18,... | collective-permute-start | bytes 3145736 | tf_op jit(solution)/shard_map/ppermute | solution.py:51
  54.0 27.2 %collective-permute-start.11 = (f32[512,512]{1,0:T(8,128)S(1)}, f32[512,512]{1,0:T(8,128)S(1)}, u32[]{:S(2)}, u32[]{:S(2)}) collective-permute-start(f32[512,512]{1,0:T(8,128)S(1)} %broadcast_select_fusion.refs_0_), channel_id=1, source_target_pairs={{0,1},{3,2},{4,5},{7,6},{8,9},{11,10},{12,13},{15,14},{16,17},{19,... | collective-permute-start | bytes 3145736 | tf_op jit(solution)/shard_map/ppermute | solution.py:51
  59.9 29.9 %collective-permute-start.14 = (f32[1024,256]{1,0:T(8,128)S(1)}, f32[1024,256]{1,0:T(8,128)S(1)}, u32[]{:S(2)}, u32[]{:S(2)}) collective-permute-start(f32[1024,256]{1,0:T(8,128)S(1)} %get-tuple-element.71.mid), channel_id=1, source_target_pairs={{1,0},{2,3},{5,4},{6,7},{9,8},{10,11},{13,12},{14,15},{17,16},{18,... | collective-permute-start | bytes 3145736 | tf_op jit(solution)/shard_map/ppermute | solution.py:51
  61.7 3.8 %collective-permute-start.12 = (f32[256,512]{1,0:T(8,128)S(1)}, f32[256,512]{1,0:T(8,128)S(1)}, u32[]{:S(2)}, u32[]{:S(2)}) collective-permute-start(f32[256,512]{1,0:T(8,128)S(1)} %slice.70), channel_id=1, source_target_pairs={{4,0},{5,1},{6,2},{7,3}} | collective-permute-start | bytes 1572872 | tf_op jit(solution)/shard_map/ppermute | solution.py:55
  63.2 37.7 %collective-permute-start.17 = (f32[512,512]{1,0:T(8,128)S(1)}, f32[512,512]{1,0:T(8,128)S(1)}, u32[]{:S(2)}, u32[]{:S(2)}) collective-permute-start(f32[512,512]{1,0:T(8,128)S(1)} %pad_maximum_fusion.2), channel_id=1, source_target_pairs={{1,2},{2,1},{5,6},{6,5},{9,10},{10,9},{13,14},{14,13},{17,18},{18,... | collective-permute-start | bytes 3145736 | tf_op jit(solution)/shard_map/ppermute | solution.py:51
  65.6 17.3 %collective-permute-start.13 = (f32[256,512]{1,0:T(8,128)S(1)}, f32[256,512]{1,0:T(8,128)S(1)}, u32[]{:S(2)}, u32[]{:S(2)}) collective-permute-start(f32[256,512]{1,0:T(8,128)S(1)} %slice_select_fusion), channel_id=1, source_target_pairs={{0,8},{1,9},{2,10},{3,11},{4,20},{5,21},{6,22},{7,23}} | collective-permute-start | bytes 1572872 | tf_op jit(solution)/shard_map/ppermute | solution.py:55
  82.9 12.2 %collective-permute-start.16 = (f32[512,512]{1,0:T(8,128)S(1)}, f32[512,512]{1,0:T(8,128)S(1)}, u32[]{:S(2)}, u32[]{:S(2)}) collective-permute-start(f32[512,512]{1,0:T(8,128)S(1)} %get-tuple-element.73.refs_0_), channel_id=1, source_target_pairs={{0,4},{1,5},{2,6},{3,7},{4,0},{5,1},{6,2},{7,3},{8,12},{9,13},{10,... | collective-permute-start | bytes 3145736 | tf_op jit(solution)/shard_map/ppermute | solution.py:55
  83.0 12.1 %collective-permute-start.15 = (f32[256,512]{1,0:T(8,128)S(1)}, f32[256,512]{1,0:T(8,128)S(1)}, u32[]{:S(2)}, u32[]{:S(2)}) collective-permute-start(f32[256,512]{1,0:T(8,128)S(1)} %broadcast_select_fusion.3), channel_id=1, source_target_pairs={{8,24},{9,25},{10,26},{11,27},{20,28},{21,29},{22,30},{23,31},{0,1... | collective-permute-start | bytes 1572872 | tf_op jit(solution)/shard_map/ppermute | solution.py:55
  88.5 27.9 %collective-permute-start.21 = (f32[1024,256]{1,0:T(8,128)S(1)}, f32[1024,256]{1,0:T(8,128)S(1)}, u32[]{:S(2)}, u32[]{:S(2)}) collective-permute-start(f32[1024,256]{1,0:T(8,128)S(1)} %get-tuple-element.96.far), channel_id=1, source_target_pairs={{1,0},{2,3},{5,4},{6,7},{9,8},{10,11},{13,12},{14,15},{17,16},{18,... | collective-permute-start | bytes 3145736 | tf_op jit(solution)/shard_map/ppermute | solution.py:51
  95.2 2.0 %collective-permute-start.18 = (f32[256,512]{1,0:T(8,128)S(1)}, f32[256,512]{1,0:T(8,128)S(1)}, u32[]{:S(2)}, u32[]{:S(2)}) collective-permute-start(f32[256,512]{1,0:T(8,128)S(1)} %broadcast_select_fusion.2.refs_2_), channel_id=1, source_target_pairs={{0,4},{1,5},{2,6},{3,7},{4,0},{5,1},{6,2},{7,3},{8,12},{9,13},{10,... | collective-permute-start | bytes 1572872 | tf_op jit(solution)/shard_map/ppermute | solution.py:55
  95.3 9.2 %collective-permute-start.20 = (f32[512,512]{1,0:T(8,128)S(1)}, f32[512,512]{1,0:T(8,128)S(1)}, u32[]{:S(2)}, u32[]{:S(2)}) collective-permute-start(f32[512,512]{1,0:T(8,128)S(1)} %broadcast_select_fusion.refs_0_), channel_id=1, source_target_pairs={{0,4},{1,5},{2,6},{3,7},{4,0},{5,1},{6,2},{7,3},{8,12},{9,13},{10,... | collective-permute-start | bytes 3145736 | tf_op jit(solution)/shard_map/ppermute | solution.py:55
  102.9 35.3 %collective-permute-start.19 = (f32[512,512]{1,0:T(8,128)S(1)}, f32[512,512]{1,0:T(8,128)S(1)}, u32[]{:S(2)}, u32[]{:S(2)}) collective-permute-start(f32[512,512]{1,0:T(8,128)S(1)} %shard_map.78), channel_id=1, source_target_pairs={{1,0},{2,3},{5,4},{6,7},{9,8},{10,11},{13,12},{14,15},{17,16},{18,... | collective-permute-start | bytes 3145736 | tf_op jit(solution)/shard_map/ppermute | solution.py:51
  104.4 3.7 %copy-start = (f32[2048,512]{1,0:T(8,128)S(1)}, f32[2048,512]{1,0:T(8,128)}, u32[]{:S(2)}) copy-start(f32[2048,512]{1,0:T(8,128)} %top.7) | copy-start | bytes 12582916

commit v7 on v6

--- a/solution.py
+++ b/solution.py
@@ -129,20 +129,18 @@
     )(place, *tops, *corners, *inverses)
 
 
-def multiply_kernel(near_end, own, both, high, low, out):
+def multiply_kernel(near_end, own, both, high, low, *outs):
     panels = jnp.concatenate([near_end[...], own[...], both[...]], axis=1)
-    out[...] = three_pass(split(panels), (high[...], low[...]))
+    value = three_pass(split(panels), (high[...], low[...]))
+    for i, out in enumerate(outs):
+        out[...] = value[i * TILE : (i + 1) * TILE]
 
 
 def multiply(panels, solved):
     rows, width = panels[0].shape[0], solved[0].shape[1]
     return pl.pallas_call(
         multiply_kernel,
-        grid=(rows // TILE,),
-        out_shape=jax.ShapeDtypeStruct((rows, width), jnp.float32),
-        in_specs=[pl.BlockSpec((TILE, v.shape[1]), lambda i: (i, 0)) for v in panels]
-        + [pl.BlockSpec(v.shape, lambda i: (0, 0)) for v in solved],
-        out_specs=pl.BlockSpec((TILE, width), lambda i: (i, 0)),
+        out_shape=[jax.ShapeDtypeStruct((TILE, width), jnp.float32)] * (rows // TILE),
         compiler_params=pltpu.CompilerParams(vmem_limit_bytes=VMEM_BYTES),
         cost_estimate=pl.CostEstimate(flops=2 * 10**9, bytes_accessed=0, transcendentals=0),
     )(*panels, *solved)
@@ -195,9 +193,9 @@
     out[...] = jnp.where(place[2] == 1, top[...] - returned[...], kept[...])
 
 
-def last_call(body, place, top, parts, fixed, out, block_of_out, flops):
+def last_call(body, place, top, parts, fixed, out, block_of_out, flops, past):
     width, count = top.shape[1], parts[0].shape[0] // TILE
-    first = top.shape[0] // TILE - count
+    first = past // TILE - count
     tile = pl.BlockSpec((TILE, width), lambda i: (first + i, 0))
     return pl.pallas_call(
         body,
@@ -215,11 +213,11 @@
 
 
 def update_last(place, top, last, solved, out):
-    return last_call(update_last_kernel, place, top, last, solved, out, False, 2 * 10**9)
-
-
-def finish(place, top, returned, out):
-    return last_call(finish_kernel, place, top, (returned,), (), out, True, 10**9)
+    return last_call(update_last_kernel, place, top, last, solved, out, False, 2 * 10**9, top.shape[0])
+
+
+def finish(place, top, returned, out, past):
+    return last_call(finish_kernel, place, top, (returned,), (), out, True, 10**9, past)
 
 
 def nothing(*refs):
@@ -340,7 +338,7 @@
 
     last = (crossed, last_own, last_both)
     sent = multiply(last, solved_end)
-    returned = along_col(sent, MID_END, every)
+    returned = [along_col(value, MID_END, every) for value in sent]
     sent, mine, other = tied((sent, mine, other))
 
     solved = solve(place, (mine, other), corner, inverses)
@@ -351,7 +349,10 @@
     rest = (rest_own, rest_swap, rest_mid, rest_far, rest_c, rest_cc)
     out = update_raw(place, test_kernel, solved, rest, block, False, out)
     out = update_last(place, test_kernel, last, solved, out)
-    return finish(place, test_kernel, returned, out)
+    for i, value in enumerate(returned):
+        out, value = tied((out, value))
+        out = finish(place, test_kernel, value, out, raw + (i + 1) * TILE)
+    return out
 
 
 def solution(mesh):

time: 141 us -> 141 us (level)
  waiting for transfers between devices: 57 us -> 54 us
  Pallas kernels: 22.3 us -> 23.8 us
    ppermute x12 -> x13, waiting for transfers between devices: 31.5 us -> 28.6 us  [along_col(): return lax.ppermute(value, AXES, pairs_of(pairs, rows))]
    pallas_call x2 -> x3, Pallas kernels: 3.61 us -> 5.35 us  [last_call(): pl.pallas_call(body, grid=(count,), out_shape=jax.ShapeDtypeStruct(top.sh...]
    ppermute x12 -> x13, starting transfers between devices: 19.5 us -> 20.8 us  [along_col(): return lax.ppermute(value, AXES, pairs_of(pairs, rows))]
  transfers between devices with their start and end apart: 22 -> 23, of which waited for: 11 -> 12; matrix products, arithmetic and copies ran while one was open for 3% -> 3% of each run, Pallas kernels for 14% -> 16%
where the time goes in v7:
time: 141 us; the launch traced here: 140 us
  starting transfers between devices  55.5 us (39%)
  waiting for transfers between devices  54 us (38%)
  Pallas kernels  23.8 us (17%)
  other arithmetic  3.67 us (3%)
  local copies, waits for them, and re-layouts  2.68 us (2%)
    ppermute x13, waiting for transfers between devices, along_col(): return lax.ppermute(value, AXES, pairs_of(pairs, rows))  28.6 us
    ppermute x9, starting transfers between devices, along_row(): lax.ppermute(value, AXES, [(a * COLS + c, b * COLS + c) for a, b in pairs...  28.4 us
    ppermute x13, starting transfers between devices, along_col(): return lax.ppermute(value, AXES, pairs_of(pairs, rows))  20.8 us
    ppermute x9, waiting for transfers between devices, along_row(): lax.ppermute(value, AXES, [(a * COLS + c, b * COLS + c) for a, b in pairs...  16.6 us
    pallas_call x2, Pallas kernels, update_raw(): pl.pallas_call(functools.partial(update_raw_kernel, blocks), grid=(group[...  8.96 us
    ppermute x1, waiting for transfers between devices, four(): lax.ppermute(jnp.where(end, last_own, lead_mid), AXES, pairs_of(MID_END,...  8.74 us
    pallas_call x2, Pallas kernels, solve(): pl.pallas_call(solve_kernel, out_shape=[part, part], in_specs=[SMEM] + [p...  7.36 us
    ppermute x1, starting transfers between devices, four(): lax.ppermute(jnp.where(end, last_own, lead_mid), AXES, pairs_of(MID_END,...  6.3 us
  transfers between devices with their start and end apart: 23, of which 12 were waited for; matrix products, arithmetic and copies ran while one was open for 3% of the time, Pallas kernels for 16%

profile of v7, /device:TPU:0, one launch (start us, length us, event | category | flops | bytes accessed | tf_op | source)
XLA Modules:
  0.0 140.1 jit_solution(12302483373933709615)
XLA Ops:
  0.0 1.3 fusion
  1.4 0.7 collective-permute-start
  2.1 0.7 collective-permute-start.1
  3.0 5.7 %collective-permute-start.2 = (f32[256,512]{1,0:T(8,128)S(1)}, f32[256,512]{1,0:T(8,128)S(1)}, u32[]{:S(2)}, u32[]{:S(2)}) collective-permute-start(f32[256,512]{1,0:T(8,128)S(1)} %get-tuple-element.120), channel_id=1, source_target_pairs={{0,4},{1,5},{2,6},{3,7},{4,0},{5,1},{6,2},{7,3}} | collective-permute-start | bytes 1572872 | tf_op jit(solution)/shard_map/ppermute | solution.py:55
  8.7 1.0 slice-done.1
  9.7 0.2 slice-done.2
  10.0 0.2 collective-permute-done.2
  10.2 1.1 maximum_select_fusion
  11.3 3.4 %collective-permute-start.3 = (f32[512,512]{1,0:T(8,128)}, f32[512,512]{1,0:T(8,128)}, u32[]{:S(2)}, u32[]{:S(2)}) collective-permute-start(f32[512,512]{1,0:T(8,128)} %maximum_select_fusion), channel_id=1, source_target_pairs={{0,8},{1,9},{2,10},{3,11},{4,20},{5,21},{6,22},{7,23}} | collective-permute-start | bytes 3145736 | tf_op jit(solution)/shard_map/ppermute | solution.py:55
  14.9 4.4 %collective-permute-start.4 = (f32[1024,256]{1,0:T(8,128)S(1)}, f32[1024,256]{1,0:T(8,128)S(1)}, u32[]{:S(2)}, u32[]{:S(2)}) collective-permute-start(f32[1024,256]{1,0:T(8,128)S(1)} %pad_maximum_fusion.own), channel_id=1, source_target_pairs={{0,1},{3,2},{1,0},{2,3},{4,5},{7,6},{5,4},{6,7},{8,9},{11,10},{9,8... | collective-permute-start | bytes 3145736 | tf_op jit(solution)/shard_map/ppermute | solution.py:51
  19.3 0.7 collective-permute-start.5
  20.1 6.3 %collective-permute-done.3.refs_3_ = f32[512,512]{1,0:T(8,128)} collective-permute-done((f32[512,512]{1,0:T(8,128)}, f32[512,512]{1,0:T(8,128)}, u32[]{:S(2)}, u32[]{:S(2)}) %collective-permute-start.3) | collective-permute-done | bytes 1048608 | tf_op jit(solution)/shard_map/ppermute | solution.py:55
  26.4 1.4 %broadcast_select_fusion.1 = f32[512,512]{1,0:T(8,128)S(1)} fusion(f32[512,512]{1,0:T(8,128)} %get-tuple-element.64, f32[512,512]{1,0:T(8,128)} %maximum_select_fusion, pred[]{:T(512)S(6)} %or.16), kind=kLoop, calls=%fused_computation.8 | loop fusion | flops 262144 | bytes 3145729 | tf_op jit(solution)/shard_map/jit(_where)/select_n | solution.py:269
  27.8 1.4 collective-permute-start.6
  29.2 0.7 collective-permute-start.8
  30.0 6.3 %collective-permute-start.7 = (f32[512,256]{1,0:T(8,128)S(1)}, f32[512,256]{1,0:T(8,128)S(1)}, u32[]{:S(2)}, u32[]{:S(2)}) collective-permute-start(f32[512,256]{1,0:T(8,128)S(1)} %broadcast_select_fusion.4), channel_id=1, source_target_pairs={{5,4},{6,7},{9,8},{10,11},{13,12},{14,15},{17,16},{18,19},{21,20},... | collective-permute-start | bytes 1572872 | tf_op jit(solution)/shard_map/ppermute | solution.py:301
  36.3 7.1 %collective-permute-done.4.refs_1_ = f32[1024,256]{1,0:T(8,128)S(1)} collective-permute-done((f32[1024,256]{1,0:T(8,128)S(1)}, f32[1024,256]{1,0:T(8,128)S(1)}, u32[]{:S(2)}, u32[]{:S(2)}) %collective-permute-start.4) | collective-permute-done | bytes 1048608 | tf_op jit(solution)/shard_map/ppermute | solution.py:51
  43.4 8.7 %collective-permute-done.7.refs_1_ = f32[512,256]{1,0:T(8,128)S(1)} collective-permute-done((f32[512,256]{1,0:T(8,128)S(1)}, f32[512,256]{1,0:T(8,128)S(1)}, u32[]{:S(2)}, u32[]{:S(2)}) %collective-permute-start.7) | collective-permute-done | bytes 524320 | tf_op jit(solution)/shard_map/ppermute | solution.py:301
  52.2 0.8 collective-permute-start.9
  53.0 0.7 collective-permute-start.10
  53.8 0.2 broadcast_select_fusion.refs_0_
  54.0 5.9 %collective-permute-start.11 = (f32[512,512]{1,0:T(8,128)S(1)}, f32[512,512]{1,0:T(8,128)S(1)}, u32[]{:S(2)}, u32[]{:S(2)}) collective-permute-start(f32[512,512]{1,0:T(8,128)S(1)} %broadcast_select_fusion.refs_0_), channel_id=1, source_target_pairs={{0,1},{3,2},{4,5},{7,6},{8,9},{11,10},{12,13},{15,14},{16,17},{19,... | collective-permute-start | bytes 3145736 | tf_op jit(solution)/shard_map/ppermute | solution.py:51
  59.9 1.3 collective-permute-start.14
  61.3 0.3 shard_map.75
  61.8 1.3 collective-permute-start.12
  63.2 0.7 collective-permute-start.17
  63.9 1.6 %collective-permute-done.12 = f32[256,512]{1,0:T(8,128)S(1)} collective-permute-done((f32[256,512]{1,0:T(8,128)S(1)}, f32[256,512]{1,0:T(8,128)S(1)}, u32[]{:S(2)}, u32[]{:S(2)}) %collective-permute-start.12) | collective-permute-done | bytes 524320 | tf_op jit(solution)/shard_map/ppermute | solution.py:55
  65.7 10.6 %collective-permute-start.13 = (f32[256,512]{1,0:T(8,128)S(1)}, f32[256,512]{1,0:T(8,128)S(1)}, u32[]{:S(2)}, u32[]{:S(2)}) collective-permute-start(f32[256,512]{1,0:T(8,128)S(1)} %slice_select_fusion), channel_id=1, source_target_pairs={{0,8},{1,9},{2,10},{3,11},{4,20},{5,21},{6,22},{7,23}} | collective-permute-start | bytes 1572872 | tf_op jit(solution)/shard_map/ppermute | solution.py:55
  76.3 4.9 %collective-permute-done.11.refs_2_ = f32[512,512]{1,0:T(8,128)S(1)} collective-permute-done((f32[512,512]{1,0:T(8,128)S(1)}, f32[512,512]{1,0:T(8,128)S(1)}, u32[]{:S(2)}, u32[]{:S(2)}) %collective-permute-start.11) | collective-permute-done | bytes 1048608 | tf_op jit(solution)/shard_map/ppermute | solution.py:51
  81.2 1.8 %collective-permute-done.13.refs_3_ = f32[256,512]{1,0:T(8,128)S(1)} collective-permute-done((f32[256,512]{1,0:T(8,128)S(1)}, f32[256,512]{1,0:T(8,128)S(1)}, u32[]{:S(2)}, u32[]{:S(2)}) %collective-permute-start.13) | collective-permute-done | bytes 524320 | tf_op jit(solution)/shard_map/ppermute | solution.py:55
  83.0 5.5 %collective-permute-start.15 = (f32[256,512]{1,0:T(8,128)S(1)}, f32[256,512]{1,0:T(8,128)S(1)}, u32[]{:S(2)}, u32[]{:S(2)}) collective-permute-start(f32[256,512]{1,0:T(8,128)S(1)} %broadcast_select_fusion.3), channel_id=1, source_target_pairs={{8,24},{9,25},{10,26},{11,27},{20,28},{21,29},{22,30},{23,31},{0,1... | collective-permute-start | bytes 1572872 | tf_op jit(solution)/shard_map/ppermute | solution.py:55
  88.5 1.3 collective-permute-start.20
  89.8 5.3 %collective-permute-done.15.refs_2_ = f32[256,512]{1,0:T(8,128)S(1)} collective-permute-done((f32[256,512]{1,0:T(8,128)S(1)}, f32[256,512]{1,0:T(8,128)S(1)}, u32[]{:S(2)}, u32[]{:S(2)}) %collective-permute-start.15) | collective-permute-done | bytes 524320 | tf_op jit(solution)/shard_map/ppermute | solution.py:55
  95.3 0.5 collective-permute-start.19
  95.8 1.4 collective-permute-done.18.refs_3_
  97.2 3.7 %shard_map.76 = (bf16[1024,512]{1,0:T(8,128)(2,1)S(1)}, bf16[1024,512]{1,0:T(8,128)(2,1)S(1)}) custom-call(s32[5]{0:T(128)S(1)} %convert_element_type.3.place, f32[512,512]{1,0:T(8,128)S(1)} %get-tuple-element.79.refs_0_, f32[512,512]{1,0:T(8,128)S(1)} %get-tuple-element.84.refs_1_, f32[256,512]{1,0:T(8,128)S(1)} %broadcast_select_fusion.2.refs_2_, ...), custom_call_target="tpu_custom_call" | custom-call | flops 3000000000 | tf_op jit(solution)/shard_map/pallas_call | solution.py:123
  100.9 1.8 %shard_map.78 = (f32[256,512]{1,0:T(8,128)S(1)}, f32[256,512]{1,0:T(8,128)S(1)}) custom-call(f32[512,256]{1,0:T(8,128)S(1)} %get-tuple-element.83.near_end.c, f32[512,256]{1,0:T(8,128)S(1)} %get-tuple-element.82.own, f32[512,512]{1,0:T(8,128)S(1)} %get-tuple-element.94.both, bf16[1024,512]{1,0:T(8,128)(2,1)S(1)} %get-tuple-element.95.high, ...), custom_call_target="tpu_custom_call" | custom-call | flops 2000000000 | tf_op jit(solution)/shard_map/pallas_call | solution.py:141
  102.7 1.3 collective-permute-start.21
  104.0 1.5 %collective-permute-start.22 = (f32[256,512]{1,0:T(8,128)S(1)}, f32[256,512]{1,0:T(8,128)S(1)}, u32[]{:S(2)}, u32[]{:S(2)}) collective-permute-start(f32[256,512]{1,0:T(8,128)S(1)} %get-tuple-element.98), channel_id=1, source_target_pairs={{1,0},{2,3},{5,4},{6,7},{9,8},{10,11},{13,12},{14,15},{17,16},{18,... | collective-permute-start | bytes 1572872 | tf_op jit(solution)/shard_map/ppermute | solution.py:51
  105.5 3.7 %shard_map.79 = (bf16[1024,512]{1,0:T(8,128)(2,1)S(1)}, bf16[1024,512]{1,0:T(8,128)(2,1)S(1)}) custom-call(s32[5]{0:T(128)S(1)} %convert_element_type.3.place, f32[512,512]{1,0:T(8,128)S(1)} %broadcast_select_fusion.refs_0_, f32[512,512]{1,0:T(8,128)S(1)} %collective-permute-done.19.refs_1_, f32[256,512]{1,0:T(8,128)S(1)} %broadcast_select_fusion.2.refs_2_, ...), custom_call_target="tpu_custom_call" | custom-call | flops 3000000000 | tf_op jit(solution)/shard_map/pallas_call | solution.py:123
  109.2 3.5 %shard_map.82.refs_2_ = f32[2048,512]{1,0:T(8,128)} custom-call(s32[5]{0:T(128)S(1)} %convert_element_type.3.place, f32[2048,512]{1,0:T(8,128)S(1)} %copy-done, bf16[1024,512]{1,0:T(8,128)(2,1)S(1)} %get-tuple-element.102.high, bf16[1024,512]{1,0:T(8,128)(2,1)S(1)} %get-tuple-element.103.low, f32[512,256]{1,0:T(8,128)S(1)} %pad_maximum_fusion.3.own, ...), custom_call_target="tpu_custom_call" | custom-call | flops 3000000000 | tf_op jit(solution)/shard_map/pallas_call | solution.py:170
  112.8 3.6 %collective-permute-done.20.refs_1_ = f32[1024,256]{1,0:T(8,128)S(1)} collective-permute-done((f32[1024,256]{1,0:T(8,128)S(1)}, f32[1024,256]{1,0:T(8,128)S(1)}, u32[]{:S(2)}, u32[]{:S(2)}) %collective-permute-start.20) | collective-permute-done | bytes 1048608 | tf_op jit(solution)/shard_map/ppermute | solution.py:51
  116.4 5.4 %shard_map.84.kept = f32[2048,512]{1,0:T(8,128)} custom-call(s32[5]{0:T(128)S(1)} %convert_element_type.3.place, f32[2048,512]{1,0:T(8,128)S(1)} %copy-done, bf16[1024,512]{1,0:T(8,128)(2,1)S(1)} %get-tuple-element.102.high, bf16[1024,512]{1,0:T(8,128)(2,1)S(1)} %get-tuple-element.103.low, ...), custom_call_target="tpu_custom_call", output_to_operand_aliasing={{}: (10, {})} | custom-call | flops 3000000000 | tf_op jit(solution)/shard_map/pallas_call | solution.py:170
  121.8 1.5 %shard_map.85.kept = f32[2048,512]{1,0:T(8,128)} custom-call(s32[5]{0:T(128)S(1)} %convert_element_type.3.place, f32[2048,512]{1,0:T(8,128)S(1)} %copy-done, f32[512,256]{1,0:T(8,128)S(1)} %get-tuple-element.83.near_end.c, f32[512,256]{1,0:T(8,128)S(1)} %get-tuple-element.82.own, ...), custom_call_target="tpu_custom_call", output_to_operand_aliasing={{}: (7, {})} | custom-call | flops 2000000000 | tf_op jit(solution)/shard_map/pallas_call | solution.py:200
  123.3 4.3 %collective-permute-done.21.returned = f32[256,512]{1,0:T(8,128)S(1)} collective-permute-done((f32[256,512]{1,0:T(8,128)S(1)}, f32[256,512]{1,0:T(8,128)S(1)}, u32[]{:S(2)}, u32[]{:S(2)}) %collective-permute-start.21) | collective-permute-done | bytes 524320 | tf_op jit(solution)/shard_map/ppermute | solution.py:51
  127.6 1.9 %shard_map.86.kept = f32[2048,512]{1,0:T(8,128)} custom-call(s32[5]{0:T(128)S(1)} %convert_element_type.3.place, f32[2048,512]{1,0:T(8,128)S(1)} %copy-done, f32[256,512]{1,0:T(8,128)S(1)} %collective-permute-done.21.returned, f32[2048,512]{1,0:T(8,128)} %shard_map.85.kept), custom_call_target="tpu_custom_call", output_to_operand_aliasing={{}: (3, {})} | custom-call | flops 1000000000 | tf_op jit(solution)/shard_map/pallas_call | solution.py:200
  129.5 8.7 %collective-permute-done.22.returned = f32[256,512]{1,0:T(8,128)S(1)} collective-permute-done((f32[256,512]{1,0:T(8,128)S(1)}, f32[256,512]{1,0:T(8,128)S(1)}, u32[]{:S(2)}, u32[]{:S(2)}) %collective-permute-start.22) | collective-permute-done | bytes 524320 | tf_op jit(solution)/shard_map/ppermute | solution.py:51
  138.2 1.9 %shard_map.87 = f32[2048,512]{1,0:T(8,128)} custom-call(s32[5]{0:T(128)S(1)} %convert_element_type.3.place, f32[2048,512]{1,0:T(8,128)S(1)} %copy-done, f32[256,512]{1,0:T(8,128)S(1)} %collective-permute-done.22.returned, f32[2048,512]{1,0:T(8,128)} %shard_map.86.kept), custom_call_target="tpu_custom_call", output_to_operand_aliasing={{}: (3, {})} | custom-call | flops 1000000000 | tf_op jit(solution)/shard_map/pallas_call | solution.py:200
  (64 shorter events, 1.2 us)
Async XLA Ops:
  0.0 2.8 %slice-start = ((f32[2048,512]{1,0:T(8,128)}), f32[512,512]{1,0:T(8,128)S(1)}, s32[]{:S(2)}) async-start(f32[2048,512]{1,0:T(8,128)} %top.9), calls=%async_computation | async-start | bytes 2097152 | tf_op jit(solution)/shard_map/slice | solution.py:281
  1.4 18.7 %collective-permute-start = (f32[512,256]{1,0:T(8,128)S(1)}, f32[512,256]{1,0:T(8,128)S(1)}, u32[]{:S(2)}, u32[]{:S(2)}) collective-permute-start(f32[512,256]{1,0:T(8,128)S(1)} %pad_maximum_fusion.3.own), channel_id=1, source_target_pairs={{4,5},{7,6},{5,4},{6,7},{8,9},{11,10},{9,8},{10,11},{12,13},{15,14... | collective-permute-start | bytes 1572872 | tf_op jit(solution)/shard_map/ppermute | solution.py:51
  2.1 18.0 %collective-permute-start.1 = (f32[512,256]{1,0:T(8,128)S(1)}, f32[512,256]{1,0:T(8,128)S(1)}, u32[]{:S(2)}, u32[]{:S(2)}) collective-permute-start(f32[512,256]{1,0:T(8,128)S(1)} %pad_maximum_fusion.3.own), channel_id=1, source_target_pairs={{5,6},{6,5},{9,10},{10,9},{13,14},{14,13},{17,18},{18,17},{21,22},... | collective-permute-start | bytes 1572872 | tf_op jit(solution)/shard_map/ppermute | solution.py:51
  3.0 7.2 %collective-permute-start.2 = (f32[256,512]{1,0:T(8,128)S(1)}, f32[256,512]{1,0:T(8,128)S(1)}, u32[]{:S(2)}, u32[]{:S(2)}) collective-permute-start(f32[256,512]{1,0:T(8,128)S(1)} %get-tuple-element.120), channel_id=1, source_target_pairs={{0,4},{1,5},{2,6},{3,7},{4,0},{5,1},{6,2},{7,3}} | collective-permute-start | bytes 1572872 | tf_op jit(solution)/shard_map/ppermute | solution.py:55
  8.7 1.0 slice-start.1
  8.7 1.2 slice-start.2
  11.3 15.0 %collective-permute-start.3 = (f32[512,512]{1,0:T(8,128)}, f32[512,512]{1,0:T(8,128)}, u32[]{:S(2)}, u32[]{:S(2)}) collective-permute-start(f32[512,512]{1,0:T(8,128)} %maximum_select_fusion), channel_id=1, source_target_pairs={{0,8},{1,9},{2,10},{3,11},{4,20},{5,21},{6,22},{7,23}} | collective-permute-start | bytes 3145736 | tf_op jit(solution)/shard_map/ppermute | solution.py:55
  14.9 28.5 %collective-permute-start.4 = (f32[1024,256]{1,0:T(8,128)S(1)}, f32[1024,256]{1,0:T(8,128)S(1)}, u32[]{:S(2)}, u32[]{:S(2)}) collective-permute-start(f32[1024,256]{1,0:T(8,128)S(1)} %pad_maximum_fusion.own), channel_id=1, source_target_pairs={{0,1},{3,2},{1,0},{2,3},{4,5},{7,6},{5,4},{6,7},{8,9},{11,10},{9,8... | collective-permute-start | bytes 3145736 | tf_op jit(solution)/shard_map/ppermute | solution.py:51
  19.3 24.1 %collective-permute-start.5 = (f32[1024,256]{1,0:T(8,128)S(1)}, f32[1024,256]{1,0:T(8,128)S(1)}, u32[]{:S(2)}, u32[]{:S(2)}) collective-permute-start(f32[1024,256]{1,0:T(8,128)S(1)} %pad_maximum_fusion.own), channel_id=1, source_target_pairs={{1,2},{2,1},{5,6},{6,5},{9,10},{10,9},{13,14},{14,13},{17,18},{18,... | collective-permute-start | bytes 3145736 | tf_op jit(solution)/shard_map/ppermute | solution.py:51
  27.8 15.6 %collective-permute-start.6 = (f32[512,512]{1,0:T(8,128)S(1)}, f32[512,512]{1,0:T(8,128)S(1)}, u32[]{:S(2)}, u32[]{:S(2)}) collective-permute-start(f32[512,512]{1,0:T(8,128)S(1)} %broadcast_select_fusion.1), channel_id=1, source_target_pairs={{8,24},{9,25},{10,26},{11,27},{20,28},{21,29},{22,30},{23,31},{0,1... | collective-permute-start | bytes 3145736 | tf_op jit(solution)/shard_map/ppermute | solution.py:55
  29.2 23.0 %collective-permute-start.8 = (f32[512,256]{1,0:T(8,128)S(1)}, f32[512,256]{1,0:T(8,128)S(1)}, u32[]{:S(2)}, u32[]{:S(2)}) collective-permute-start(f32[512,256]{1,0:T(8,128)S(1)} %get-tuple-element.68.swap), channel_id=1, source_target_pairs={{5,6},{6,5},{9,10},{10,9},{13,14},{14,13},{17,18},{18,17},{21,22},... | collective-permute-start | bytes 1572872 | tf_op jit(solution)/shard_map/ppermute | solution.py:51
  30.0 22.2 %collective-permute-start.7 = (f32[512,256]{1,0:T(8,128)S(1)}, f32[512,256]{1,0:T(8,128)S(1)}, u32[]{:S(2)}, u32[]{:S(2)}) collective-permute-start(f32[512,256]{1,0:T(8,128)S(1)} %broadcast_select_fusion.4), channel_id=1, source_target_pairs={{5,4},{6,7},{9,8},{10,11},{13,12},{14,15},{17,16},{18,19},{21,20},... | collective-permute-start | bytes 1572872 | tf_op jit(solution)/shard_map/ppermute | solution.py:301
  52.2 9.0 %copy-start.1 = (f32[512,512]{1,0:T(8,128)S(1)}, f32[512,512]{1,0:T(8,128)}, u32[]{:S(2)}) copy-start(f32[512,512]{1,0:T(8,128)} %one) | copy-start | bytes 3145732
  52.2 9.1 %copy-start.2 = (f32[512,512]{1,0:T(8,128)S(1)}, f32[512,512]{1,0:T(8,128)}, u32[]{:S(2)}) copy-start(f32[512,512]{1,0:T(8,128)} %two) | copy-start | bytes 3145732
  52.2 9.4 %collective-permute-start.9 = (f32[512,256]{1,0:T(8,128)S(1)}, f32[512,256]{1,0:T(8,128)S(1)}, u32[]{:S(2)}, u32[]{:S(2)}) collective-permute-start(f32[512,256]{1,0:T(8,128)S(1)} %get-tuple-element.72.far), channel_id=1, source_target_pairs={{5,4},{6,7},{9,8},{10,11},{13,12},{14,15},{17,16},{18,19},{21,20},... | collective-permute-start | bytes 1572872 | tf_op jit(solution)/shard_map/ppermute | solution.py:51
  53.0 23.2 %collective-permute-start.10 = (f32[1024,256]{1,0:T(8,128)S(1)}, f32[1024,256]{1,0:T(8,128)S(1)}, u32[]{:S(2)}, u32[]{:S(2)}) collective-permute-start(f32[1024,256]{1,0:T(8,128)S(1)} %get-tuple-element.74.swap), channel_id=1, source_target_pairs={{1,2},{2,1},{5,6},{6,5},{9,10},{10,9},{13,14},{14,13},{17,18},{18,... | collective-permute-start | bytes 3145736 | tf_op jit(solution)/shard_map/ppermute | solution.py:51
  54.0 27.2 %collective-permute-start.11 = (f32[512,512]{1,0:T(8,128)S(1)}, f32[512,512]{1,0:T(8,128)S(1)}, u32[]{:S(2)}, u32[]{:S(2)}) collective-permute-start(f32[512,512]{1,0:T(8,128)S(1)} %broadcast_select_fusion.refs_0_), channel_id=1, source_target_pairs={{0,1},{3,2},{4,5},{7,6},{8,9},{11,10},{12,13},{15,14},{16,17},{19,... | collective-permute-start | bytes 3145736 | tf_op jit(solution)/shard_map/ppermute | solution.py:51
  59.9 29.9 %collective-permute-start.14 = (f32[1024,256]{1,0:T(8,128)S(1)}, f32[1024,256]{1,0:T(8,128)S(1)}, u32[]{:S(2)}, u32[]{:S(2)}) collective-permute-start(f32[1024,256]{1,0:T(8,128)S(1)} %get-tuple-element.77.mid), channel_id=1, source_target_pairs={{1,0},{2,3},{5,4},{6,7},{9,8},{10,11},{13,12},{14,15},{17,16},{18,... | collective-permute-start | bytes 3145736 | tf_op jit(solution)/shard_map/ppermute | solution.py:51
  61.8 3.8 %collective-permute-start.12 = (f32[256,512]{1,0:T(8,128)S(1)}, f32[256,512]{1,0:T(8,128)S(1)}, u32[]{:S(2)}, u32[]{:S(2)}) collective-permute-start(f32[256,512]{1,0:T(8,128)S(1)} %slice.70), channel_id=1, source_target_pairs={{4,0},{5,1},{6,2},{7,3}} | collective-permute-start | bytes 1572872 | tf_op jit(solution)/shard_map/ppermute | solution.py:55
  63.2 37.7 %collective-permute-start.17 = (f32[512,512]{1,0:T(8,128)S(1)}, f32[512,512]{1,0:T(8,128)S(1)}, u32[]{:S(2)}, u32[]{:S(2)}) collective-permute-start(f32[512,512]{1,0:T(8,128)S(1)} %pad_maximum_fusion.2), channel_id=1, source_target_pairs={{1,2},{2,1},{5,6},{6,5},{9,10},{10,9},{13,14},{14,13},{17,18},{18,... | collective-permute-start | bytes 3145736 | tf_op jit(solution)/shard_map/ppermute | solution.py:51
  65.7 17.2 %collective-permute-start.13 = (f32[256,512]{1,0:T(8,128)S(1)}, f32[256,512]{1,0:T(8,128)S(1)}, u32[]{:S(2)}, u32[]{:S(2)}) collective-permute-start(f32[256,512]{1,0:T(8,128)S(1)} %slice_select_fusion), channel_id=1, source_target_pairs={{0,8},{1,9},{2,10},{3,11},{4,20},{5,21},{6,22},{7,23}} | collective-permute-start | bytes 1572872 | tf_op jit(solution)/shard_map/ppermute | solution.py:55
  82.9 12.2 %collective-permute-start.16 = (f32[512,512]{1,0:T(8,128)S(1)}, f32[512,512]{1,0:T(8,128)S(1)}, u32[]{:S(2)}, u32[]{:S(2)}) collective-permute-start(f32[512,512]{1,0:T(8,128)S(1)} %get-tuple-element.79.refs_0_), channel_id=1, source_target_pairs={{0,4},{1,5},{2,6},{3,7},{4,0},{5,1},{6,2},{7,3},{8,12},{9,13},{10,... | collective-permute-start | bytes 3145736 | tf_op jit(solution)/shard_map/ppermute | solution.py:55
  83.0 12.1 %collective-permute-start.15 = (f32[256,512]{1,0:T(8,128)S(1)}, f32[256,512]{1,0:T(8,128)S(1)}, u32[]{:S(2)}, u32[]{:S(2)}) collective-permute-start(f32[256,512]{1,0:T(8,128)S(1)} %broadcast_select_fusion.3), channel_id=1, source_target_pairs={{8,24},{9,25},{10,26},{11,27},{20,28},{21,29},{22,30},{23,31},{0,1... | collective-permute-start | bytes 1572872 | tf_op jit(solution)/shard_map/ppermute | solution.py:55
  88.5 27.9 %collective-permute-start.20 = (f32[1024,256]{1,0:T(8,128)S(1)}, f32[1024,256]{1,0:T(8,128)S(1)}, u32[]{:S(2)}, u32[]{:S(2)}) collective-permute-start(f32[1024,256]{1,0:T(8,128)S(1)} %get-tuple-element.104.far), channel_id=1, source_target_pairs={{1,0},{2,3},{5,4},{6,7},{9,8},{10,11},{13,12},{14,15},{17,16},{18,... | collective-permute-start | bytes 3145736 | tf_op jit(solution)/shard_map/ppermute | solution.py:51
  95.2 2.0 %collective-permute-start.18 = (f32[256,512]{1,0:T(8,128)S(1)}, f32[256,512]{1,0:T(8,128)S(1)}, u32[]{:S(2)}, u32[]{:S(2)}) collective-permute-start(f32[256,512]{1,0:T(8,128)S(1)} %broadcast_select_fusion.2.refs_2_), channel_id=1, source_target_pairs={{0,4},{1,5},{2,6},{3,7},{4,0},{5,1},{6,2},{7,3},{8,12},{9,13},{10,... | collective-permute-start | bytes 1572872 | tf_op jit(solution)/shard_map/ppermute | solution.py:55
  95.3 10.2 %collective-permute-start.19 = (f32[512,512]{1,0:T(8,128)S(1)}, f32[512,512]{1,0:T(8,128)S(1)}, u32[]{:S(2)}, u32[]{:S(2)}) collective-permute-start(f32[512,512]{1,0:T(8,128)S(1)} %broadcast_select_fusion.refs_0_), channel_id=1, source_target_pairs={{0,4},{1,5},{2,6},{3,7},{4,0},{5,1},{6,2},{7,3},{8,12},{9,13},{10,... | collective-permute-start | bytes 3145736 | tf_op jit(solution)/shard_map/ppermute | solution.py:55
  102.7 24.9 %collective-permute-start.21 = (f32[256,512]{1,0:T(8,128)S(1)}, f32[256,512]{1,0:T(8,128)S(1)}, u32[]{:S(2)}, u32[]{:S(2)}) collective-permute-start(f32[256,512]{1,0:T(8,128)S(1)} %get-tuple-element.97), channel_id=1, source_target_pairs={{1,0},{2,3},{5,4},{6,7},{9,8},{10,11},{13,12},{14,15},{17,16},{18,... | collective-permute-start | bytes 1572872 | tf_op jit(solution)/shard_map/ppermute | solution.py:51
  104.0 34.2 %collective-permute-start.22 = (f32[256,512]{1,0:T(8,128)S(1)}, f32[256,512]{1,0:T(8,128)S(1)}, u32[]{:S(2)}, u32[]{:S(2)}) collective-permute-start(f32[256,512]{1,0:T(8,128)S(1)} %get-tuple-element.98), channel_id=1, source_target_pairs={{1,0},{2,3},{5,4},{6,7},{9,8},{10,11},{13,12},{14,15},{17,16},{18,... | collective-permute-start | bytes 1572872 | tf_op jit(solution)/shard_map/ppermute | solution.py:51
  105.5 3.7 %copy-start = (f32[2048,512]{1,0:T(8,128)S(1)}, f32[2048,512]{1,0:T(8,128)}, u32[]{:S(2)}) copy-start(f32[2048,512]{1,0:T(8,128)} %top.9) | copy-start | bytes 12582916

commit v8 on v7

--- a/solution.py
+++ b/solution.py
@@ -308,11 +308,11 @@
     hop = along_col(mine, END_MID, every)
     rest_far = along_col(rest_swap, MID_MID, every)
     inverses = split_inverses(*tied((first_inverse, second_inverse, token))[:2])
-    token, crossed, lead_far = stage(token, crossed, lead_far)
+    token, lead_far = stage(token, lead_far)
 
     lead_cc = along_col(lead_far, MID_END, most)
     rest_c = along_col(rest_mid, MID_END, every)
-    token, lead_cc = stage(token, lead_cc)
+    token, lead_cc, crossed = stage(token, lead_cc, crossed)
 
     slabs = [v[:, :slab] for v in (lead_own, lead_swap, lead_mid, lead_far, crossed, lead_cc)]
     corner = ordered(*slabs)

time: 141 us -> 141 us (level)
  waiting for transfers between devices: 54 us -> 50.2 us
  starting transfers between devices: 55.5 us -> 59.2 us
    ppermute x9, waiting for transfers between devices: 16.6 us -> 26.4 us  [along_row(): lax.ppermute(value, AXES, [(a * COLS + c, b * COLS + c) for a, b in pairs...]
    ppermute x1, waiting for transfers between devices: 8.74 us -> 0.01 us  [four(): lax.ppermute(jnp.where(end, last_own, lead_mid), AXES, pairs_of(MID_END,...]
    ppermute x13, waiting for transfers between devices: 28.6 us -> 23.7 us  [along_col(): return lax.ppermute(value, AXES, pairs_of(pairs, rows))]
    ppermute x9, starting transfers between devices: 28.4 us -> 31 us  [along_row(): lax.ppermute(value, AXES, [(a * COLS + c, b * COLS + c) for a, b in pairs...]
  transfers between devices with their start and end apart: 23 -> 23, of which waited for: 12 -> 10; matrix products, arithmetic and copies ran while one was open for 3% -> 3% of each run, Pallas kernels for 16% -> 16%
where the time goes in v8:
time: 141 us; the launch traced here: 140 us
  starting transfers between devices  59.2 us (42%)
  waiting for transfers between devices  50.2 us (36%)
  Pallas kernels  23.8 us (17%)
  other arithmetic  3.67 us (3%)
  local copies, waits for them, and re-layouts  2.69 us (2%)
    ppermute x9, starting transfers between devices, along_row(): lax.ppermute(value, AXES, [(a * COLS + c, b * COLS + c) for a, b in pairs...  31 us
    ppermute x9, waiting for transfers between devices, along_row(): lax.ppermute(value, AXES, [(a * COLS + c, b * COLS + c) for a, b in pairs...  26.4 us
    ppermute x13, waiting for transfers between devices, along_col(): return lax.ppermute(value, AXES, pairs_of(pairs, rows))  23.7 us
    ppermute x13, starting transfers between devices, along_col(): return lax.ppermute(value, AXES, pairs_of(pairs, rows))  21.9 us
    pallas_call x2, Pallas kernels, update_raw(): pl.pallas_call(functools.partial(update_raw_kernel, blocks), grid=(group[...  8.96 us
    pallas_call x2, Pallas kernels, solve(): pl.pallas_call(solve_kernel, out_shape=[part, part], in_specs=[SMEM] + [p...  7.36 us
    ppermute x1, starting transfers between devices, four(): lax.ppermute(jnp.where(end, last_own, lead_mid), AXES, pairs_of(MID_END,...  6.3 us
    pallas_call x3, Pallas kernels, last_call(): pl.pallas_call(body, grid=(count,), out_shape=jax.ShapeDtypeStruct(top.sh...  5.35 us
  transfers between devices with their start and end apart: 23, of which 10 were waited for; matrix products, arithmetic and copies ran while one was open for 3% of the time, Pallas kernels for 16%

profile of v8, /device:TPU:0, one launch (start us, length us, event | category | flops | bytes accessed | tf_op | source)
XLA Modules:
  0.0 140.1 jit_solution(1516237153824327001)
XLA Ops:
  0.0 1.3 fusion
  1.4 0.7 collective-permute-start
  2.1 0.7 collective-permute-start.1
  2.8 0.1 fusion.2
  3.0 5.7 %collective-permute-start.2 = (f32[256,512]{1,0:T(8,128)S(1)}, f32[256,512]{1,0:T(8,128)S(1)}, u32[]{:S(2)}, u32[]{:S(2)}) collective-permute-start(f32[256,512]{1,0:T(8,128)S(1)} %get-tuple-element.120), channel_id=1, source_target_pairs={{0,4},{1,5},{2,6},{3,7},{4,0},{5,1},{6,2},{7,3}} | collective-permute-start | bytes 1572872 | tf_op jit(solution)/shard_map/ppermute | solution.py:55
  8.7 1.0 slice-done.1
  9.7 0.2 slice-done.2
  10.0 0.2 collective-permute-done.2
  10.2 1.1 maximum_select_fusion
  11.3 3.4 %collective-permute-start.3 = (f32[512,512]{1,0:T(8,128)}, f32[512,512]{1,0:T(8,128)}, u32[]{:S(2)}, u32[]{:S(2)}) collective-permute-start(f32[512,512]{1,0:T(8,128)} %maximum_select_fusion), channel_id=1, source_target_pairs={{0,8},{1,9},{2,10},{3,11},{4,20},{5,21},{6,22},{7,23}} | collective-permute-start | bytes 3145736 | tf_op jit(solution)/shard_map/ppermute | solution.py:55
  14.9 4.4 %collective-permute-start.4 = (f32[1024,256]{1,0:T(8,128)S(1)}, f32[1024,256]{1,0:T(8,128)S(1)}, u32[]{:S(2)}, u32[]{:S(2)}) collective-permute-start(f32[1024,256]{1,0:T(8,128)S(1)} %pad_maximum_fusion.own), channel_id=1, source_target_pairs={{0,1},{3,2},{1,0},{2,3},{4,5},{7,6},{5,4},{6,7},{8,9},{11,10},{9,8... | collective-permute-start | bytes 3145736 | tf_op jit(solution)/shard_map/ppermute | solution.py:51
  19.3 0.7 collective-permute-start.5
  20.1 6.3 %collective-permute-done.3.refs_3_ = f32[512,512]{1,0:T(8,128)} collective-permute-done((f32[512,512]{1,0:T(8,128)}, f32[512,512]{1,0:T(8,128)}, u32[]{:S(2)}, u32[]{:S(2)}) %collective-permute-start.3) | collective-permute-done | bytes 1048608 | tf_op jit(solution)/shard_map/ppermute | solution.py:55
  26.4 1.4 %broadcast_select_fusion.1 = f32[512,512]{1,0:T(8,128)S(1)} fusion(f32[512,512]{1,0:T(8,128)} %get-tuple-element.64, f32[512,512]{1,0:T(8,128)} %maximum_select_fusion, pred[]{:T(512)S(6)} %or.16), kind=kLoop, calls=%fused_computation.8 | loop fusion | flops 262144 | bytes 3145729 | tf_op jit(solution)/shard_map/jit(_where)/select_n | solution.py:269
  27.8 1.4 collective-permute-start.6
  29.2 0.7 collective-permute-start.7
  30.0 6.3 %collective-permute-start.9 = (f32[512,256]{1,0:T(8,128)S(1)}, f32[512,256]{1,0:T(8,128)S(1)}, u32[]{:S(2)}, u32[]{:S(2)}) collective-permute-start(f32[512,256]{1,0:T(8,128)S(1)} %broadcast_select_fusion.4), channel_id=1, source_target_pairs={{5,4},{6,7},{9,8},{10,11},{13,12},{14,15},{17,16},{18,19},{21,20},... | collective-permute-start | bytes 1572872 | tf_op jit(solution)/shard_map/ppermute | solution.py:301
  36.3 7.1 %collective-permute-done.4.refs_1_ = f32[1024,256]{1,0:T(8,128)S(1)} collective-permute-done((f32[1024,256]{1,0:T(8,128)S(1)}, f32[1024,256]{1,0:T(8,128)S(1)}, u32[]{:S(2)}, u32[]{:S(2)}) %collective-permute-start.4) | collective-permute-done | bytes 1048608 | tf_op jit(solution)/shard_map/ppermute | solution.py:51
  43.5 0.8 collective-permute-start.8
  44.3 0.7 collective-permute-start.10
  45.1 0.2 broadcast_select_fusion.refs_0_
  45.3 7.1 %collective-permute-start.11 = (f32[512,512]{1,0:T(8,128)S(1)}, f32[512,512]{1,0:T(8,128)S(1)}, u32[]{:S(2)}, u32[]{:S(2)}) collective-permute-start(f32[512,512]{1,0:T(8,128)S(1)} %broadcast_select_fusion.refs_0_), channel_id=1, source_target_pairs={{0,1},{3,2},{4,5},{7,6},{8,9},{11,10},{12,13},{15,14},{16,17},{19,... | collective-permute-start | bytes 3145736 | tf_op jit(solution)/shard_map/ppermute | solution.py:51
  52.4 1.3 collective-permute-start.14
  53.7 0.3 shard_map.75
  54.2 1.3 collective-permute-start.12
  55.5 0.1 pad_maximum_fusion.2
  55.6 0.7 collective-permute-start.17
  56.4 6.6 %collective-permute-done.12 = f32[256,512]{1,0:T(8,128)S(1)} collective-permute-done((f32[256,512]{1,0:T(8,128)S(1)}, f32[256,512]{1,0:T(8,128)S(1)}, u32[]{:S(2)}, u32[]{:S(2)}) %collective-permute-start.12) | collective-permute-done | bytes 524320 | tf_op jit(solution)/shard_map/ppermute | solution.py:55
  63.1 13.2 %collective-permute-start.13 = (f32[256,512]{1,0:T(8,128)S(1)}, f32[256,512]{1,0:T(8,128)S(1)}, u32[]{:S(2)}, u32[]{:S(2)}) collective-permute-start(f32[256,512]{1,0:T(8,128)S(1)} %slice_select_fusion), channel_id=1, source_target_pairs={{0,8},{1,9},{2,10},{3,11},{4,20},{5,21},{6,22},{7,23}} | collective-permute-start | bytes 1572872 | tf_op jit(solution)/shard_map/ppermute | solution.py:55
  76.3 6.6 %collective-permute-done.13.refs_3_ = f32[256,512]{1,0:T(8,128)S(1)} collective-permute-done((f32[256,512]{1,0:T(8,128)S(1)}, f32[256,512]{1,0:T(8,128)S(1)}, u32[]{:S(2)}, u32[]{:S(2)}) %collective-permute-start.13) | collective-permute-done | bytes 524320 | tf_op jit(solution)/shard_map/ppermute | solution.py:55
  83.0 5.4 %collective-permute-start.15 = (f32[256,512]{1,0:T(8,128)S(1)}, f32[256,512]{1,0:T(8,128)S(1)}, u32[]{:S(2)}, u32[]{:S(2)}) collective-permute-start(f32[256,512]{1,0:T(8,128)S(1)} %broadcast_select_fusion.3), channel_id=1, source_target_pairs={{8,24},{9,25},{10,26},{11,27},{20,28},{21,29},{22,30},{23,31},{0,1... | collective-permute-start | bytes 1572872 | tf_op jit(solution)/shard_map/ppermute | solution.py:55
  88.5 1.3 collective-permute-start.20
  89.8 5.3 %collective-permute-done.15.refs_2_ = f32[256,512]{1,0:T(8,128)S(1)} collective-permute-done((f32[256,512]{1,0:T(8,128)S(1)}, f32[256,512]{1,0:T(8,128)S(1)}, u32[]{:S(2)}, u32[]{:S(2)}) %collective-permute-start.15) | collective-permute-done | bytes 524320 | tf_op jit(solution)/shard_map/ppermute | solution.py:55
  95.3 0.5 collective-permute-start.19
  95.8 1.4 collective-permute-done.18.refs_3_
  97.2 3.7 %shard_map.76 = (bf16[1024,512]{1,0:T(8,128)(2,1)S(1)}, bf16[1024,512]{1,0:T(8,128)(2,1)S(1)}) custom-call(s32[5]{0:T(128)S(1)} %convert_element_type.3.place, f32[512,512]{1,0:T(8,128)S(1)} %get-tuple-element.79.refs_0_, f32[512,512]{1,0:T(8,128)S(1)} %get-tuple-element.84.refs_1_, f32[256,512]{1,0:T(8,128)S(1)} %broadcast_select_fusion.2.refs_2_, ...), custom_call_target="tpu_custom_call" | custom-call | flops 3000000000 | tf_op jit(solution)/shard_map/pallas_call | solution.py:123
  100.9 1.8 %shard_map.78 = (f32[256,512]{1,0:T(8,128)S(1)}, f32[256,512]{1,0:T(8,128)S(1)}) custom-call(f32[512,256]{1,0:T(8,128)S(1)} %get-tuple-element.83.near_end.c, f32[512,256]{1,0:T(8,128)S(1)} %get-tuple-element.82.own, f32[512,512]{1,0:T(8,128)S(1)} %get-tuple-element.94.both, bf16[1024,512]{1,0:T(8,128)(2,1)S(1)} %get-tuple-element.95.high, ...), custom_call_target="tpu_custom_call" | custom-call | flops 2000000000 | tf_op jit(solution)/shard_map/pallas_call | solution.py:141
  102.7 1.3 collective-permute-start.21
  104.0 1.5 %collective-permute-start.22 = (f32[256,512]{1,0:T(8,128)S(1)}, f32[256,512]{1,0:T(8,128)S(1)}, u32[]{:S(2)}, u32[]{:S(2)}) collective-permute-start(f32[256,512]{1,0:T(8,128)S(1)} %get-tuple-element.98), channel_id=1, source_target_pairs={{1,0},{2,3},{5,4},{6,7},{9,8},{10,11},{13,12},{14,15},{17,16},{18,... | collective-permute-start | bytes 1572872 | tf_op jit(solution)/shard_map/ppermute | solution.py:51
  105.5 3.7 %shard_map.79 = (bf16[1024,512]{1,0:T(8,128)(2,1)S(1)}, bf16[1024,512]{1,0:T(8,128)(2,1)S(1)}) custom-call(s32[5]{0:T(128)S(1)} %convert_element_type.3.place, f32[512,512]{1,0:T(8,128)S(1)} %broadcast_select_fusion.refs_0_, f32[512,512]{1,0:T(8,128)S(1)} %collective-permute-done.19.refs_1_, f32[256,512]{1,0:T(8,128)S(1)} %broadcast_select_fusion.2.refs_2_, ...), custom_call_target="tpu_custom_call" | custom-call | flops 3000000000 | tf_op jit(solution)/shard_map/pallas_call | solution.py:123
  109.2 3.5 %shard_map.82.refs_2_ = f32[2048,512]{1,0:T(8,128)} custom-call(s32[5]{0:T(128)S(1)} %convert_element_type.3.place, f32[2048,512]{1,0:T(8,128)S(1)} %copy-done, bf16[1024,512]{1,0:T(8,128)(2,1)S(1)} %get-tuple-element.102.high, bf16[1024,512]{1,0:T(8,128)(2,1)S(1)} %get-tuple-element.103.low, f32[512,256]{1,0:T(8,128)S(1)} %pad_maximum_fusion.3.own, ...), custom_call_target="tpu_custom_call" | custom-call | flops 3000000000 | tf_op jit(solution)/shard_map/pallas_call | solution.py:170
  112.8 3.6 %collective-permute-done.20.refs_1_ = f32[1024,256]{1,0:T(8,128)S(1)} collective-permute-done((f32[1024,256]{1,0:T(8,128)S(1)}, f32[1024,256]{1,0:T(8,128)S(1)}, u32[]{:S(2)}, u32[]{:S(2)}) %collective-permute-start.20) | collective-permute-done | bytes 1048608 | tf_op jit(solution)/shard_map/ppermute | solution.py:51
  116.3 5.4 %shard_map.84.kept = f32[2048,512]{1,0:T(8,128)} custom-call(s32[5]{0:T(128)S(1)} %convert_element_type.3.place, f32[2048,512]{1,0:T(8,128)S(1)} %copy-done, bf16[1024,512]{1,0:T(8,128)(2,1)S(1)} %get-tuple-element.102.high, bf16[1024,512]{1,0:T(8,128)(2,1)S(1)} %get-tuple-element.103.low, ...), custom_call_target="tpu_custom_call", output_to_operand_aliasing={{}: (10, {})} | custom-call | flops 3000000000 | tf_op jit(solution)/shard_map/pallas_call | solution.py:170
  121.8 1.5 %shard_map.85.kept = f32[2048,512]{1,0:T(8,128)} custom-call(s32[5]{0:T(128)S(1)} %convert_element_type.3.place, f32[2048,512]{1,0:T(8,128)S(1)} %copy-done, f32[512,256]{1,0:T(8,128)S(1)} %get-tuple-element.83.near_end.c, f32[512,256]{1,0:T(8,128)S(1)} %get-tuple-element.82.own, ...), custom_call_target="tpu_custom_call", output_to_operand_aliasing={{}: (7, {})} | custom-call | flops 2000000000 | tf_op jit(solution)/shard_map/pallas_call | solution.py:200
  123.3 4.3 %collective-permute-done.21.returned = f32[256,512]{1,0:T(8,128)S(1)} collective-permute-done((f32[256,512]{1,0:T(8,128)S(1)}, f32[256,512]{1,0:T(8,128)S(1)}, u32[]{:S(2)}, u32[]{:S(2)}) %collective-permute-start.21) | collective-permute-done | bytes 524320 | tf_op jit(solution)/shard_map/ppermute | solution.py:51
  127.6 1.9 %shard_map.86.kept = f32[2048,512]{1,0:T(8,128)} custom-call(s32[5]{0:T(128)S(1)} %convert_element_type.3.place, f32[2048,512]{1,0:T(8,128)S(1)} %copy-done, f32[256,512]{1,0:T(8,128)S(1)} %collective-permute-done.21.returned, f32[2048,512]{1,0:T(8,128)} %shard_map.85.kept), custom_call_target="tpu_custom_call", output_to_operand_aliasing={{}: (3, {})} | custom-call | flops 1000000000 | tf_op jit(solution)/shard_map/pallas_call | solution.py:200
  129.5 8.7 %collective-permute-done.22.returned = f32[256,512]{1,0:T(8,128)S(1)} collective-permute-done((f32[256,512]{1,0:T(8,128)S(1)}, f32[256,512]{1,0:T(8,128)S(1)}, u32[]{:S(2)}, u32[]{:S(2)}) %collective-permute-start.22) | collective-permute-done | bytes 524320 | tf_op jit(solution)/shard_map/ppermute | solution.py:51
  138.2 1.9 %shard_map.87 = f32[2048,512]{1,0:T(8,128)} custom-call(s32[5]{0:T(128)S(1)} %convert_element_type.3.place, f32[2048,512]{1,0:T(8,128)S(1)} %copy-done, f32[256,512]{1,0:T(8,128)S(1)} %collective-permute-done.22.returned, f32[2048,512]{1,0:T(8,128)} %shard_map.86.kept), custom_call_target="tpu_custom_call", output_to_operand_aliasing={{}: (3, {})} | custom-call | flops 1000000000 | tf_op jit(solution)/shard_map/pallas_call | solution.py:200
  (64 shorter events, 1.0 us)
Async XLA Ops:
  0.0 2.8 %slice-start = ((f32[2048,512]{1,0:T(8,128)}), f32[512,512]{1,0:T(8,128)S(1)}, s32[]{:S(2)}) async-start(f32[2048,512]{1,0:T(8,128)} %top.9), calls=%async_computation | async-start | bytes 2097152 | tf_op jit(solution)/shard_map/slice | solution.py:281
  1.4 18.7 %collective-permute-start = (f32[512,256]{1,0:T(8,128)S(1)}, f32[512,256]{1,0:T(8,128)S(1)}, u32[]{:S(2)}, u32[]{:S(2)}) collective-permute-start(f32[512,256]{1,0:T(8,128)S(1)} %pad_maximum_fusion.3.own), channel_id=1, source_target_pairs={{4,5},{7,6},{5,4},{6,7},{8,9},{11,10},{9,8},{10,11},{12,13},{15,14... | collective-permute-start | bytes 1572872 | tf_op jit(solution)/shard_map/ppermute | solution.py:51
  2.1 18.0 %collective-permute-start.1 = (f32[512,256]{1,0:T(8,128)S(1)}, f32[512,256]{1,0:T(8,128)S(1)}, u32[]{:S(2)}, u32[]{:S(2)}) collective-permute-start(f32[512,256]{1,0:T(8,128)S(1)} %pad_maximum_fusion.3.own), channel_id=1, source_target_pairs={{5,6},{6,5},{9,10},{10,9},{13,14},{14,13},{17,18},{18,17},{21,22},... | collective-permute-start | bytes 1572872 | tf_op jit(solution)/shard_map/ppermute | solution.py:51
  3.0 7.2 %collective-permute-start.2 = (f32[256,512]{1,0:T(8,128)S(1)}, f32[256,512]{1,0:T(8,128)S(1)}, u32[]{:S(2)}, u32[]{:S(2)}) collective-permute-start(f32[256,512]{1,0:T(8,128)S(1)} %get-tuple-element.120), channel_id=1, source_target_pairs={{0,4},{1,5},{2,6},{3,7},{4,0},{5,1},{6,2},{7,3}} | collective-permute-start | bytes 1572872 | tf_op jit(solution)/shard_map/ppermute | solution.py:55
  8.7 1.0 slice-start.1
  8.7 1.2 slice-start.2
  11.3 15.0 %collective-permute-start.3 = (f32[512,512]{1,0:T(8,128)}, f32[512,512]{1,0:T(8,128)}, u32[]{:S(2)}, u32[]{:S(2)}) collective-permute-start(f32[512,512]{1,0:T(8,128)} %maximum_select_fusion), channel_id=1, source_target_pairs={{0,8},{1,9},{2,10},{3,11},{4,20},{5,21},{6,22},{7,23}} | collective-permute-start | bytes 3145736 | tf_op jit(solution)/shard_map/ppermute | solution.py:55
  14.9 28.5 %collective-permute-start.4 = (f32[1024,256]{1,0:T(8,128)S(1)}, f32[1024,256]{1,0:T(8,128)S(1)}, u32[]{:S(2)}, u32[]{:S(2)}) collective-permute-start(f32[1024,256]{1,0:T(8,128)S(1)} %pad_maximum_fusion.own), channel_id=1, source_target_pairs={{0,1},{3,2},{1,0},{2,3},{4,5},{7,6},{5,4},{6,7},{8,9},{11,10},{9,8... | collective-permute-start | bytes 3145736 | tf_op jit(solution)/shard_map/ppermute | solution.py:51
  19.3 24.1 %collective-permute-start.5 = (f32[1024,256]{1,0:T(8,128)S(1)}, f32[1024,256]{1,0:T(8,128)S(1)}, u32[]{:S(2)}, u32[]{:S(2)}) collective-permute-start(f32[1024,256]{1,0:T(8,128)S(1)} %pad_maximum_fusion.own), channel_id=1, source_target_pairs={{1,2},{2,1},{5,6},{6,5},{9,10},{10,9},{13,14},{14,13},{17,18},{18,... | collective-permute-start | bytes 3145736 | tf_op jit(solution)/shard_map/ppermute | solution.py:51
  27.8 15.6 %collective-permute-start.6 = (f32[512,512]{1,0:T(8,128)S(1)}, f32[512,512]{1,0:T(8,128)S(1)}, u32[]{:S(2)}, u32[]{:S(2)}) collective-permute-start(f32[512,512]{1,0:T(8,128)S(1)} %broadcast_select_fusion.1), channel_id=1, source_target_pairs={{8,24},{9,25},{10,26},{11,27},{20,28},{21,29},{22,30},{23,31},{0,1... | collective-permute-start | bytes 3145736 | tf_op jit(solution)/shard_map/ppermute | solution.py:55
  29.2 14.3 %collective-permute-start.7 = (f32[512,256]{1,0:T(8,128)S(1)}, f32[512,256]{1,0:T(8,128)S(1)}, u32[]{:S(2)}, u32[]{:S(2)}) collective-permute-start(f32[512,256]{1,0:T(8,128)S(1)} %get-tuple-element.66.swap), channel_id=1, source_target_pairs={{5,6},{6,5},{9,10},{10,9},{13,14},{14,13},{17,18},{18,17},{21,22},... | collective-permute-start | bytes 1572872 | tf_op jit(solution)/shard_map/ppermute | solution.py:51
  30.0 24.0 %collective-permute-start.9 = (f32[512,256]{1,0:T(8,128)S(1)}, f32[512,256]{1,0:T(8,128)S(1)}, u32[]{:S(2)}, u32[]{:S(2)}) collective-permute-start(f32[512,256]{1,0:T(8,128)S(1)} %broadcast_select_fusion.4), channel_id=1, source_target_pairs={{5,4},{6,7},{9,8},{10,11},{13,12},{14,15},{17,16},{18,19},{21,20},... | collective-permute-start | bytes 1572872 | tf_op jit(solution)/shard_map/ppermute | solution.py:301
  43.5 10.2 %copy-start.1 = (f32[512,512]{1,0:T(8,128)S(1)}, f32[512,512]{1,0:T(8,128)}, u32[]{:S(2)}) copy-start(f32[512,512]{1,0:T(8,128)} %one) | copy-start | bytes 3145732
  43.5 10.2 %copy-start.2 = (f32[512,512]{1,0:T(8,128)S(1)}, f32[512,512]{1,0:T(8,128)}, u32[]{:S(2)}) copy-start(f32[512,512]{1,0:T(8,128)} %two) | copy-start | bytes 3145732
  43.5 10.5 %collective-permute-start.8 = (f32[512,256]{1,0:T(8,128)S(1)}, f32[512,256]{1,0:T(8,128)S(1)}, u32[]{:S(2)}, u32[]{:S(2)}) collective-permute-start(f32[512,256]{1,0:T(8,128)S(1)} %get-tuple-element.68.far), channel_id=1, source_target_pairs={{5,4},{6,7},{9,8},{10,11},{13,12},{14,15},{17,16},{18,19},{21,20},... | collective-permute-start | bytes 1572872 | tf_op jit(solution)/shard_map/ppermute | solution.py:51
  44.3 32.0 %collective-permute-start.10 = (f32[1024,256]{1,0:T(8,128)S(1)}, f32[1024,256]{1,0:T(8,128)S(1)}, u32[]{:S(2)}, u32[]{:S(2)}) collective-permute-start(f32[1024,256]{1,0:T(8,128)S(1)} %get-tuple-element.74.swap), channel_id=1, source_target_pairs={{1,2},{2,1},{5,6},{6,5},{9,10},{10,9},{13,14},{14,13},{17,18},{18,... | collective-permute-start | bytes 3145736 | tf_op jit(solution)/shard_map/ppermute | solution.py:51
  45.3 31.0 %collective-permute-start.11 = (f32[512,512]{1,0:T(8,128)S(1)}, f32[512,512]{1,0:T(8,128)S(1)}, u32[]{:S(2)}, u32[]{:S(2)}) collective-permute-start(f32[512,512]{1,0:T(8,128)S(1)} %broadcast_select_fusion.refs_0_), channel_id=1, source_target_pairs={{0,1},{3,2},{4,5},{7,6},{8,9},{11,10},{12,13},{15,14},{16,17},{19,... | collective-permute-start | bytes 3145736 | tf_op jit(solution)/shard_map/ppermute | solution.py:51
  52.4 37.4 %collective-permute-start.14 = (f32[1024,256]{1,0:T(8,128)S(1)}, f32[1024,256]{1,0:T(8,128)S(1)}, u32[]{:S(2)}, u32[]{:S(2)}) collective-permute-start(f32[1024,256]{1,0:T(8,128)S(1)} %get-tuple-element.77.mid), channel_id=1, source_target_pairs={{1,0},{2,3},{5,4},{6,7},{9,8},{10,11},{13,12},{14,15},{17,16},{18,... | collective-permute-start | bytes 3145736 | tf_op jit(solution)/shard_map/ppermute | solution.py:51
  54.2 8.8 %collective-permute-start.12 = (f32[256,512]{1,0:T(8,128)S(1)}, f32[256,512]{1,0:T(8,128)S(1)}, u32[]{:S(2)}, u32[]{:S(2)}) collective-permute-start(f32[256,512]{1,0:T(8,128)S(1)} %slice.70), channel_id=1, source_target_pairs={{4,0},{5,1},{6,2},{7,3}} | collective-permute-start | bytes 1572872 | tf_op jit(solution)/shard_map/ppermute | solution.py:55
  55.6 45.2 %collective-permute-start.17 = (f32[512,512]{1,0:T(8,128)S(1)}, f32[512,512]{1,0:T(8,128)S(1)}, u32[]{:S(2)}, u32[]{:S(2)}) collective-permute-start(f32[512,512]{1,0:T(8,128)S(1)} %pad_maximum_fusion.2), channel_id=1, source_target_pairs={{1,2},{2,1},{5,6},{6,5},{9,10},{10,9},{13,14},{14,13},{17,18},{18,... | collective-permute-start | bytes 3145736 | tf_op jit(solution)/shard_map/ppermute | solution.py:51
  63.1 19.9 %collective-permute-start.13 = (f32[256,512]{1,0:T(8,128)S(1)}, f32[256,512]{1,0:T(8,128)S(1)}, u32[]{:S(2)}, u32[]{:S(2)}) collective-permute-start(f32[256,512]{1,0:T(8,128)S(1)} %slice_select_fusion), channel_id=1, source_target_pairs={{0,8},{1,9},{2,10},{3,11},{4,20},{5,21},{6,22},{7,23}} | collective-permute-start | bytes 1572872 | tf_op jit(solution)/shard_map/ppermute | solution.py:55
  82.9 12.2 %collective-permute-start.16 = (f32[512,512]{1,0:T(8,128)S(1)}, f32[512,512]{1,0:T(8,128)S(1)}, u32[]{:S(2)}, u32[]{:S(2)}) collective-permute-start(f32[512,512]{1,0:T(8,128)S(1)} %get-tuple-element.79.refs_0_), channel_id=1, source_target_pairs={{0,4},{1,5},{2,6},{3,7},{4,0},{5,1},{6,2},{7,3},{8,12},{9,13},{10,... | collective-permute-start | bytes 3145736 | tf_op jit(solution)/shard_map/ppermute | solution.py:55
  83.0 12.1 %collective-permute-start.15 = (f32[256,512]{1,0:T(8,128)S(1)}, f32[256,512]{1,0:T(8,128)S(1)}, u32[]{:S(2)}, u32[]{:S(2)}) collective-permute-start(f32[256,512]{1,0:T(8,128)S(1)} %broadcast_select_fusion.3), channel_id=1, source_target_pairs={{8,24},{9,25},{10,26},{11,27},{20,28},{21,29},{22,30},{23,31},{0,1... | collective-permute-start | bytes 1572872 | tf_op jit(solution)/shard_map/ppermute | solution.py:55
  88.5 27.9 %collective-permute-start.20 = (f32[1024,256]{1,0:T(8,128)S(1)}, f32[1024,256]{1,0:T(8,128)S(1)}, u32[]{:S(2)}, u32[]{:S(2)}) collective-permute-start(f32[1024,256]{1,0:T(8,128)S(1)} %get-tuple-element.104.far), channel_id=1, source_target_pairs={{1,0},{2,3},{5,4},{6,7},{9,8},{10,11},{13,12},{14,15},{17,16},{18,... | collective-permute-start | bytes 3145736 | tf_op jit(solution)/shard_map/ppermute | solution.py:51
  95.2 2.0 %collective-permute-start.18 = (f32[256,512]{1,0:T(8,128)S(1)}, f32[256,512]{1,0:T(8,128)S(1)}, u32[]{:S(2)}, u32[]{:S(2)}) collective-permute-start(f32[256,512]{1,0:T(8,128)S(1)} %broadcast_select_fusion.2.refs_2_), channel_id=1, source_target_pairs={{0,4},{1,5},{2,6},{3,7},{4,0},{5,1},{6,2},{7,3},{8,12},{9,13},{10,... | collective-permute-start | bytes 1572872 | tf_op jit(solution)/shard_map/ppermute | solution.py:55
  95.3 10.2 %collective-permute-start.19 = (f32[512,512]{1,0:T(8,128)S(1)}, f32[512,512]{1,0:T(8,128)S(1)}, u32[]{:S(2)}, u32[]{:S(2)}) collective-permute-start(f32[512,512]{1,0:T(8,128)S(1)} %broadcast_select_fusion.refs_0_), channel_id=1, source_target_pairs={{0,4},{1,5},{2,6},{3,7},{4,0},{5,1},{6,2},{7,3},{8,12},{9,13},{10,... | collective-permute-start | bytes 3145736 | tf_op jit(solution)/shard_map/ppermute | solution.py:55
  102.7 24.9 %collective-permute-start.21 = (f32[256,512]{1,0:T(8,128)S(1)}, f32[256,512]{1,0:T(8,128)S(1)}, u32[]{:S(2)}, u32[]{:S(2)}) collective-permute-start(f32[256,512]{1,0:T(8,128)S(1)} %get-tuple-element.97), channel_id=1, source_target_pairs={{1,0},{2,3},{5,4},{6,7},{9,8},{10,11},{13,12},{14,15},{17,16},{18,... | collective-permute-start | bytes 1572872 | tf_op jit(solution)/shard_map/ppermute | solution.py:51
  104.0 34.2 %collective-permute-start.22 = (f32[256,512]{1,0:T(8,128)S(1)}, f32[256,512]{1,0:T(8,128)S(1)}, u32[]{:S(2)}, u32[]{:S(2)}) collective-permute-start(f32[256,512]{1,0:T(8,128)S(1)} %get-tuple-element.98), channel_id=1, source_target_pairs={{1,0},{2,3},{5,4},{6,7},{9,8},{10,11},{13,12},{14,15},{17,16},{18,... | collective-permute-start | bytes 1572872 | tf_op jit(solution)/shard_map/ppermute | solution.py:51
  105.5 3.7 %copy-start = (f32[2048,512]{1,0:T(8,128)S(1)}, f32[2048,512]{1,0:T(8,128)}, u32[]{:S(2)}) copy-start(f32[2048,512]{1,0:T(8,128)} %top.9) | copy-start | bytes 12582916

commit v9 on v8

--- a/solution.py
+++ b/solution.py
@@ -71,7 +71,7 @@
     return one(left[0], right[0]) + (one(left[0], right[1]) + one(left[1], right[0]))
 
 
-TILE = 256
+TILE, SHORT = 256, 128
 VMEM_BYTES = 32 * 2**20
 SMEM = pl.BlockSpec(memory_space=pltpu.SMEM)
 
@@ -132,15 +132,14 @@
 def multiply_kernel(near_end, own, both, high, low, *outs):
     panels = jnp.concatenate([near_end[...], own[...], both[...]], axis=1)
     value = three_pass(split(panels), (high[...], low[...]))
-    for i, out in enumerate(outs):
-        out[...] = value[i * TILE : (i + 1) * TILE]
+    outs[0][...], outs[1][...] = value[:-SHORT], value[-SHORT:]
 
 
 def multiply(panels, solved):
     rows, width = panels[0].shape[0], solved[0].shape[1]
     return pl.pallas_call(
         multiply_kernel,
-        out_shape=[jax.ShapeDtypeStruct((TILE, width), jnp.float32)] * (rows // TILE),
+        out_shape=[jax.ShapeDtypeStruct((n, width), jnp.float32) for n in (rows - SHORT, SHORT)],
         compiler_params=pltpu.CompilerParams(vmem_limit_bytes=VMEM_BYTES),
         cost_estimate=pl.CostEstimate(flops=2 * 10**9, bytes_accessed=0, transcendentals=0),
     )(*panels, *solved)
@@ -194,15 +193,16 @@
 
 
 def last_call(body, place, top, parts, fixed, out, block_of_out, flops, past):
-    width, count = top.shape[1], parts[0].shape[0] // TILE
-    first = past // TILE - count
-    tile = pl.BlockSpec((TILE, width), lambda i: (first + i, 0))
+    step = SHORT if parts[0].shape[0] % TILE else TILE
+    width, count = top.shape[1], parts[0].shape[0] // step
+    first = past // step - count
+    tile = pl.BlockSpec((step, width), lambda i: (first + i, 0))
     return pl.pallas_call(
         body,
         grid=(count,),
         out_shape=jax.ShapeDtypeStruct(top.shape, top.dtype),
         in_specs=[SMEM, tile]
-        + [pl.BlockSpec((TILE, v.shape[1]), lambda i: (i, 0)) for v in parts]
+        + [pl.BlockSpec((step, v.shape[1]), lambda i: (i, 0)) for v in parts]
         + [pl.BlockSpec(v.shape, lambda i: (0, 0)) for v in fixed]
         + [tile if block_of_out else pl.BlockSpec(memory_space=pl.ANY)],
         out_specs=tile,
@@ -349,9 +349,9 @@
     rest = (rest_own, rest_swap, rest_mid, rest_far, rest_c, rest_cc)
     out = update_raw(place, test_kernel, solved, rest, block, False, out)
     out = update_last(place, test_kernel, last, solved, out)
-    for i, value in enumerate(returned):
+    for past, value in zip((rows - SHORT, rows), returned):
         out, value = tied((out, value))
-        out = finish(place, test_kernel, value, out, raw + (i + 1) * TILE)
+        out = finish(place, test_kernel, value, out, past)
     return out
 
 

time: 141 us -> 141 us (level)
  no operation moved by 1% of the time
where the time goes in v9:
time: 141 us; the launch traced here: 140 us
  starting transfers between devices  59.2 us (42%)
  waiting for transfers between devices  49.2 us (35%)
  Pallas kernels  24.6 us (17%)
  other arithmetic  3.7 us (3%)
  local copies, waits for them, and re-layouts  2.69 us (2%)
    ppermute x9, starting transfers between devices, along_row(): lax.ppermute(value, AXES, [(a * COLS + c, b * COLS + c) for a, b in pairs...  31 us
    ppermute x9, waiting for transfers between devices, along_row(): lax.ppermute(value, AXES, [(a * COLS + c, b * COLS + c) for a, b in pairs...  26.4 us
    ppermute x13, waiting for transfers between devices, along_col(): return lax.ppermute(value, AXES, pairs_of(pairs, rows))  22.7 us
    ppermute x13, starting transfers between devices, along_col(): return lax.ppermute(value, AXES, pairs_of(pairs, rows))  21.9 us
    pallas_call x2, Pallas kernels, update_raw(): pl.pallas_call(functools.partial(update_raw_kernel, blocks), grid=(group[...  8.96 us
    pallas_call x2, Pallas kernels, solve(): pl.pallas_call(solve_kernel, out_shape=[part, part], in_specs=[SMEM] + [p...  7.36 us
    ppermute x1, starting transfers between devices, four(): lax.ppermute(jnp.where(end, last_own, lead_mid), AXES, pairs_of(MID_END,...  6.3 us
    pallas_call x3, Pallas kernels, last_call(): pl.pallas_call(body, grid=(count,), out_shape=jax.ShapeDtypeStruct(top.sh...  6.12 us
  transfers between devices with their start and end apart: 23, of which 10 were waited for; matrix products, arithmetic and copies ran while one was open for 3% of the time, Pallas kernels for 16%

profile of v9, /device:TPU:0, one launch (start us, length us, event | category | flops | bytes accessed | tf_op | source)
XLA Modules:
  0.0 139.9 jit_solution(16403581979769849070)
XLA Ops:
  0.0 1.3 fusion
  1.4 0.7 collective-permute-start
  2.1 0.7 collective-permute-start.1
  2.8 0.1 fusion.2
  3.0 5.7 %collective-permute-start.2 = (f32[256,512]{1,0:T(8,128)S(1)}, f32[256,512]{1,0:T(8,128)S(1)}, u32[]{:S(2)}, u32[]{:S(2)}) collective-permute-start(f32[256,512]{1,0:T(8,128)S(1)} %get-tuple-element.120), channel_id=1, source_target_pairs={{0,4},{1,5},{2,6},{3,7},{4,0},{5,1},{6,2},{7,3}} | collective-permute-start | bytes 1572872 | tf_op jit(solution)/shard_map/ppermute | solution.py:55
  8.7 1.0 slice-done.1
  9.7 0.2 slice-done.2
  10.0 0.2 collective-permute-done.2
  10.2 1.1 maximum_select_fusion
  11.3 3.4 %collective-permute-start.3 = (f32[512,512]{1,0:T(8,128)}, f32[512,512]{1,0:T(8,128)}, u32[]{:S(2)}, u32[]{:S(2)}) collective-permute-start(f32[512,512]{1,0:T(8,128)} %maximum_select_fusion), channel_id=1, source_target_pairs={{0,8},{1,9},{2,10},{3,11},{4,20},{5,21},{6,22},{7,23}} | collective-permute-start | bytes 3145736 | tf_op jit(solution)/shard_map/ppermute | solution.py:55
  14.9 4.4 %collective-permute-start.4 = (f32[1024,256]{1,0:T(8,128)S(1)}, f32[1024,256]{1,0:T(8,128)S(1)}, u32[]{:S(2)}, u32[]{:S(2)}) collective-permute-start(f32[1024,256]{1,0:T(8,128)S(1)} %pad_maximum_fusion.own), channel_id=1, source_target_pairs={{0,1},{3,2},{1,0},{2,3},{4,5},{7,6},{5,4},{6,7},{8,9},{11,10},{9,8... | collective-permute-start | bytes 3145736 | tf_op jit(solution)/shard_map/ppermute | solution.py:51
  19.3 0.7 collective-permute-start.5
  20.1 6.3 %collective-permute-done.3.refs_3_ = f32[512,512]{1,0:T(8,128)} collective-permute-done((f32[512,512]{1,0:T(8,128)}, f32[512,512]{1,0:T(8,128)}, u32[]{:S(2)}, u32[]{:S(2)}) %collective-permute-start.3) | collective-permute-done | bytes 1048608 | tf_op jit(solution)/shard_map/ppermute | solution.py:55
  26.4 1.4 %broadcast_select_fusion.1 = f32[512,512]{1,0:T(8,128)S(1)} fusion(f32[512,512]{1,0:T(8,128)} %get-tuple-element.64, f32[512,512]{1,0:T(8,128)} %maximum_select_fusion, pred[]{:T(512)S(6)} %or.16), kind=kLoop, calls=%fused_computation.8 | loop fusion | flops 262144 | bytes 3145729 | tf_op jit(solution)/shard_map/jit(_where)/select_n | solution.py:269
  27.8 1.4 collective-permute-start.6
  29.2 0.7 collective-permute-start.7
  30.0 6.3 %collective-permute-start.9 = (f32[512,256]{1,0:T(8,128)S(1)}, f32[512,256]{1,0:T(8,128)S(1)}, u32[]{:S(2)}, u32[]{:S(2)}) collective-permute-start(f32[512,256]{1,0:T(8,128)S(1)} %broadcast_select_fusion.4), channel_id=1, source_target_pairs={{5,4},{6,7},{9,8},{10,11},{13,12},{14,15},{17,16},{18,19},{21,20},... | collective-permute-start | bytes 1572872 | tf_op jit(solution)/shard_map/ppermute | solution.py:301
  36.3 7.1 %collective-permute-done.4.refs_1_ = f32[1024,256]{1,0:T(8,128)S(1)} collective-permute-done((f32[1024,256]{1,0:T(8,128)S(1)}, f32[1024,256]{1,0:T(8,128)S(1)}, u32[]{:S(2)}, u32[]{:S(2)}) %collective-permute-start.4) | collective-permute-done | bytes 1048608 | tf_op jit(solution)/shard_map/ppermute | solution.py:51
  43.5 0.8 collective-permute-start.8
  44.3 0.7 collective-permute-start.10
  45.1 0.2 broadcast_select_fusion.refs_0_
  45.3 7.1 %collective-permute-start.11 = (f32[512,512]{1,0:T(8,128)S(1)}, f32[512,512]{1,0:T(8,128)S(1)}, u32[]{:S(2)}, u32[]{:S(2)}) collective-permute-start(f32[512,512]{1,0:T(8,128)S(1)} %broadcast_select_fusion.refs_0_), channel_id=1, source_target_pairs={{0,1},{3,2},{4,5},{7,6},{8,9},{11,10},{12,13},{15,14},{16,17},{19,... | collective-permute-start | bytes 3145736 | tf_op jit(solution)/shard_map/ppermute | solution.py:51
  52.4 1.3 collective-permute-start.14
  53.7 0.3 shard_map.75
  54.2 1.3 collective-permute-start.12
  55.5 0.1 pad_maximum_fusion.2
  55.7 0.7 collective-permute-start.17
  56.4 6.6 %collective-permute-done.12 = f32[256,512]{1,0:T(8,128)S(1)} collective-permute-done((f32[256,512]{1,0:T(8,128)S(1)}, f32[256,512]{1,0:T(8,128)S(1)}, u32[]{:S(2)}, u32[]{:S(2)}) %collective-permute-start.12) | collective-permute-done | bytes 524320 | tf_op jit(solution)/shard_map/ppermute | solution.py:55
  63.1 13.2 %collective-permute-start.13 = (f32[256,512]{1,0:T(8,128)S(1)}, f32[256,512]{1,0:T(8,128)S(1)}, u32[]{:S(2)}, u32[]{:S(2)}) collective-permute-start(f32[256,512]{1,0:T(8,128)S(1)} %slice_select_fusion), channel_id=1, source_target_pairs={{0,8},{1,9},{2,10},{3,11},{4,20},{5,21},{6,22},{7,23}} | collective-permute-start | bytes 1572872 | tf_op jit(solution)/shard_map/ppermute | solution.py:55
  76.3 6.6 %collective-permute-done.13.refs_3_ = f32[256,512]{1,0:T(8,128)S(1)} collective-permute-done((f32[256,512]{1,0:T(8,128)S(1)}, f32[256,512]{1,0:T(8,128)S(1)}, u32[]{:S(2)}, u32[]{:S(2)}) %collective-permute-start.13) | collective-permute-done | bytes 524320 | tf_op jit(solution)/shard_map/ppermute | solution.py:55
  83.1 5.4 %collective-permute-start.15 = (f32[256,512]{1,0:T(8,128)S(1)}, f32[256,512]{1,0:T(8,128)S(1)}, u32[]{:S(2)}, u32[]{:S(2)}) collective-permute-start(f32[256,512]{1,0:T(8,128)S(1)} %broadcast_select_fusion.3), channel_id=1, source_target_pairs={{8,24},{9,25},{10,26},{11,27},{20,28},{21,29},{22,30},{23,31},{0,1... | collective-permute-start | bytes 1572872 | tf_op jit(solution)/shard_map/ppermute | solution.py:55
  88.5 1.3 collective-permute-start.20
  89.8 5.3 %collective-permute-done.15.refs_2_ = f32[256,512]{1,0:T(8,128)S(1)} collective-permute-done((f32[256,512]{1,0:T(8,128)S(1)}, f32[256,512]{1,0:T(8,128)S(1)}, u32[]{:S(2)}, u32[]{:S(2)}) %collective-permute-start.15) | collective-permute-done | bytes 524320 | tf_op jit(solution)/shard_map/ppermute | solution.py:55
  95.3 0.5 collective-permute-start.19
  95.8 1.4 collective-permute-done.18.refs_3_
  97.2 3.7 %shard_map.76 = (bf16[1024,512]{1,0:T(8,128)(2,1)S(1)}, bf16[1024,512]{1,0:T(8,128)(2,1)S(1)}) custom-call(s32[5]{0:T(128)S(1)} %convert_element_type.3.place, f32[512,512]{1,0:T(8,128)S(1)} %get-tuple-element.79.refs_0_, f32[512,512]{1,0:T(8,128)S(1)} %get-tuple-element.84.refs_1_, f32[256,512]{1,0:T(8,128)S(1)} %broadcast_select_fusion.2.refs_2_, ...), custom_call_target="tpu_custom_call" | custom-call | flops 3000000000 | tf_op jit(solution)/shard_map/pallas_call | solution.py:123
  100.9 1.8 %shard_map.78 = (f32[384,512]{1,0:T(8,128)S(1)}, f32[128,512]{1,0:T(8,128)S(1)}) custom-call(f32[512,256]{1,0:T(8,128)S(1)} %get-tuple-element.83.near_end.c, f32[512,256]{1,0:T(8,128)S(1)} %get-tuple-element.82.own, f32[512,512]{1,0:T(8,128)S(1)} %get-tuple-element.94.both, bf16[1024,512]{1,0:T(8,128)(2,1)S(1)} %get-tuple-element.95.high, ...), custom_call_target="tpu_custom_call" | custom-call | flops 2000000000 | tf_op jit(solution)/shard_map/pallas_call | solution.py:140
  102.7 1.3 collective-permute-start.21
  104.0 1.5 %collective-permute-start.22 = (f32[128,512]{1,0:T(8,128)S(1)}, f32[128,512]{1,0:T(8,128)S(1)}, u32[]{:S(2)}, u32[]{:S(2)}) collective-permute-start(f32[128,512]{1,0:T(8,128)S(1)} %get-tuple-element.98), channel_id=1, source_target_pairs={{1,0},{2,3},{5,4},{6,7},{9,8},{10,11},{13,12},{14,15},{17,16},{18,... | collective-permute-start | bytes 786440 | tf_op jit(solution)/shard_map/ppermute | solution.py:51
  105.5 3.7 %shard_map.79 = (bf16[1024,512]{1,0:T(8,128)(2,1)S(1)}, bf16[1024,512]{1,0:T(8,128)(2,1)S(1)}) custom-call(s32[5]{0:T(128)S(1)} %convert_element_type.3.place, f32[512,512]{1,0:T(8,128)S(1)} %broadcast_select_fusion.refs_0_, f32[512,512]{1,0:T(8,128)S(1)} %collective-permute-done.19.refs_1_, f32[256,512]{1,0:T(8,128)S(1)} %broadcast_select_fusion.2.refs_2_, ...), custom_call_target="tpu_custom_call" | custom-call | flops 3000000000 | tf_op jit(solution)/shard_map/pallas_call | solution.py:123
  109.2 3.5 %shard_map.82.refs_2_ = f32[2048,512]{1,0:T(8,128)} custom-call(s32[5]{0:T(128)S(1)} %convert_element_type.3.place, f32[2048,512]{1,0:T(8,128)S(1)} %copy-done, bf16[1024,512]{1,0:T(8,128)(2,1)S(1)} %get-tuple-element.102.high, bf16[1024,512]{1,0:T(8,128)(2,1)S(1)} %get-tuple-element.103.low, f32[512,256]{1,0:T(8,128)S(1)} %pad_maximum_fusion.3.own, ...), custom_call_target="tpu_custom_call" | custom-call | flops 3000000000 | tf_op jit(solution)/shard_map/pallas_call | solution.py:169
  112.8 3.6 %collective-permute-done.20.refs_1_ = f32[1024,256]{1,0:T(8,128)S(1)} collective-permute-done((f32[1024,256]{1,0:T(8,128)S(1)}, f32[1024,256]{1,0:T(8,128)S(1)}, u32[]{:S(2)}, u32[]{:S(2)}) %collective-permute-start.20) | collective-permute-done | bytes 1048608 | tf_op jit(solution)/shard_map/ppermute | solution.py:51
  116.3 5.4 %shard_map.84.kept = f32[2048,512]{1,0:T(8,128)} custom-call(s32[5]{0:T(128)S(1)} %convert_element_type.3.place, f32[2048,512]{1,0:T(8,128)S(1)} %copy-done, bf16[1024,512]{1,0:T(8,128)(2,1)S(1)} %get-tuple-element.102.high, bf16[1024,512]{1,0:T(8,128)(2,1)S(1)} %get-tuple-element.103.low, ...), custom_call_target="tpu_custom_call", output_to_operand_aliasing={{}: (10, {})} | custom-call | flops 3000000000 | tf_op jit(solution)/shard_map/pallas_call | solution.py:169
  121.8 1.5 %shard_map.85.kept = f32[2048,512]{1,0:T(8,128)} custom-call(s32[5]{0:T(128)S(1)} %convert_element_type.3.place, f32[2048,512]{1,0:T(8,128)S(1)} %copy-done, f32[512,256]{1,0:T(8,128)S(1)} %get-tuple-element.83.near_end.c, f32[512,256]{1,0:T(8,128)S(1)} %get-tuple-element.82.own, ...), custom_call_target="tpu_custom_call", output_to_operand_aliasing={{}: (7, {})} | custom-call | flops 2000000000 | tf_op jit(solution)/shard_map/pallas_call | solution.py:200
  123.3 9.9 %collective-permute-done.21.returned = f32[384,512]{1,0:T(8,128)S(1)} collective-permute-done((f32[384,512]{1,0:T(8,128)S(1)}, f32[384,512]{1,0:T(8,128)S(1)}, u32[]{:S(2)}, u32[]{:S(2)}) %collective-permute-start.21) | collective-permute-done | bytes 786464 | tf_op jit(solution)/shard_map/ppermute | solution.py:51
  133.2 2.9 %shard_map.86.kept = f32[2048,512]{1,0:T(8,128)} custom-call(s32[5]{0:T(128)S(1)} %convert_element_type.3.place, f32[2048,512]{1,0:T(8,128)S(1)} %copy-done, f32[384,512]{1,0:T(8,128)S(1)} %collective-permute-done.21.returned, f32[2048,512]{1,0:T(8,128)} %shard_map.85.kept), custom_call_target="tpu_custom_call", output_to_operand_aliasing={{}: (3, {})} | custom-call | flops 1000000000 | tf_op jit(solution)/shard_map/pallas_call | solution.py:200
  136.1 2.1 %collective-permute-done.22.returned = f32[128,512]{1,0:T(8,128)S(1)} collective-permute-done((f32[128,512]{1,0:T(8,128)S(1)}, f32[128,512]{1,0:T(8,128)S(1)}, u32[]{:S(2)}, u32[]{:S(2)}) %collective-permute-start.22) | collective-permute-done | bytes 262176 | tf_op jit(solution)/shard_map/ppermute | solution.py:51
  138.2 1.7 %shard_map.87 = f32[2048,512]{1,0:T(8,128)} custom-call(s32[5]{0:T(128)S(1)} %convert_element_type.3.place, f32[2048,512]{1,0:T(8,128)S(1)} %copy-done, f32[128,512]{1,0:T(8,128)S(1)} %collective-permute-done.22.returned, f32[2048,512]{1,0:T(8,128)} %shard_map.86.kept), custom_call_target="tpu_custom_call", output_to_operand_aliasing={{}: (3, {})} | custom-call | flops 1000000000 | tf_op jit(solution)/shard_map/pallas_call | solution.py:200
  (64 shorter events, 1.0 us)
Async XLA Ops:
  0.0 2.8 %slice-start = ((f32[2048,512]{1,0:T(8,128)}), f32[512,512]{1,0:T(8,128)S(1)}, s32[]{:S(2)}) async-start(f32[2048,512]{1,0:T(8,128)} %top.9), calls=%async_computation | async-start | bytes 2097152 | tf_op jit(solution)/shard_map/slice | solution.py:281
  1.4 18.7 %collective-permute-start = (f32[512,256]{1,0:T(8,128)S(1)}, f32[512,256]{1,0:T(8,128)S(1)}, u32[]{:S(2)}, u32[]{:S(2)}) collective-permute-start(f32[512,256]{1,0:T(8,128)S(1)} %pad_maximum_fusion.3.own), channel_id=1, source_target_pairs={{4,5},{7,6},{5,4},{6,7},{8,9},{11,10},{9,8},{10,11},{12,13},{15,14... | collective-permute-start | bytes 1572872 | tf_op jit(solution)/shard_map/ppermute | solution.py:51
  2.1 18.0 %collective-permute-start.1 = (f32[512,256]{1,0:T(8,128)S(1)}, f32[512,256]{1,0:T(8,128)S(1)}, u32[]{:S(2)}, u32[]{:S(2)}) collective-permute-start(f32[512,256]{1,0:T(8,128)S(1)} %pad_maximum_fusion.3.own), channel_id=1, source_target_pairs={{5,6},{6,5},{9,10},{10,9},{13,14},{14,13},{17,18},{18,17},{21,22},... | collective-permute-start | bytes 1572872 | tf_op jit(solution)/shard_map/ppermute | solution.py:51
  3.0 7.2 %collective-permute-start.2 = (f32[256,512]{1,0:T(8,128)S(1)}, f32[256,512]{1,0:T(8,128)S(1)}, u32[]{:S(2)}, u32[]{:S(2)}) collective-permute-start(f32[256,512]{1,0:T(8,128)S(1)} %get-tuple-element.120), channel_id=1, source_target_pairs={{0,4},{1,5},{2,6},{3,7},{4,0},{5,1},{6,2},{7,3}} | collective-permute-start | bytes 1572872 | tf_op jit(solution)/shard_map/ppermute | solution.py:55
  8.7 1.0 slice-start.1
  8.7 1.2 slice-start.2
  11.3 15.0 %collective-permute-start.3 = (f32[512,512]{1,0:T(8,128)}, f32[512,512]{1,0:T(8,128)}, u32[]{:S(2)}, u32[]{:S(2)}) collective-permute-start(f32[512,512]{1,0:T(8,128)} %maximum_select_fusion), channel_id=1, source_target_pairs={{0,8},{1,9},{2,10},{3,11},{4,20},{5,21},{6,22},{7,23}} | collective-permute-start | bytes 3145736 | tf_op jit(solution)/shard_map/ppermute | solution.py:55
  14.9 28.5 %collective-permute-start.4 = (f32[1024,256]{1,0:T(8,128)S(1)}, f32[1024,256]{1,0:T(8,128)S(1)}, u32[]{:S(2)}, u32[]{:S(2)}) collective-permute-start(f32[1024,256]{1,0:T(8,128)S(1)} %pad_maximum_fusion.own), channel_id=1, source_target_pairs={{0,1},{3,2},{1,0},{2,3},{4,5},{7,6},{5,4},{6,7},{8,9},{11,10},{9,8... | collective-permute-start | bytes 3145736 | tf_op jit(solution)/shard_map/ppermute | solution.py:51
  19.3 24.1 %collective-permute-start.5 = (f32[1024,256]{1,0:T(8,128)S(1)}, f32[1024,256]{1,0:T(8,128)S(1)}, u32[]{:S(2)}, u32[]{:S(2)}) collective-permute-start(f32[1024,256]{1,0:T(8,128)S(1)} %pad_maximum_fusion.own), channel_id=1, source_target_pairs={{1,2},{2,1},{5,6},{6,5},{9,10},{10,9},{13,14},{14,13},{17,18},{18,... | collective-permute-start | bytes 3145736 | tf_op jit(solution)/shard_map/ppermute | solution.py:51
  27.8 15.6 %collective-permute-start.6 = (f32[512,512]{1,0:T(8,128)S(1)}, f32[512,512]{1,0:T(8,128)S(1)}, u32[]{:S(2)}, u32[]{:S(2)}) collective-permute-start(f32[512,512]{1,0:T(8,128)S(1)} %broadcast_select_fusion.1), channel_id=1, source_target_pairs={{8,24},{9,25},{10,26},{11,27},{20,28},{21,29},{22,30},{23,31},{0,1... | collective-permute-start | bytes 3145736 | tf_op jit(solution)/shard_map/ppermute | solution.py:55
  29.2 14.3 %collective-permute-start.7 = (f32[512,256]{1,0:T(8,128)S(1)}, f32[512,256]{1,0:T(8,128)S(1)}, u32[]{:S(2)}, u32[]{:S(2)}) collective-permute-start(f32[512,256]{1,0:T(8,128)S(1)} %get-tuple-element.66.swap), channel_id=1, source_target_pairs={{5,6},{6,5},{9,10},{10,9},{13,14},{14,13},{17,18},{18,17},{21,22},... | collective-permute-start | bytes 1572872 | tf_op jit(solution)/shard_map/ppermute | solution.py:51
  30.0 24.0 %collective-permute-start.9 = (f32[512,256]{1,0:T(8,128)S(1)}, f32[512,256]{1,0:T(8,128)S(1)}, u32[]{:S(2)}, u32[]{:S(2)}) collective-permute-start(f32[512,256]{1,0:T(8,128)S(1)} %broadcast_select_fusion.4), channel_id=1, source_target_pairs={{5,4},{6,7},{9,8},{10,11},{13,12},{14,15},{17,16},{18,19},{21,20},... | collective-permute-start | bytes 1572872 | tf_op jit(solution)/shard_map/ppermute | solution.py:301
  43.5 10.2 %copy-start.1 = (f32[512,512]{1,0:T(8,128)S(1)}, f32[512,512]{1,0:T(8,128)}, u32[]{:S(2)}) copy-start(f32[512,512]{1,0:T(8,128)} %one) | copy-start | bytes 3145732
  43.5 10.2 %copy-start.2 = (f32[512,512]{1,0:T(8,128)S(1)}, f32[512,512]{1,0:T(8,128)}, u32[]{:S(2)}) copy-start(f32[512,512]{1,0:T(8,128)} %two) | copy-start | bytes 3145732
  43.5 10.5 %collective-permute-start.8 = (f32[512,256]{1,0:T(8,128)S(1)}, f32[512,256]{1,0:T(8,128)S(1)}, u32[]{:S(2)}, u32[]{:S(2)}) collective-permute-start(f32[512,256]{1,0:T(8,128)S(1)} %get-tuple-element.68.far), channel_id=1, source_target_pairs={{5,4},{6,7},{9,8},{10,11},{13,12},{14,15},{17,16},{18,19},{21,20},... | collective-permute-start | bytes 1572872 | tf_op jit(solution)/shard_map/ppermute | solution.py:51
  44.3 32.0 %collective-permute-start.10 = (f32[1024,256]{1,0:T(8,128)S(1)}, f32[1024,256]{1,0:T(8,128)S(1)}, u32[]{:S(2)}, u32[]{:S(2)}) collective-permute-start(f32[1024,256]{1,0:T(8,128)S(1)} %get-tuple-element.74.swap), channel_id=1, source_target_pairs={{1,2},{2,1},{5,6},{6,5},{9,10},{10,9},{13,14},{14,13},{17,18},{18,... | collective-permute-start | bytes 3145736 | tf_op jit(solution)/shard_map/ppermute | solution.py:51
  45.3 31.1 %collective-permute-start.11 = (f32[512,512]{1,0:T(8,128)S(1)}, f32[512,512]{1,0:T(8,128)S(1)}, u32[]{:S(2)}, u32[]{:S(2)}) collective-permute-start(f32[512,512]{1,0:T(8,128)S(1)} %broadcast_select_fusion.refs_0_), channel_id=1, source_target_pairs={{0,1},{3,2},{4,5},{7,6},{8,9},{11,10},{12,13},{15,14},{16,17},{19,... | collective-permute-start | bytes 3145736 | tf_op jit(solution)/shard_map/ppermute | solution.py:51
  52.4 37.4 %collective-permute-start.14 = (f32[1024,256]{1,0:T(8,128)S(1)}, f32[1024,256]{1,0:T(8,128)S(1)}, u32[]{:S(2)}, u32[]{:S(2)}) collective-permute-start(f32[1024,256]{1,0:T(8,128)S(1)} %get-tuple-element.77.mid), channel_id=1, source_target_pairs={{1,0},{2,3},{5,4},{6,7},{9,8},{10,11},{13,12},{14,15},{17,16},{18,... | collective-permute-start | bytes 3145736 | tf_op jit(solution)/shard_map/ppermute | solution.py:51
  54.2 8.8 %collective-permute-start.12 = (f32[256,512]{1,0:T(8,128)S(1)}, f32[256,512]{1,0:T(8,128)S(1)}, u32[]{:S(2)}, u32[]{:S(2)}) collective-permute-start(f32[256,512]{1,0:T(8,128)S(1)} %slice.70), channel_id=1, source_target_pairs={{4,0},{5,1},{6,2},{7,3}} | collective-permute-start | bytes 1572872 | tf_op jit(solution)/shard_map/ppermute | solution.py:55
  55.7 45.2 %collective-permute-start.17 = (f32[512,512]{1,0:T(8,128)S(1)}, f32[512,512]{1,0:T(8,128)S(1)}, u32[]{:S(2)}, u32[]{:S(2)}) collective-permute-start(f32[512,512]{1,0:T(8,128)S(1)} %pad_maximum_fusion.2), channel_id=1, source_target_pairs={{1,2},{2,1},{5,6},{6,5},{9,10},{10,9},{13,14},{14,13},{17,18},{18,... | collective-permute-start | bytes 3145736 | tf_op jit(solution)/shard_map/ppermute | solution.py:51
  63.1 19.9 %collective-permute-start.13 = (f32[256,512]{1,0:T(8,128)S(1)}, f32[256,512]{1,0:T(8,128)S(1)}, u32[]{:S(2)}, u32[]{:S(2)}) collective-permute-start(f32[256,512]{1,0:T(8,128)S(1)} %slice_select_fusion), channel_id=1, source_target_pairs={{0,8},{1,9},{2,10},{3,11},{4,20},{5,21},{6,22},{7,23}} | collective-permute-start | bytes 1572872 | tf_op jit(solution)/shard_map/ppermute | solution.py:55
  83.0 12.2 %collective-permute-start.16 = (f32[512,512]{1,0:T(8,128)S(1)}, f32[512,512]{1,0:T(8,128)S(1)}, u32[]{:S(2)}, u32[]{:S(2)}) collective-permute-start(f32[512,512]{1,0:T(8,128)S(1)} %get-tuple-element.79.refs_0_), channel_id=1, source_target_pairs={{0,4},{1,5},{2,6},{3,7},{4,0},{5,1},{6,2},{7,3},{8,12},{9,13},{10,... | collective-permute-start | bytes 3145736 | tf_op jit(solution)/shard_map/ppermute | solution.py:55
  83.1 12.1 %collective-permute-start.15 = (f32[256,512]{1,0:T(8,128)S(1)}, f32[256,512]{1,0:T(8,128)S(1)}, u32[]{:S(2)}, u32[]{:S(2)}) collective-permute-start(f32[256,512]{1,0:T(8,128)S(1)} %broadcast_select_fusion.3), channel_id=1, source_target_pairs={{8,24},{9,25},{10,26},{11,27},{20,28},{21,29},{22,30},{23,31},{0,1... | collective-permute-start | bytes 1572872 | tf_op jit(solution)/shard_map/ppermute | solution.py:55
  88.5 27.9 %collective-permute-start.20 = (f32[1024,256]{1,0:T(8,128)S(1)}, f32[1024,256]{1,0:T(8,128)S(1)}, u32[]{:S(2)}, u32[]{:S(2)}) collective-permute-start(f32[1024,256]{1,0:T(8,128)S(1)} %get-tuple-element.104.far), channel_id=1, source_target_pairs={{1,0},{2,3},{5,4},{6,7},{9,8},{10,11},{13,12},{14,15},{17,16},{18,... | collective-permute-start | bytes 3145736 | tf_op jit(solution)/shard_map/ppermute | solution.py:51
  95.2 2.0 %collective-permute-start.18 = (f32[256,512]{1,0:T(8,128)S(1)}, f32[256,512]{1,0:T(8,128)S(1)}, u32[]{:S(2)}, u32[]{:S(2)}) collective-permute-start(f32[256,512]{1,0:T(8,128)S(1)} %broadcast_select_fusion.2.refs_2_), channel_id=1, source_target_pairs={{0,4},{1,5},{2,6},{3,7},{4,0},{5,1},{6,2},{7,3},{8,12},{9,13},{10,... | collective-permute-start | bytes 1572872 | tf_op jit(solution)/shard_map/ppermute | solution.py:55
  95.3 10.2 %collective-permute-start.19 = (f32[512,512]{1,0:T(8,128)S(1)}, f32[512,512]{1,0:T(8,128)S(1)}, u32[]{:S(2)}, u32[]{:S(2)}) collective-permute-start(f32[512,512]{1,0:T(8,128)S(1)} %broadcast_select_fusion.refs_0_), channel_id=1, source_target_pairs={{0,4},{1,5},{2,6},{3,7},{4,0},{5,1},{6,2},{7,3},{8,12},{9,13},{10,... | collective-permute-start | bytes 3145736 | tf_op jit(solution)/shard_map/ppermute | solution.py:55
  102.7 30.5 %collective-permute-start.21 = (f32[384,512]{1,0:T(8,128)S(1)}, f32[384,512]{1,0:T(8,128)S(1)}, u32[]{:S(2)}, u32[]{:S(2)}) collective-permute-start(f32[384,512]{1,0:T(8,128)S(1)} %get-tuple-element.97), channel_id=1, source_target_pairs={{1,0},{2,3},{5,4},{6,7},{9,8},{10,11},{13,12},{14,15},{17,16},{18,... | collective-permute-start | bytes 2359304 | tf_op jit(solution)/shard_map/ppermute | solution.py:51
  104.0 34.2 %collective-permute-start.22 = (f32[128,512]{1,0:T(8,128)S(1)}, f32[128,512]{1,0:T(8,128)S(1)}, u32[]{:S(2)}, u32[]{:S(2)}) collective-permute-start(f32[128,512]{1,0:T(8,128)S(1)} %get-tuple-element.98), channel_id=1, source_target_pairs={{1,0},{2,3},{5,4},{6,7},{9,8},{10,11},{13,12},{14,15},{17,16},{18,... | collective-permute-start | bytes 786440 | tf_op jit(solution)/shard_map/ppermute | solution.py:51
  105.5 3.7 %copy-start = (f32[2048,512]{1,0:T(8,128)S(1)}, f32[2048,512]{1,0:T(8,128)}, u32[]{:S(2)}) copy-start(f32[2048,512]{1,0:T(8,128)} %top.9) | copy-start | bytes 12582916
